TPU v7x, 32 devices: a whole 2x2x4 slice. The times are simulated.
32 devices in a mesh: dp: 16 (over z, x, core), tensor: 2 (over y).
Axes of the slice: x: 2, y: 2, z: 4, core: 2. Of those that a mesh axis runs over, the one named last changes fastest.
Arguments:
- hidden: bfloat16 [16, 1024, 1024], P('dp', 'tensor'), may hold values from -6 to 6
- pre_gain: float32 [1024], replicated, may hold values from 0.5 to 1.5
- zx_weight: bfloat16 [1024, 4096], P('dp', 'tensor'), may hold values from -0.1875 to 0.1875
- bc_weight: bfloat16 [1024, 256], P('dp'), may hold values from -0.1875 to 0.1875
- step_weight: bfloat16 [1024, 32], P('dp', 'tensor'), may hold values from -0.1875 to 0.1875
- conv_x_weight: float32 [4, 2048], P(None, 'tensor'), may hold values from -2 to 2
- conv_x_bias: float32 [2048], P('tensor'), may hold values from -2 to 2
- conv_bc_weight: float32 [4, 256], replicated, may hold values from -2 to 2
- conv_bc_bias: float32 [256], replicated, may hold values from -2 to 2
- step_bias: float32 [32], P('tensor'), may hold values from -6 to -2
- decay_log: float32 [32], P('tensor'), may hold values from 0 to 2.77
- skip_gain: float32 [32], P('tensor'), may hold values from 0.5 to 1.5
- norm_gain: float32 [2048], P('tensor'), may hold values from 0.5 to 1.5
- out_weight: bfloat16 [2048, 1024], P('tensor', 'dp'), may hold values from -0.125 to 0.125
- segment_ids: int32 [16, 1024], P('dp'), may hold values from 0 to 3, never falling along the last dimension, each value on 1 to 512 neighbouring positions
- pad_mask: int32 [16, 1024], P('dp'), may hold values 0 or 1
- grad_out: bfloat16 [16, 1024, 1024], P('dp', 'tensor'), may hold values from -6 to 6
Outputs:
- output: bfloat16 [16, 1024, 1024], P('dp', 'tensor')
- grad_hidden: bfloat16 [16, 1024, 1024], P('dp', 'tensor')
- grad_pre_gain: float32 [1024], replicated
- grad_zx_weight: float32 [1024, 4096], P('dp', 'tensor')
- grad_bc_weight: float32 [1024, 256], P('dp')
- grad_step_weight: float32 [1024, 32], P('dp', 'tensor')
- grad_conv_x_weight: float32 [4, 2048], P(None, 'tensor')
- grad_conv_x_bias: float32 [2048], P('tensor')
- grad_conv_bc_weight: float32 [4, 256], replicated
- grad_conv_bc_bias: float32 [256], replicated
- grad_step_bias: float32 [32], P('tensor')
- grad_decay_log: float32 [32], P('tensor')
- grad_skip_gain: float32 [32], P('tensor')
- grad_norm_gain: float32 [2048], P('tensor')
- grad_out_weight: float32 [2048, 1024], P('tensor', 'dp')
Inputs may be any that keep to these rules, and one draw needn't show every extreme that they name: `segment_ids`: along each sequence the ids never fall; a document, a run of equal ids, holds 1 to 512 tokens.
All inputs are finite; a program needn't handle non-finite values. No bound on the sum of `pad_mask` on one device may be relied on, other than what follows from the above.
Results may differ from a plain program's by a relative error of at most 0.012.
The roundings to bfloat16 on the way count: a program that leaves them out, or rounds other values in their place, can miss the bound.
Values may be sent and summed in bfloat16 or wider, within the bound.
A program may use at most 192 MiB of HBM per device.

v0:
```python
import jax
import jax.numpy as jnp
from jax import lax
from jax.sharding import PartitionSpec as P

HEADDIM = 64
STATE = 128
SPAN = 256


epsilon = 1e-05
highest_precision = lax.Precision.HIGHEST


def rounded(value):
    return lax.optimization_barrier(value.astype(jnp.bfloat16)).astype(jnp.float32)


def filter_kernel_length(inputs, weight, bias_row, segment):
    length = inputs.shape[1]
    summed = bias_row + weight[0] * inputs
    for offset in range(1, weight.shape[0]):
        shifted = jnp.pad(inputs, ((0, 0), (offset, 0), (0, 0)))[:, :length]
        earlier = jnp.pad(segment, ((0, 0), (offset, 0)), constant_values=-1)[:, :length]
        summed = summed + weight[offset] * jnp.where((earlier == segment)[:, :, None], shifted, 0.0)
    return summed


def state_scan(values_in, keys_in, queries_in, step_size, rates, segment):
    seq_count, length, head_count, head_width = values_in.shape
    blocks = length // SPAN

    def to_blocks(array):
        return jnp.moveaxis(array.reshape((seq_count, blocks, SPAN) + array.shape[2:]), 1, 0)

    positions = jnp.arange(SPAN)
    causal = positions[:, None] >= positions[None, :]

    def advance(carry_in, block):
        carry_state, last_doc = carry_in
        block_values, block_keys, block_queries, block_steps, block_docs = block
        log_decay = jnp.cumsum(block_steps * rates, axis=1)
        inside = (causal[None] & (block_docs[:, :, None] == block_docs[:, None, :]))[..., None]
        spread = log_decay[:, :, None, :] - log_decay[:, None, :, :]
        forgetting_factors = jnp.where(inside, jnp.exp(jnp.where(inside, spread, 0.0)), 0.0)
        scores = jnp.einsum("stn,sun->stu", block_queries, block_keys, precision=highest_precision)
        mixing = scores[..., None] * forgetting_factors * block_steps[:, None, :, :]
        result = jnp.einsum("stuh,suhp->sthp", mixing, block_values, precision=highest_precision)
        carried = jnp.where((block_docs == last_doc[:, None])[..., None], jnp.exp(log_decay), 0.0)
        result = result + carried[..., None] * jnp.einsum(
            "stn,shpn->sthp", block_queries, carry_state, precision=highest_precision
        )
        tail_doc = block_docs[:, -1]
        tail_keep = (block_docs == tail_doc[:, None])[..., None]
        toward = (
            jnp.where(
                tail_keep, jnp.exp(jnp.where(tail_keep, log_decay[:, -1:, :] - log_decay, 0.0)), 0.0
            )
            * block_steps
        )
        persist = jnp.where((tail_doc == last_doc)[:, None], jnp.exp(log_decay[:, -1, :]), 0.0)
        new_state = persist[:, :, None, None] * carry_state + jnp.einsum(
            "suh,suhp,sun->shpn", toward, block_values, block_keys, precision=highest_precision
        )
        return ((new_state, tail_doc), result)

    start = (
        jnp.zeros((seq_count, head_count, head_width, keys_in.shape[-1]), jnp.float32),
        jnp.full((seq_count,), -1, jnp.int32),
    )
    ignored, pieces = lax.scan(
        jax.checkpoint(advance),
        start,
        (
            to_blocks(values_in),
            to_blocks(keys_in),
            to_blocks(queries_in),
            to_blocks(step_size),
            to_blocks(segment),
        ),
    )
    return jnp.moveaxis(pieces, 0, 1).reshape(seq_count, length, head_count, head_width)


def body(
    hidden,
    pre_gain,
    zx_weight,
    bc_weight,
    step_weight,
    conv_x_weight,
    conv_x_bias,
    conv_bc_weight,
    conv_bc_bias,
    step_bias,
    decay_log,
    skip_gain,
    norm_gain,
    out_weight,
    segment_ids,
    pad_mask,
    grad_out,
):
    complete_gate_input, complete_bc_values, complete_steps, output_columns = (
        lax.all_gather(zx_weight, "dp", axis=0, tiled=True),
        lax.all_gather(bc_weight, "dp", axis=0, tiled=True),
        lax.all_gather(step_weight, "dp", axis=0, tiled=True),
        lax.all_gather(out_weight, "dp", axis=1, tiled=True),
    )
    hidden_f = hidden.astype(jnp.float32)
    inv_rms = lax.rsqrt(jnp.mean(hidden_f * hidden_f, axis=-1, keepdims=True) + epsilon)
    local_normalized = (hidden_f * inv_rms * pre_gain).astype(jnp.bfloat16)
    bc_own = jnp.einsum(
        "zbp,py->zby", local_normalized, complete_bc_values, preferred_element_type=jnp.float32
    ).astype(jnp.bfloat16)
    normalized_input, proj_bc = (
        lax.all_gather(local_normalized, "tensor", axis=1, tiled=True),
        lax.all_gather(bc_own, "tensor", axis=1, tiled=True),
    )
    seq_count, length = (normalized_input.shape[0], normalized_input.shape[1])
    head_count = complete_steps.shape[1]
    inner_here = head_count * HEADDIM
    inner_all = inner_here * lax.axis_size("tensor")
    proj_zx = jnp.einsum(
        "zbp,py->zby", normalized_input, complete_gate_input, preferred_element_type=jnp.float32
    ).astype(jnp.bfloat16)
    proj_zx = proj_zx.reshape(seq_count, length, head_count, 2, HEADDIM)
    unactivated_step = jnp.einsum(
        "qar,rj->qaj", normalized_input, complete_steps, preferred_element_type=jnp.float32
    )
    pad_f = pad_mask.astype(jnp.float32)[..., None]
    gate_in = proj_zx[:, :, :, 0, :].reshape(seq_count, length, inner_here).astype(jnp.float32)
    value_in = (
        proj_zx[:, :, :, 1, :].reshape(seq_count, length, inner_here).astype(jnp.float32) * pad_f
    )
    bc_in = proj_bc.astype(jnp.float32) * pad_f

    def convolve(source_x, source_bc, weight_x, bias_x, weight_bc, bias_bc):
        return (
            jax.nn.silu(filter_kernel_length(source_x, weight_x, bias_x, segment_ids)),
            jax.nn.silu(filter_kernel_length(source_bc, weight_bc, bias_bc, segment_ids)),
        )

    (conv_pre_x, conv_pre_bc), conv_pull = jax.vjp(
        convolve, value_in, bc_in, conv_x_weight, conv_x_bias, conv_bc_weight, conv_bc_bias
    )
    conv_values = rounded(conv_pre_x)
    conv_bc = rounded(conv_pre_bc)

    def mixer(values_f, maps_f, raw_steps, bias_steps, decay_logs, skip_heads, gate_f):
        step_size = jax.nn.softplus(raw_steps + bias_steps) * pad_f
        rates = -jnp.exp(decay_logs)
        values4 = values_f.reshape(seq_count, length, head_count, HEADDIM)
        mixed = (
            state_scan(
                values4, maps_f[..., :STATE], maps_f[..., STATE:], step_size, rates, segment_ids
            )
            + skip_heads[:, None] * values4
        )
        return mixed.reshape(seq_count, length, inner_here) * jax.nn.silu(gate_f)

    gated, mixer_pull = jax.vjp(
        mixer, conv_values, conv_bc, unactivated_step, step_bias, decay_log, skip_gain, gate_in
    )
    square_sum = lax.psum(jnp.sum(gated * gated, axis=-1), "tensor")
    gate_rms = lax.rsqrt(square_sum / inner_all + epsilon)[..., None]
    scaled = gated * gate_rms
    rescaled_mixer_result = (scaled * norm_gain).astype(jnp.bfloat16)
    partial_out = jnp.einsum(
        "mqo,ok->mqk", rescaled_mixer_result, output_columns, preferred_element_type=jnp.float32
    )
    mixed_own = lax.psum_scatter(partial_out, "tensor", scatter_dimension=1, tiled=True)
    output = (hidden_f + mixed_own).astype(jnp.bfloat16)
    sensitivity_per_token_matrix = lax.all_gather(grad_out, "tensor", axis=1, tiled=True)
    normalized_gradient = jnp.einsum(
        "oir,kr->oik",
        sensitivity_per_token_matrix,
        output_columns,
        preferred_element_type=jnp.float32,
    )
    partial_output = jnp.einsum(
        "pio,pis->os",
        rescaled_mixer_result,
        sensitivity_per_token_matrix,
        preferred_element_type=jnp.float32,
    )
    grad_norm = jnp.sum(scaled * normalized_gradient, axis=(0, 1))
    weighted = normalized_gradient * norm_gain
    cross_sum = lax.psum(jnp.sum(weighted * gated, axis=-1), "tensor")
    grad_gated = gate_rms * weighted - gated * gate_rms**3 * (cross_sum / inner_all)[..., None]
    (
        grad_values,
        grad_maps,
        sensitivity_interval_before_softplus,
        grad_step_bias,
        grad_decay,
        grad_skip,
        grad_gate,
    ) = mixer_pull(grad_gated)
    (
        sensitivity_entering_signal,
        grad_bc_in,
        grad_cxw,
        sensitivity_filter_offset_main,
        grad_cbw,
        grad_cbb,
    ) = conv_pull((grad_values, grad_maps))
    gate_input_gradient = jnp.stack(
        [
            grad_gate.reshape(seq_count, length, head_count, HEADDIM),
            (sensitivity_entering_signal * pad_f).reshape(seq_count, length, head_count, HEADDIM),
        ],
        axis=3,
    )
    gate_input_gradient = gate_input_gradient.reshape(seq_count, length, 2 * inner_here).astype(
        jnp.bfloat16
    )
    step_gradient = sensitivity_interval_before_softplus.astype(jnp.bfloat16)
    partial_gate_input_gradient = jnp.einsum(
        "fup,fuj->pj", normalized_input, gate_input_gradient, preferred_element_type=jnp.float32
    )
    grad_step_part = jnp.einsum(
        "cni,cne->ie", normalized_input, step_gradient, preferred_element_type=jnp.float32
    )
    partial_input_gradient = jnp.einsum(
        "gqt,it->gqi", gate_input_gradient, complete_gate_input, preferred_element_type=jnp.float32
    )
    partial_input_gradient = partial_input_gradient + jnp.einsum(
        "jno,ao->jna", step_gradient, complete_steps, preferred_element_type=jnp.float32
    )
    grad_normed_own, grad_bc_own = (
        lax.psum_scatter(partial_input_gradient, "tensor", scatter_dimension=1, tiled=True),
        lax.psum_scatter(grad_bc_in * pad_f, "tensor", scatter_dimension=1, tiled=True),
    )
    lower_bc_gradient = grad_bc_own.astype(jnp.bfloat16)
    grad_bc_part = jnp.einsum(
        "fup,fuj->pj", local_normalized, lower_bc_gradient, preferred_element_type=jnp.float32
    )
    grad_normed_own = grad_normed_own + jnp.einsum(
        "gqt,it->gqi", lower_bc_gradient, complete_bc_values, preferred_element_type=jnp.float32
    )
    scaled_in = hidden_f * inv_rms
    grad_pre_part = jnp.sum(scaled_in * grad_normed_own, axis=(0, 1))
    gain_grad = grad_normed_own * pre_gain
    grad_hidden = (
        grad_out.astype(jnp.float32)
        + inv_rms * gain_grad
        - hidden_f * inv_rms**3 * jnp.mean(hidden_f * gain_grad, axis=-1, keepdims=True)
    )
    grad_zx_weight, grad_step_weight, grad_out_weight, bc_rows = (
        lax.psum_scatter(partial_gate_input_gradient, "dp", scatter_dimension=0, tiled=True),
        lax.psum_scatter(grad_step_part, "dp", scatter_dimension=0, tiled=True),
        lax.psum_scatter(partial_output, "dp", scatter_dimension=1, tiled=True),
        lax.psum_scatter(grad_bc_part, "dp", scatter_dimension=0, tiled=True),
    )
    grad_bc_weight = lax.psum(bc_rows, "tensor")
    head_sums = lax.psum(
        (
            grad_cxw,
            sensitivity_filter_offset_main,
            grad_step_bias,
            grad_decay,
            grad_skip,
            grad_norm,
        ),
        "dp",
    )
    shared = lax.psum((grad_cbw, grad_cbb, grad_pre_part), ("dp", "tensor"))
    return (
        output,
        grad_hidden.astype(jnp.bfloat16),
        shared[2],
        grad_zx_weight,
        grad_bc_weight,
        grad_step_weight,
        head_sums[0],
        head_sums[1],
        shared[0],
        shared[1],
        head_sums[2],
        head_sums[3],
        head_sums[4],
        head_sums[5],
        grad_out_weight,
    )


def solution(mesh):
    placed = (
        P("dp", "tensor", None),
        P(),
        P("dp", "tensor"),
        P("dp", None),
        P("dp", "tensor"),
        P(None, "tensor"),
        P("tensor"),
        P(),
        P(),
        P("tensor"),
        P("tensor"),
        P("tensor"),
        P("tensor"),
        P("tensor", "dp"),
        P("dp", None),
        P("dp", None),
        P("dp", "tensor", None),
    )
    return jax.shard_map(
        body,
        mesh=mesh,
        in_specs=placed,
        out_specs=(
            P("dp", "tensor", None),
            P("dp", "tensor", None),
            P(),
            P("dp", "tensor"),
            P("dp", None),
            P("dp", "tensor"),
            P(None, "tensor"),
            P("tensor"),
            P(),
            P(),
            P("tensor"),
            P("tensor"),
            P("tensor"),
            P("tensor"),
            P("tensor", "dp"),
        ),
        check_vma=False,
    )
```

profile of v0, /device:TPU:0, one launch (start us, length us, event | category | flops | bytes accessed | tf_op | source)
XLA Modules:
  0.0 998.7 jit_solution(11364763153178625265)
XLA Ops:
  16.0 23.2 %all-gather.1 = bf16[16,64,16]{1,2,0:T(8,128)(2,1)S(1)} all-gather(bf16[1,64,16]{1,2,0:T(8,128)(2,1)S(1)} %bitcast.715), channel_id=1, replica_groups=mesh['dp'=16,'tensor'=2] {'dp'}, dimensions={0}, use_global_device_ids=true | all-gather | bytes 34816 | tf_op jit(solution)/shard_map/all_gather | solution.py:107
  39.4 18.9 %all_gather.24 = bf16[1024,256]{1,0:T(8,128)(2,1)S(1)} all-gather(bf16[64,256]{1,0:T(8,128)(2,1)S(1)} %copy-done.46), channel_id=1, replica_groups=mesh['dp'=16,'tensor'=2] {'dp'}, dimensions={0}, use_global_device_ids=true | all-gather | bytes 557056 | tf_op jit(solution)/shard_map/all_gather | solution.py:106
  60.2 9.2 all-gather
  73.6 2.9 fusion.194
  77.2 24.2 %all-gather.9.cloned.1.call-done = bf16[1024,2048]{1,0:T(8,128)(2,1)} async-done(((bf16[64,2048]{1,0:T(8,128)(2,1)}), bf16[1024,2048]{1,0:T(8,128)(2,1)}) %all-gather.9.cloned.1.call-update) | async-done | bytes 4194320 | tf_op jit(solution)/shard_map/all_gather | solution.py:105
  101.4 9.3 convolution_convert_fusion
  110.7 6.5 copy.266
  117.1 5.0 fusion.207
  124.7 5.3 copy.267
  130.0 2.5 broadcast_multiply_fusion
  132.6 5.2 multiply_convert_fusion.1
  137.8 4.5 reshape.1573
  142.3 7.7 copy.270
  152.5 88.8 %while.46 = (s32[]{:T(128)}, f32[1,16,64,128]{3,2,1,0:T(8,128)S(1)}, s32[1]{0:T(128)}, f32[4,1,256,16,64]{2,4,3,1,0:T(8,128)}, f32[4,1,16,64,128]{4,3,2,1,0:T(8,...) while((s32[]{:T(128)}, ...), condition=%wide.region_4.5_spmd.clone, body=%wide.region_1.4_spmd.clone.sunk | while | flops 1718706688 | bytes 9564526 | solution.py:71
  167.3 7.2 fusion.287
  189.4 7.1 fusion.287
  211.5 7.1 fusion.287
  233.6 7.1 fusion.287
  241.4 8.1 copy.301
  249.4 7.6 reshape.1568
  257.1 7.6 reshape.1567
  264.7 5.4 copy.280
  270.1 5.4 copy.276
  275.5 5.7 multiply_reduce_fusion.8
  281.1 4.9 psum.84
  286.1 10.2 %multiply_reduce_fusion.2 = (f32[1024]{0:T(1024)}, f32[1024]{0:T(1024)S(1)}, f32[1024,1024]{1,0:T(8,128)}) fusion(f32[1024]{0:T(1024)S(1)} %bitcast.685, f32[1024,1024]{1,0:T(8,128)} %copy.280, f32[1024,1024]{1,0:T(8,128)} %reshape.1568, bf16[1,1024,1024]{2,1,0:T(8,128)(2,1)S(1)} %get-tuple-element.914, f32[1024]{0:T(1024)S(1)} %mul.895, ...), kind=kOutput, calls=%fused_computation.217 | convolution fusion | flops 2162161664 | bytes 18894848 | tf_op jit(solution)/shard_map/oir,kr->oik/dot_general | solution.py:175
  296.3 4.9 psum.85
  301.3 8.1 fusion.145
  309.4 7.2 reshape.1569
  316.7 7.7 copy.289
  329.1 171.9 %while.47 = (s32[]{:T(128)}, f32[16]{0:T(128)}, f32[1,16,64,128]{3,2,1,0:T(8,128)S(1)}, f32[4,1,256,16,64]{2,4,3,1,0:T(8,128)}, f32[4,1,256,128]{3,2,0,1:T(8,128...) while((s32[]{:T(128)}, f32[16]{0:T(128)}, ...), condition=%wide.region_23.24_spmd.clone, body=%wide.region_10.23_spmd.clone.sunk | while | flops 3951227392 | bytes 28799988 | solution.py:71
  345.1 7.4 fusion.307
  365.7 5.9 fusion.314
  387.5 7.4 fusion.307
  408.7 6.0 fusion.314
  430.5 7.4 fusion.307
  451.7 6.0 fusion.314
  473.5 7.4 fusion.307
  494.7 5.9 fusion.314
  501.1 4.3 fusion.200
  508.3 7.9 fusion.142
  516.2 4.0 copy.282
  520.2 8.1 copy.305
  528.3 7.6 reshape.1570
  535.9 15.1 %multiply_reduce_fusion.6 = (f32[1024]{0:T(1024)S(1)}, f32[1024]{0:T(1024)S(1)}, f32[1024]{0:T(1024)S(1)}, f32[1024]{0:T(1024)S(1)}, f32[1024]{0:T(1024)S(1)}, /*index=5*/f32[1,1024,1024]{2,1,0:T(8,128)}) fusion(f32[1,1024,1024]{2,1,0:T(8,128)} %copy-done.2, pred[1024]{0:T(1024)(128)(4,1)S(1)} %copy-done.32, pred[1024]{0:T(1024)(128)(4,1)S(1)} %copy-done.28, ...), kind=kLoop, calls=%fused_computation.221 | loop fusion | flops 24112128 | bytes 20999168 | tf_op jit(solution)/shard_map/transpose(jvp())/reduce_sum | solution.py:25
  553.7 3.9 multiply_select_fusion.1
  557.6 2.8 fusion.140
  560.5 2.6 copy.292
  563.0 2.7 maximum_convert_fusion
  570.1 7.6 fusion.211
  577.8 2.7 add_bitcast_fusion.1
  580.6 7.2 convolution_bitcast_fusion.7
  587.9 21.5 %reduce-scatter.18.cloned.1.call-done = f32[64,256]{1,0:T(8,128)} async-done(((f32[1024,256]{1,0:T(8,128)}), f32[64,256]{1,0:T(8,128)}) %reduce-scatter.18.cloned.1.call-update) | async-done | bytes 65552 | tf_op jit(solution)/shard_map/reduce_scatter | solution.py:254
  609.4 7.3 fusion.160
  616.8 9.2 fusion.166
  626.9 57.8 %all-reduce.28 = (f32[4,1024]{1,0:T(4,128)}, f32[1024]{0:T(1024)}, f32[16]{0:T(128)}, f32[16]{0:T(128)}, f32[16]{0:T(128)}, /*index=5*/f32[1024]{0:T(1024)}) all-reduce(f32[4,1024]{1,0:T(4,128)S(1)} %pad_add_fusion, f32[1024]{0:T(1024)S(1)} %get-tuple-element.821, ...), channel_id=1, replica_groups=mesh['dp'=16,'tensor'=2] {'dp'}, use_global_device_ids=true, to_apply=%region_37.38 | all-reduce | flops 6192 | bytes 49536 | tf_op jit(solution)/shard_map/psum | solution.py:257
  686.2 37.9 %reduce-scatter.12.cloned.1.call-done = f32[1,512,1024]{2,1,0:T(8,128)} async-done(((f32[1,1024,1024]{2,1,0:T(8,128)}), f32[1,512,1024]{2,1,0:T(8,128)}) %reduce-scatter.12.cloned.1.call-update) | async-done | bytes 2097168 | tf_op jit(solution)/shard_map/reduce_scatter | solution.py:232
  724.0 2.8 fusion.152
  726.9 40.0 %all-reduce.27 = (f32[1024]{0:T(1024)}, f32[4,256]{1,0:T(4,128)}, f32[256]{0:T(256)}) all-reduce(f32[1024]{0:T(1024)S(1)} %get-tuple-element.822, f32[4,256]{1,0:T(4,128)S(1)} %pad_add_fusion.1, f32[256]{0:T(256)S(1)} %get-tuple-element.827), channel_id=1, replica_groups=mesh['dp'=16,'tensor'=2] {'dp','tensor'}, use_global_device_ids=true, to_apply=%region_28.29 | all-reduce | flops 2304 | bytes 18432 | tf_op jit(solution)/shard_map/psum | solution.py:268
  766.9 15.0 %reduce-scatter.10.cloned.1.call-done = f32[1,512,1024]{2,1,0:T(8,128)} async-done(((f32[1,1024,1024]{2,1,0:T(8,128)}), f32[1,512,1024]{2,1,0:T(8,128)}) %reduce-scatter.10.cloned.1.call-update) | async-done | bytes 2097168 | tf_op jit(solution)/shard_map/reduce_scatter | solution.py:172
  781.9 4.0 fusion.157
  785.9 18.8 %all-reduce.31.cloned.1.call-done = f32[64,256]{1,0:T(8,128)} async-done(((f32[64,256]{1,0:T(8,128)}), f32[64,256]{1,0:T(8,128)}) %all-reduce.31.cloned.1.call-update) | async-done | bytes 65552 | tf_op jit(solution)/shard_map/psum | solution.py:256
  804.7 77.4 %reduce-scatter.20.cloned.1.call-done = f32[1024,64]{0,1:T(8,128)} async-done(((f32[1024,1024]{0,1:T(8,128)}), f32[1024,64]{0,1:T(8,128)}) %reduce-scatter.20.cloned.1.call-update) | async-done | bytes 262160 | tf_op jit(solution)/shard_map/reduce_scatter | solution.py:253
  882.1 108.0 %reduce-scatter.16.cloned.1.call-done = f32[64,2048]{1,0:T(8,128)} async-done(((f32[1024,2048]{1,0:T(8,128)}), f32[64,2048]{1,0:T(8,128)}) %reduce-scatter.16.cloned.1.call-update) | async-done | bytes 524304 | tf_op jit(solution)/shard_map/reduce_scatter | solution.py:251
  (580 shorter events, 205.2 us)
Async XLA Ops:
  7.2 7.5 copy-start.71
  7.2 8.4 copy-start.66
  7.2 8.5 copy-start.67
  7.2 8.5 copy-start.70
  7.2 8.7 copy-start.50
  7.2 8.8 copy-start.64
  7.2 32.1 %copy-start.46 = (bf16[64,256]{1,0:T(8,128)(2,1)S(1)}, bf16[64,256]{1,0:T(8,128)(2,1)}, u32[]{:S(2)}) copy-start(bf16[64,256]{1,0:T(8,128)(2,1)} %param.24) | copy-start | bytes 98308
  7.3 66.4 %all-gather.7.cloned.1.call-start = ((), (), s32[]{:S(2)}) async-start(), calls=%async_computation.7 | async-start | bytes 3145728 | tf_op jit(solution)/shard_map/all_gather | solution.py:117
  12.5 57.7 %copy-start.68 = (f32[256]{0:T(256)S(1)}, f32[256]{0:T(256)}, u32[]{:S(2)}) copy-start(f32[256]{0:T(256)} %param.29) | copy-start | bytes 3076
  12.5 88.9 %all-gather.9.cloned.1.call-start = ((), (), s32[]{:S(2)}) async-start(), calls=%async_computation.8 | async-start | bytes 4456448 | tf_op jit(solution)/shard_map/all_gather | solution.py:105
  13.3 272.8 %all-gather.13.cloned.1.call-start = ((), (), s32[]{:S(2)}) async-start(), calls=%async_computation.11 | async-start | bytes 3145728 | tf_op jit(solution)/shard_map/all_gather | solution.py:174
  14.0 272.1 %all-gather.11.cloned.1.call-start = ((), (), s32[]{:S(2)}) async-start(), calls=%async_computation.9 | async-start | bytes 2228224 | tf_op jit(solution)/shard_map/all_gather | solution.py:108
  14.6 536.5 %reduce-scatter.14.cloned.1.call-start = ((), (), s32[]{:S(2)}) async-start(), calls=%async_computation.13 | async-start | bytes 1572864 | tf_op jit(solution)/shard_map/reduce_scatter | solution.py:233
  15.6 116.9 %copy-start.27 = (pred[1024]{0:T(1024)(128)(4,1)}, pred[1024]{0:T(1024)(128)(4,1)S(1)}, u32[]{:S(2)}) copy-start(pred[1024]{0:T(1024)(128)(4,1)S(1)} %get-tuple-element.832) | copy-start | bytes 3076
  15.7 116.9 %copy-start.29 = (pred[1024]{0:T(1024)(128)(4,1)}, pred[1024]{0:T(1024)(128)(4,1)S(1)}, u32[]{:S(2)}) copy-start(pred[1024]{0:T(1024)(128)(4,1)S(1)} %get-tuple-element.833) | copy-start | bytes 3076
  15.7 116.9 %copy-start.31 = (pred[1024]{0:T(1024)(128)(4,1)}, pred[1024]{0:T(1024)(128)(4,1)S(1)}, u32[]{:S(2)}) copy-start(pred[1024]{0:T(1024)(128)(4,1)S(1)} %get-tuple-element.834) | copy-start | bytes 3076
  15.7 114.3 %copy-start.16 = (f32[1,1024]{1,0:T(1,128)}, f32[1,1024]{1,0:T(1,128)S(1)}, u32[]{:S(2)}) copy-start(f32[1,1024]{1,0:T(1,128)S(1)} %convert_element_type.132) | copy-start | bytes 12292
  15.7 57.8 %copy-start.54 = (f32[1,256]{1,0:T(1,128)}, f32[1,256]{1,0:T(1,128)S(1)}, u32[]{:S(2)}) copy-start(f32[1,256]{1,0:T(1,128)S(1)} %get-tuple-element.948) | copy-start | bytes 3076
  15.7 57.8 %copy-start.56 = (f32[1,256]{1,0:T(1,128)}, f32[1,256]{1,0:T(1,128)S(1)}, u32[]{:S(2)}) copy-start(f32[1,256]{1,0:T(1,128)S(1)} %get-tuple-element.949) | copy-start | bytes 3076
  15.8 57.8 %copy-start.58 = (f32[1,256]{1,0:T(1,128)}, f32[1,256]{1,0:T(1,128)S(1)}, u32[]{:S(2)}) copy-start(f32[1,256]{1,0:T(1,128)S(1)} %get-tuple-element.950) | copy-start | bytes 3076
  15.8 57.8 %copy-start.60 = (f32[1,256]{1,0:T(1,128)}, f32[1,256]{1,0:T(1,128)S(1)}, u32[]{:S(2)}) copy-start(f32[1,256]{1,0:T(1,128)S(1)} %get-tuple-element.951) | copy-start | bytes 3076
  15.9 285.3 %copy-start.21 = (f32[1024]{0:T(1024)}, f32[1024]{0:T(1024)S(1)}, u32[]{:S(2)}) copy-start(f32[1024]{0:T(1024)S(1)} %mul.895) | copy-start | bytes 12292
  15.9 116.6 %copy-start.33 = (f32[1,1024]{1,0:T(1,128)}, f32[1,1024]{1,0:T(1,128)S(1)}, u32[]{:S(2)}) copy-start(f32[1,1024]{1,0:T(1,128)S(1)} %get-tuple-element.945) | copy-start | bytes 12292
  16.0 116.6 %copy-start.35 = (f32[1,1024]{1,0:T(1,128)}, f32[1,1024]{1,0:T(1,128)S(1)}, u32[]{:S(2)}) copy-start(f32[1,1024]{1,0:T(1,128)S(1)} %get-tuple-element.946) | copy-start | bytes 12292
  16.0 116.6 %copy-start.37 = (f32[1,1024]{1,0:T(1,128)}, f32[1,1024]{1,0:T(1,128)S(1)}, u32[]{:S(2)}) copy-start(f32[1,1024]{1,0:T(1,128)S(1)} %get-tuple-element.947) | copy-start | bytes 12292
  16.0 116.6 %copy-start.44 = (f32[1,1024]{1,0:T(1,128)}, f32[1,1024]{1,0:T(1,128)S(1)}, u32[]{:S(2)}) copy-start(f32[1,1024]{1,0:T(1,128)S(1)} %get-tuple-element.944) | copy-start | bytes 12292
  39.4 34.2 %copy-start.12 = (bf16[1024,16]{0,1:T(8,128)(2,1)}, bf16[1024,16]{0,1:T(8,128)(2,1)S(1)}, u32[]{:S(2)}) copy-start(bf16[1024,16]{0,1:T(8,128)(2,1)S(1)} %reshape.1526) | copy-start | bytes 98308
  58.3 11.2 %copy-start.10 = (bf16[1024,256]{1,0:T(8,128)(2,1)}, bf16[1024,256]{1,0:T(8,128)(2,1)S(1)}, u32[]{:S(2)}) copy-start(bf16[1024,256]{1,0:T(8,128)(2,1)S(1)} %all_gather.24) | copy-start | bytes 1572868
  58.3 15.4 %copy-start.69 = (f32[16]{0:T(128)S(1)}, f32[16]{0:T(128)}, u32[]{:S(2)}) copy-start(f32[16]{0:T(128)} %param.30) | copy-start | bytes 196
  69.6 41.1 %copy-start.6 = (f32[1,1024,256]{2,1,0:T(8,128)}, f32[1,1024,256]{2,1,0:T(8,128)S(1)}, u32[]{:S(2)}) copy-start(f32[1,1024,256]{2,1,0:T(8,128)S(1)} %convert_multiply_fusion.4) | copy-start | bytes 3145732
  137.8 163.5 %copy-start = (bf16[1,1024,1024]{2,1,0:T(8,128)(2,1)}, bf16[1,1024,1024]{2,1,0:T(8,128)(2,1)S(1)}, u32[]{:S(2)}) copy-start(bf16[1,1024,1024]{2,1,0:T(8,128)(2,1)S(1)} %get-tuple-element.914) | copy-start | bytes 6291460
  275.4 10.7 %copy-start.51 = (f32[1024]{0:T(1024)S(1)}, f32[1024]{0:T(1024)}, u32[]{:S(2)}) copy-start(f32[1024]{0:T(1024)} %param.33) | copy-start | bytes 12292
  286.0 15.2 %copy-start.23 = (f32[1,1024]{1,0:T(1,128)}, f32[1,1024]{1,0:T(1,128)S(1)}, u32[]{:S(2)}) copy-start(f32[1,1024]{1,0:T(1,128)S(1)} %add_rsqrt_fusion) | copy-start | bytes 12292
  286.1 15.2 %copy-start.40 = (f32[1024]{0:T(1024)}, f32[1024]{0:T(1024)S(1)}, u32[]{:S(2)}) copy-start(f32[1024]{0:T(1024)S(1)} %multiply_multiply_fusion.1) | copy-start | bytes 12292
  301.3 8.2 copy-start.42
  329.3 11.6 %copy-start.25 = (f32[16]{0:T(128)}, f32[16]{0:T(128)S(1)}, u32[]{:S(2)}) copy-start(f32[16]{0:T(128)S(1)} %get-tuple-element.1180) | copy-start | bytes 196 | tf_op jit(solution)/shard_map/transpose(jvp())/while
  341.1 11.4 %copy-start.11 = (f32[256,16]{0,1:T(8,128)}, f32[256,16]{0,1:T(8,128)S(1)}, u32[]{:S(2)}) copy-start(f32[256,16]{0,1:T(8,128)S(1)} %fusion.305) | copy-start | bytes 49156 | tf_op jit(solution)/shard_map/transpose(jvp())/while
  341.9 15.0 %copy-start.18 = (f32[16]{0:T(128)}, f32[16]{0:T(128)S(1)}, u32[]{:S(2)}) copy-start(f32[16]{0:T(128)S(1)} %get-tuple-element.1194) | copy-start | bytes 196 | tf_op jit(solution)/shard_map/transpose(jvp())/while
  345.1 7.4 copy-start.8
  371.6 11.6 %copy-start.25 = (f32[16]{0:T(128)}, f32[16]{0:T(128)S(1)}, u32[]{:S(2)}) copy-start(f32[16]{0:T(128)S(1)} %get-tuple-element.1180) | copy-start | bytes 196 | tf_op jit(solution)/shard_map/transpose(jvp())/while
  383.5 11.4 %copy-start.11 = (f32[256,16]{0,1:T(8,128)}, f32[256,16]{0,1:T(8,128)S(1)}, u32[]{:S(2)}) copy-start(f32[256,16]{0,1:T(8,128)S(1)} %fusion.305) | copy-start | bytes 49156 | tf_op jit(solution)/shard_map/transpose(jvp())/while
  384.2 15.0 %copy-start.18 = (f32[16]{0:T(128)}, f32[16]{0:T(128)S(1)}, u32[]{:S(2)}) copy-start(f32[16]{0:T(128)S(1)} %get-tuple-element.1194) | copy-start | bytes 196 | tf_op jit(solution)/shard_map/transpose(jvp())/while
  414.6 11.6 %copy-start.25 = (f32[16]{0:T(128)}, f32[16]{0:T(128)S(1)}, u32[]{:S(2)}) copy-start(f32[16]{0:T(128)S(1)} %get-tuple-element.1180) | copy-start | bytes 196 | tf_op jit(solution)/shard_map/transpose(jvp())/while
  426.5 11.4 %copy-start.11 = (f32[256,16]{0,1:T(8,128)}, f32[256,16]{0,1:T(8,128)S(1)}, u32[]{:S(2)}) copy-start(f32[256,16]{0,1:T(8,128)S(1)} %fusion.305) | copy-start | bytes 49156 | tf_op jit(solution)/shard_map/transpose(jvp())/while
  427.2 15.0 %copy-start.18 = (f32[16]{0:T(128)}, f32[16]{0:T(128)S(1)}, u32[]{:S(2)}) copy-start(f32[16]{0:T(128)S(1)} %get-tuple-element.1194) | copy-start | bytes 196 | tf_op jit(solution)/shard_map/transpose(jvp())/while
  457.6 11.6 %copy-start.25 = (f32[16]{0:T(128)}, f32[16]{0:T(128)S(1)}, u32[]{:S(2)}) copy-start(f32[16]{0:T(128)S(1)} %get-tuple-element.1180) | copy-start | bytes 196 | tf_op jit(solution)/shard_map/transpose(jvp())/while
  469.5 11.4 %copy-start.11 = (f32[256,16]{0,1:T(8,128)}, f32[256,16]{0,1:T(8,128)S(1)}, u32[]{:S(2)}) copy-start(f32[256,16]{0,1:T(8,128)S(1)} %fusion.305) | copy-start | bytes 49156 | tf_op jit(solution)/shard_map/transpose(jvp())/while
  470.2 15.0 %copy-start.18 = (f32[16]{0:T(128)}, f32[16]{0:T(128)S(1)}, u32[]{:S(2)}) copy-start(f32[16]{0:T(128)S(1)} %get-tuple-element.1194) | copy-start | bytes 196 | tf_op jit(solution)/shard_map/transpose(jvp())/while
  507.8 101.5 %reduce-scatter.18.cloned.1.call-start = ((), (), s32[]{:S(2)}) async-start(), calls=%async_computation.15 | async-start | bytes 1114112 | tf_op jit(solution)/shard_map/reduce_scatter | solution.py:254
  535.9 15.1 %copy-start.5 = (bf16[1,512,1024]{2,1,0:T(8,128)(2,1)S(1)}, bf16[1,512,1024]{2,1,0:T(8,128)(2,1)}, u32[]{:S(2)}) copy-start(bf16[1,512,1024]{2,1,0:T(8,128)(2,1)} %fusion.151) | copy-start | bytes 3145732
  535.9 17.7 %copy-start.34 = (f32[1,1024]{1,0:T(1,128)S(1)}, f32[1,1024]{1,0:T(1,128)}, u32[]{:S(2)}) copy-start(f32[1,1024]{1,0:T(1,128)} %copy-done.33) | copy-start | bytes 12292
  535.9 17.7 %copy-start.36 = (f32[1,1024]{1,0:T(1,128)S(1)}, f32[1,1024]{1,0:T(1,128)}, u32[]{:S(2)}) copy-start(f32[1,1024]{1,0:T(1,128)} %copy-done.35) | copy-start | bytes 12292
  535.9 17.7 %copy-start.38 = (f32[1,1024]{1,0:T(1,128)S(1)}, f32[1,1024]{1,0:T(1,128)}, u32[]{:S(2)}) copy-start(f32[1,1024]{1,0:T(1,128)} %copy-done.37) | copy-start | bytes 12292
  553.6 131.2 %reduce-scatter.22.cloned.1.call-start = ((), (), s32[]{:S(2)}) async-start(), calls=%async_computation.18 | async-start | bytes 557056
  570.1 154.0 %reduce-scatter.12.cloned.1.call-start = ((), (), s32[]{:S(2)}) async-start(), calls=%async_computation.12 | async-start | bytes 6291456 | tf_op jit(solution)/shard_map/reduce_scatter | solution.py:232
  570.1 7.7 copy-start.13
  580.5 201.4 %reduce-scatter.10.cloned.1.call-start = ((), (), s32[]{:S(2)}) async-start(), calls=%async_computation.10 | async-start | bytes 6291456 | tf_op jit(solution)/shard_map/reduce_scatter | solution.py:172
  587.8 216.9 %all-reduce.31.cloned.1.call-start = ((), (), s32[]{:S(2)}) async-start(), calls=%async_computation.16 | async-start | bytes 131072 | tf_op jit(solution)/shard_map/psum | solution.py:256
  609.4 272.8 %reduce-scatter.20.cloned.1.call-start = ((), (), s32[]{:S(2)}) async-start(), calls=%async_computation.17 | async-start | bytes 4456448 | tf_op jit(solution)/shard_map/reduce_scatter | solution.py:253
  616.7 373.4 %reduce-scatter.16.cloned.1.call-start = ((), (), s32[]{:S(2)}) async-start(), calls=%async_computation.14 | async-start | bytes 8912896 | tf_op jit(solution)/shard_map/reduce_scatter | solution.py:251
  626.0 98.1 %copy-start.4 = (bf16[1,512,1024]{2,1,0:T(8,128)(2,1)S(1)}, bf16[1,512,1024]{2,1,0:T(8,128)(2,1)}, u32[]{:S(2)}) copy-start(bf16[1,512,1024]{2,1,0:T(8,128)(2,1)} %param.21) | copy-start | bytes 3145732
  626.0 98.1 %copy-start.39 = (f32[1024]{0:T(1024)S(1)}, f32[1024]{0:T(1024)}, u32[]{:S(2)}) copy-start(f32[1024]{0:T(1024)} %param.22) | copy-start | bytes 12292
  626.0 98.0 %copy-start.48 = (f32[512]{0:T(512)S(1)}, f32[512]{0:T(512)}, u32[]{:S(2)}) copy-start(f32[512]{0:T(512)} %copy-done.47) | copy-start | bytes 6148
  626.0 155.9 %copy-start.62 = (f32[512]{0:T(512)S(1)}, f32[512]{0:T(512)}, u32[]{:S(2)}) copy-start(f32[512]{0:T(512)} %get-tuple-element.952) | copy-start | bytes 6148
  (42 other events, 165.3 us)
Sparse Core Ops, SparseCore 0:
  12.6 35.8 all-gather.6
  50.6 50.7 all-gather.8
  102.9 31.6 all-gather.12
  136.6 41.3 all-gather.10
  507.9 18.8 reduce-scatter.13
  553.7 55.6 reduce-scatter.17
  613.4 54.7 reduce-scatter.21
  670.7 53.3 reduce-scatter.11
  726.3 55.5 reduce-scatter.9
  784.1 20.5 all-reduce.30
  809.6 72.4 reduce-scatter.19
  886.6 103.5 reduce-scatter.15
where the time goes:
time: 1010 us; the launch traced here: 999 us
  waiting for transfers between devices  305 us (30%)
  matrix products  204 us (20%)
  local copies, waits for them, and re-layouts  175 us (17%)
  blocking collectives  159 us (16%)
  other arithmetic  127 us (13%)
  between operations  15.4 us (2%)
  loops' own time  12.7 us (1%)
    reduce_scatter x1, waiting for transfers between devices, body(): lax.psum_scatter(partial_gate_input_gradient, 'dp', scatter_dimension=0,...  108 us
    dot_general x12, matrix products, advance(): jnp.einsum('stuh,suhp->sthp', mixing, block_values, precision=highest_pre...  81.8 us
    reduce_scatter x1, waiting for transfers between devices, body(): lax.psum_scatter(partial_output, 'dp', scatter_dimension=1, tiled=True)  77.4 us
    psum x1, blocking collectives, body(): lax.psum((grad_cxw, sensitivity_filter_offset_main, grad_step_bias, grad_...  57.8 us
    psum x1, blocking collectives, body(): shared = lax.psum((grad_cbw, grad_cbb, grad_pre_part), ('dp', 'tensor'))  40 us
    reduce_scatter x1, waiting for transfers between devices, body(): lax.psum_scatter(partial_input_gradient, 'tensor', scatter_dimension=1, t...  37.9 us
    all_gather x1, waiting for transfers between devices, body(): lax.all_gather(zx_weight, 'dp', axis=0, tiled=True)  24.2 us
    squeeze x24, local copies, waits for them, and re-layouts, state_scan(): lax.scan(jax.checkpoint(advance), start, (to_blocks(values_in), to_blocks...  23.4 us
  transfers between devices with their start and end apart: 12, of which 7 were waited for; matrix products, arithmetic and copies ran while one was open for 29% of the time, Pallas kernels for 0%

commit v1 on v0

v1 whole, which is shorter than its diff:
```python
import functools
import jax
import jax.numpy as jnp
from jax import lax
from jax.experimental import pallas as pl
from jax.experimental.pallas import tpu as pltpu
from jax.sharding import PartitionSpec as P

HEADDIM = 64
STATE = 128
CHUNK = 128
TAPS = 4
HALO = 8
AUX = 16
LOG2E = 1.4426950408889634
FAR = -1e30
epsilon = 1e-05
BF = jnp.bfloat16
F32 = jnp.float32


def sigmoid(v):
    return 0.5 * jnp.tanh(0.5 * v) + 0.5


def split3(v):
    a = v.astype(BF)
    r = v - a.astype(F32)
    b = r.astype(BF)
    c = (r - b.astype(F32)).astype(BF)
    return a, b, c


def dot_nn(a, b):
    return lax.dot_general(a, b, (((1,), (0,)), ((), ())), preferred_element_type=F32)


def dot_nt(a, b):
    return lax.dot_general(a, b, (((1,), (1,)), ((), ())), preferred_element_type=F32)


def exact_dot(v, ones):
    rows = v.shape[0]
    out = dot_nn(jnp.concatenate(split3(v), axis=0), ones)
    return out[:rows] + out[rows : 2 * rows] + out[2 * rows :]


def iota2(shape, dim):
    return lax.broadcasted_iota(jnp.int32, shape, dim)


def pieces(raw, bias, rate, aux, tri):
    pad = aux[1:2]
    pre = raw + bias
    soft = jnp.maximum(pre, 0.0) + jnp.log1p(jnp.exp(-jnp.abs(pre)))
    dt = soft * pad
    cum = exact_dot(dt * rate, tri) * LOG2E
    carried = jnp.exp2(cum) * aux[5:6]
    toward = jnp.exp2(cum[:, CHUNK - 1 : CHUNK] - cum) * aux[6:7]
    return dt, cum, carried, toward


def expander(heads, inner, place):
    row = lax.rem(iota2((256, inner), 0), 128)
    head = lax.div(iota2((256, inner), 1), HEADDIM)
    return jnp.where(row == head + place, 1.0, 0.0).astype(BF)


def collector(inner, place):
    head = lax.div(iota2((inner, 128), 0), HEADDIM)
    lane = iota2((inner, 128), 1)
    return jnp.where(lane == head + place, 1.0, 0.0).astype(BF)


def hi_lo(cols):
    hi = cols.astype(BF)
    return jnp.concatenate([hi, (cols - hi.astype(F32)).astype(BF)], axis=1)


def compact(rows_list):
    used = sum(r.shape[0] for r in rows_list)
    if used < 128:
        rows_list = list(rows_list) + [jnp.zeros((128 - used, CHUNK), F32)]
    return jnp.concatenate(rows_list, axis=0).T


def split_pair(first, second, low):
    gate = jnp.where(low, first, pltpu.roll(second, HEADDIM, 1))
    value = jnp.where(low, pltpu.roll(first, HEADDIM, 1), second)
    return gate, value


def forward_kernel(
    heads, zx_ref, bc_ref, raw_ref, aux_ref, g_ref, cw_ref, cbw_ref, hp_ref,
    mixed_ref, gated_ref, cv_ref, pre_ref, cbc_ref, pbc_ref, st_ref, stat_ref,
    state, ubuf, bbuf, vd, yint, expand, tri_ref,
):
    inner = heads * HEADDIM
    pairs = heads // 2
    first = (pl.program_id(0) == 0) & (pl.program_id(1) == 0)

    @pl.when(first)
    def _():
        for i, place in enumerate((AUX + heads, AUX + 2 * heads, AUX + 3 * heads)):
            expand[i] = expander(heads, inner, place)
        tri_ref[...] = jnp.where(iota2((CHUNK, CHUNK), 0) <= iota2((CHUNK, CHUNK), 1), 1.0, 0.0).astype(BF)

    @pl.when(pl.program_id(1) == 0)
    def _():
        state[...] = jnp.zeros_like(state)
        ubuf[0:HALO] = jnp.zeros((HALO, inner), F32)
        bbuf[0:HALO] = jnp.zeros((HALO, 2 * STATE), F32)

    aux = aux_ref[0]
    dt, cum, carried, toward = pieces(raw_ref[0], hp_ref[0], hp_ref[1], aux, tri_ref[...])
    cols = compact([aux, cum, dt, carried, toward])
    both = hi_lo(cols)
    dtx = dot_nn(both, expand[0])
    carx = dot_nn(both, expand[1])
    towx = dot_nn(both, expand[2])
    pad = cols[:, 1:2]
    same = [None] + [cols[:, 1 + k : 2 + k] for k in range(1, TAPS)]
    low = iota2((CHUNK, 128), 1) < HEADDIM

    bbuf[HALO:] = bc_ref[0].astype(F32) * pad
    maps = cbw_ref[TAPS : TAPS + 1] + cbw_ref[0:1] * bbuf[HALO:]
    for k in range(1, TAPS):
        maps = maps + cbw_ref[k : k + 1] * (same[k] * bbuf[HALO - k : HALO - k + CHUNK])
    pbc_ref[0] = maps.astype(BF)
    maps = (maps * sigmoid(maps)).astype(BF)
    cbc_ref[0] = maps
    bbuf[0:HALO] = bbuf[CHUNK : CHUNK + HALO]
    keys, queries = maps[:, :STATE], maps[:, STATE:]
    scores = dot_nt(queries, keys)
    keys_t = keys.astype(F32).T.astype(BF)

    for p in range(pairs):
        s = slice(128 * p, 128 * p + 128)
        x0 = zx_ref[0, :, 256 * p : 256 * p + 128].astype(F32)
        x1 = zx_ref[0, :, 256 * p + 128 : 256 * p + 256].astype(F32)
        value = jnp.where(low, pltpu.roll(x0, HEADDIM, 1), x1)
        ubuf[HALO:, s] = value * pad
        pre = cw_ref[TAPS : TAPS + 1, s] + cw_ref[0:1, s] * ubuf[HALO:, s]
        for k in range(1, TAPS):
            pre = pre + cw_ref[k : k + 1, s] * (same[k] * ubuf[HALO - k : HALO - k + CHUNK, s])
        pre_ref[0, :, s] = pre.astype(BF)
        cv = (pre * sigmoid(pre)).astype(BF)
        cv_ref[0, :, s] = cv
        vd[:, s] = (cv.astype(F32) * dtx[:, s]).astype(BF)
    ubuf[0:HALO] = ubuf[CHUNK : CHUNK + HALO]

    old = state[...]
    old_b = old.astype(BF)
    st_ref[0, 0] = old_b
    yint[...] = dot_nn(queries, old_b) * carx
    state[...] = carx[CHUNK - 1 : CHUNK] * old + dot_nn(keys_t, (vd[...].astype(F32) * towx).astype(BF))

    inside = (iota2((CHUNK, CHUNK), 0) >= iota2((CHUNK, CHUNK), 1)) & (cols[:, 0:1] == aux[0:1])
    fence = jnp.where(inside, 0.0, FAR)
    squares = jnp.zeros((CHUNK, 128), F32)
    cross = jnp.zeros((CHUNK, 128), F32)
    for p in range(pairs):
        s = slice(128 * p, 128 * p + 128)
        mix = []
        for h in (2 * p, 2 * p + 1):
            decay = jnp.exp2(cols[:, AUX + h : AUX + h + 1] - cum[h : h + 1] + fence)
            mix.append((scores * decay).astype(BF))
        v = vd[:, s]
        zero = jnp.zeros_like(v)
        stacked = jnp.concatenate([jnp.where(low, v, zero), jnp.where(low, zero, v)], axis=0)
        y = dot_nn(jnp.concatenate(mix, axis=1), stacked)
        mixed = y + yint[:, s] + cw_ref[5:6, s] * cv_ref[0, :, s].astype(F32)
        x0 = zx_ref[0, :, 256 * p : 256 * p + 128].astype(F32)
        x1 = zx_ref[0, :, 256 * p + 128 : 256 * p + 256].astype(F32)
        gate = jnp.where(low, x0, pltpu.roll(x1, HEADDIM, 1))
        gated = mixed * (gate * sigmoid(gate))
        mixed_ref[0, :, s] = mixed.astype(BF)
        gated_ref[0, :, s] = gated.astype(BF)
        squares = squares + gated * gated
        cross = cross + gated * (g_ref[0, :, s].astype(F32) * cw_ref[6:7, s])
    lane = iota2((CHUNK, 128), 1)
    sums = jnp.where(lane == 0, jnp.sum(squares, axis=1, keepdims=True), 0.0)
    sums = jnp.where(lane == 1, jnp.sum(cross, axis=1, keepdims=True), sums)
    stat_ref[0] = sums.T[0:8]


def backward_kernel(
    heads, zx_ref, bc_ref, raw_ref, aux_ref, g_ref, mixed_ref, cv_ref, pre_ref, cbc_ref, pbc_ref,
    st_ref, stat_ref, cw_ref, cbw_ref, hp_ref,
    gzx_ref, gbc_ref, gstep_ref, gch_ref, gmap_ref, ghead_ref,
    dstate, cbuf, dbuf, vd, gm_s, gmc_s, ggate_s, cs_s, bs_s, expand, collect, tri_ref, suf_ref,
):
    inner = heads * HEADDIM
    pairs = heads // 2
    first = (pl.program_id(0) == 0) & (pl.program_id(1) == 0)

    @pl.when(first)
    def _():
        for i, place in enumerate((AUX + heads, AUX + 2 * heads, AUX + 3 * heads)):
            expand[i] = expander(heads, inner, place)
        collect[0] = collector(inner, heads)
        collect[1] = collector(inner, 2 * heads)
        r, c = iota2((CHUNK, CHUNK), 0), iota2((CHUNK, CHUNK), 1)
        tri_ref[...] = jnp.where(r <= c, 1.0, 0.0).astype(BF)
        suf_ref[...] = jnp.where(r >= c, 1.0, 0.0).astype(BF)
        gch_ref[...] = jnp.zeros_like(gch_ref)
        gmap_ref[...] = jnp.zeros_like(gmap_ref)
        ghead_ref[...] = jnp.zeros_like(ghead_ref)

    @pl.when(pl.program_id(1) == 0)
    def _():
        dstate[...] = jnp.zeros_like(dstate)
        cbuf[CHUNK:] = jnp.zeros((HALO, inner), F32)
        dbuf[CHUNK:] = jnp.zeros((HALO, 2 * STATE), F32)

    aux = aux_ref[0]
    rate = hp_ref[1]
    dt, cum, carried, toward = pieces(raw_ref[0], hp_ref[0], rate, aux, tri_ref[...])
    cols = compact([aux, cum, dt, carried, toward, stat_ref[0]])
    both = hi_lo(cols)
    dtx = dot_nn(both, expand[0])
    carx = dot_nn(both, expand[1])
    towx = dot_nn(both, expand[2])
    pad = cols[:, 1:2]
    ahead = [None] + [cols[:, 7 + k : 8 + k] for k in range(1, TAPS)]
    base = AUX + 4 * heads
    rms, pull = cols[:, base : base + 1], cols[:, base + 1 : base + 2]
    low = iota2((CHUNK, 128), 1) < HEADDIM
    maps = cbc_ref[0]
    keys, queries = maps[:, :STATE], maps[:, STATE:]
    queries_t = queries.astype(F32).T.astype(BF)
    scores_t = dot_nt(keys, queries)

    for p in range(pairs):
        s = slice(128 * p, 128 * p + 128)
        x0 = zx_ref[0, :, 256 * p : 256 * p + 128].astype(F32)
        x1 = zx_ref[0, :, 256 * p + 128 : 256 * p + 256].astype(F32)
        gate = jnp.where(low, x0, pltpu.roll(x1, HEADDIM, 1))
        sig = sigmoid(gate)
        act = gate * sig
        mixed = mixed_ref[0, :, s].astype(F32)
        gated = mixed * act
        g = g_ref[0, :, s].astype(F32)
        grad_gated = rms * (g * cw_ref[6:7, s]) - gated * pull
        gm = grad_gated * act
        ggate_s[:, s] = (grad_gated * mixed * (sig * (1.0 + gate * (1.0 - sig)))).astype(BF)
        gm_s[:, s] = gm.astype(BF)
        gmc_s[:, s] = (gm * carx[:, s]).astype(BF)
        cv = cv_ref[0, :, s].astype(F32)
        vd[:, s] = (cv * dtx[:, s]).astype(BF)
        gch_ref[5:6, s] += jnp.sum(gm * cv, axis=0, keepdims=True)
        gch_ref[6:7, s] += jnp.sum(gated * rms * g, axis=0, keepdims=True)

    ds = dstate[...]
    ds_b = ds.astype(BF)
    st = st_ref[0, 0]
    gmc = gmc_s[...]
    cs = dot_nn(queries, st)
    bs = dot_nn(keys, ds_b) * towx
    bs_s[...] = bs
    reach = dot_nn((gmc.astype(F32) * cs).astype(BF), collect[1])
    reach = reach + dot_nn((bs * cv_ref[0].astype(F32)).astype(BF), collect[0])
    grad_q = dot_nt(gmc, st)
    grad_k = dot_nt((vd[...].astype(F32) * towx).astype(BF), ds_b)
    keep = carx[CHUNK - 1 : CHUNK]
    held = jnp.sum(st.astype(F32) * ds, axis=0, keepdims=True) * keep
    dstate[...] = keep * ds + dot_nn(queries_t, gmc)

    inside = (iota2((CHUNK, CHUNK), 0) <= iota2((CHUNK, CHUNK), 1)) & (cols[:, 0:1] == aux[0:1])
    fence = jnp.where(inside, 0.0, FAR)
    grad_scores_t = jnp.zeros((CHUNK, CHUNK), F32)
    lane = iota2((CHUNK, 128), 1)
    gathered = reach
    row_sums = []
    for p in range(pairs):
        s = slice(128 * p, 128 * p + 128)
        gm_b = gm_s[:, s]
        zero = jnp.zeros_like(gm_b)
        gm_two = jnp.concatenate([jnp.where(low, gm_b, zero), jnp.where(low, zero, gm_b)], axis=0)
        near = dot_nt(vd[:, s], gm_two)
        mix = []
        for j in range(2):
            h = 2 * p + j
            decay = jnp.exp2(cum[h : h + 1] - cols[:, AUX + h : AUX + h + 1] + fence)
            mix.append((scores_t * decay).astype(BF))
            weighed = decay * near[:, CHUNK * j : CHUNK * j + CHUNK]
            grad_scores_t = grad_scores_t + weighed
            pairs_g = weighed * scores_t
            row_sums.append(jnp.sum(pairs_g, axis=0, keepdims=True))
            gathered = jnp.where(lane == h, jnp.sum(pairs_g, axis=1, keepdims=True), gathered)
        z = dot_nn(jnp.concatenate(mix, axis=1), gm_two)
        gm = gm_b.astype(F32)
        grad_v = cw_ref[5:6, s] * gm + dtx[:, s] * (z + bs_s[:, s])
        x0 = zx_ref[0, :, 256 * p : 256 * p + 128].astype(F32)
        x1 = zx_ref[0, :, 256 * p + 128 : 256 * p + 256].astype(F32)
        u = jnp.where(low, pltpu.roll(x0, HEADDIM, 1), x1) * pad
        pre = pre_ref[0, :, s].astype(F32)
        sig = sigmoid(pre)
        c = grad_v * (sig * (1.0 + pre * (1.0 - sig)))
        cbuf[0:CHUNK, s] = c
        gu = cw_ref[0:1, s] * c
        gch_ref[4:5, s] += jnp.sum(c, axis=0, keepdims=True)
        gch_ref[0:1, s] += jnp.sum(c * u, axis=0, keepdims=True)
        for k in range(1, TAPS):
            shifted = ahead[k] * cbuf[k : k + CHUNK, s]
            gu = gu + cw_ref[k : k + 1, s] * shifted
            gch_ref[k : k + 1, s] += jnp.sum(shifted * u, axis=0, keepdims=True)
        gu = gu * pad
        ggate = ggate_s[:, s].astype(F32)
        gzx_ref[0, :, 256 * p : 256 * p + 128] = jnp.where(low, ggate, pltpu.roll(gu, HEADDIM, 1)).astype(BF)
        gzx_ref[0, :, 256 * p + 128 : 256 * p + 256] = jnp.where(low, pltpu.roll(ggate, HEADDIM, 1), gu).astype(BF)
    cbuf[CHUNK:] = cbuf[0:HALO]

    gst = grad_scores_t.astype(BF)
    grad_k = grad_k + dot_nn(gst, queries)
    grad_q = grad_q + dot_nn(grad_scores_t.T.astype(BF), keys)
    pbc = pbc_ref[0].astype(F32)
    sig = sigmoid(pbc)
    c = jnp.concatenate([grad_k, grad_q], axis=1) * (sig * (1.0 + pbc * (1.0 - sig)))
    dbuf[0:CHUNK] = c
    u = bc_ref[0].astype(F32) * pad
    gu = cbw_ref[0:1] * c
    gmap_ref[4:5] += jnp.sum(c, axis=0, keepdims=True)
    gmap_ref[0:1] += jnp.sum(c * u, axis=0, keepdims=True)
    for k in range(1, TAPS):
        shifted = ahead[k] * dbuf[k : k + CHUNK]
        gu = gu + cbw_ref[k : k + 1] * shifted
        gmap_ref[k : k + 1] += jnp.sum(shifted * u, axis=0, keepdims=True)
    gbc_ref[0] = gu * pad
    dbuf[CHUNK:] = dbuf[0:HALO]

    across = gathered.T
    col_sum = across[0:heads]
    kx = across[heads : 2 * heads]
    rint = across[2 * heads : 3 * heads]
    row_sum = jnp.concatenate(row_sums, axis=0)
    k_all = kx * dt
    held_head = exact_dot(jnp.broadcast_to(held, (16, inner)), collect[0])
    held_col = jnp.broadcast_to(held_head[0:1], (CHUNK, 128)).T[heads : 2 * heads]
    diff = row_sum + rint - col_sum - k_all
    grad_a = exact_dot(diff, suf_ref[...]) + jnp.sum(k_all, axis=1, keepdims=True) + held_col
    direct = jnp.where(dt > 0.0, col_sum / jnp.where(dt > 0.0, dt, 1.0), 0.0)
    grad_dt = direct + kx + rate * grad_a
    graw = grad_dt * aux[1:2] * sigmoid(raw_ref[0] + hp_ref[0])
    gstep_ref[0] = graw
    ghead_ref[0] += graw
    ghead_ref[1] += rate * dt * grad_a


def mixer_forward(zx, bc, raw, aux, g, cw, cbw, hp):
    seqs, length, wide = zx.shape
    inner = wide // 2
    heads = inner // HEADDIM
    chunks = length // CHUNK
    token = lambda width: pl.BlockSpec((1, CHUNK, width), lambda s, c: (s, c, 0))
    row = lambda high: pl.BlockSpec((1, high, CHUNK), lambda s, c: (s, 0, c))
    whole = lambda *shape: pl.BlockSpec(shape, lambda s, c: (0,) * len(shape))
    sds = jax.ShapeDtypeStruct
    return pl.pallas_call(
        functools.partial(forward_kernel, heads),
        grid=(seqs, chunks),
        in_specs=[
            token(wide), token(2 * STATE), row(heads), row(AUX), token(inner),
            whole(8, inner), whole(8, 2 * STATE), whole(2, heads, 128),
        ],
        out_specs=[
            token(inner), token(inner), token(inner), token(inner), token(2 * STATE), token(2 * STATE),
            pl.BlockSpec((1, 1, STATE, inner), lambda s, c: (s, c, 0, 0)), row(8),
        ],
        out_shape=[
            sds((seqs, length, inner), BF), sds((seqs, length, inner), BF), sds((seqs, length, inner), BF),
            sds((seqs, length, inner), BF), sds((seqs, length, 2 * STATE), BF), sds((seqs, length, 2 * STATE), BF),
            sds((seqs, chunks, STATE, inner), BF), sds((seqs, 8, length), F32),
        ],
        scratch_shapes=[
            pltpu.VMEM((STATE, inner), F32), pltpu.VMEM((HALO + CHUNK, inner), F32),
            pltpu.VMEM((HALO + CHUNK, 2 * STATE), F32), pltpu.VMEM((CHUNK, inner), BF),
            pltpu.VMEM((CHUNK, inner), F32), pltpu.VMEM((3, 256, inner), BF), pltpu.VMEM((CHUNK, CHUNK), BF),
        ],
        compiler_params=pltpu.CompilerParams(vmem_limit_bytes=40 * 1024 * 1024),
        name="mixer_forward",
    )(zx, bc, raw, aux, g, cw, cbw, hp)


def mixer_backward(zx, bc, raw, aux, g, mixed, cv, pre, cbc, pbc, st, stat, cw, cbw, hp):
    seqs, length, wide = zx.shape
    inner = wide // 2
    heads = inner // HEADDIM
    chunks = length // CHUNK
    last = chunks - 1
    token = lambda width: pl.BlockSpec((1, CHUNK, width), lambda s, c: (s, last - c, 0))
    row = lambda high: pl.BlockSpec((1, high, CHUNK), lambda s, c: (s, 0, last - c))
    whole = lambda *shape: pl.BlockSpec(shape, lambda s, c: (0,) * len(shape))
    sds = jax.ShapeDtypeStruct
    return pl.pallas_call(
        functools.partial(backward_kernel, heads),
        grid=(seqs, chunks),
        in_specs=[
            token(wide), token(2 * STATE), row(heads), row(AUX), token(inner), token(inner), token(inner),
            token(inner), token(2 * STATE), token(2 * STATE),
            pl.BlockSpec((1, 1, STATE, inner), lambda s, c: (s, last - c, 0, 0)), row(8),
            whole(8, inner), whole(8, 2 * STATE), whole(2, heads, 128),
        ],
        out_specs=[
            token(wide), token(2 * STATE), row(heads),
            whole(8, inner), whole(8, 2 * STATE), whole(2, heads, 128),
        ],
        out_shape=[
            sds((seqs, length, wide), BF), sds((seqs, length, 2 * STATE), F32), sds((seqs, heads, length), F32),
            sds((8, inner), F32), sds((8, 2 * STATE), F32), sds((2, heads, 128), F32),
        ],
        scratch_shapes=[
            pltpu.VMEM((STATE, inner), F32), pltpu.VMEM((CHUNK + HALO, inner), F32),
            pltpu.VMEM((CHUNK + HALO, 2 * STATE), F32), pltpu.VMEM((CHUNK, inner), BF),
            pltpu.VMEM((CHUNK, inner), BF), pltpu.VMEM((CHUNK, inner), BF), pltpu.VMEM((CHUNK, inner), BF),
            pltpu.VMEM((CHUNK, inner), F32), pltpu.VMEM((CHUNK, inner), F32),
            pltpu.VMEM((3, 256, inner), BF), pltpu.VMEM((2, inner, 128), BF),
            pltpu.VMEM((CHUNK, CHUNK), BF), pltpu.VMEM((CHUNK, CHUNK), BF),
        ],
        compiler_params=pltpu.CompilerParams(vmem_limit_bytes=40 * 1024 * 1024),
        name="mixer_backward",
    )(zx, bc, raw, aux, g, mixed, cv, pre, cbc, pbc, st, stat, cw, cbw, hp)


def doc_flags(segment, pad_mask):
    seqs, length = segment.shape
    position = lax.broadcasted_iota(jnp.int32, segment.shape, 1)
    rows = [segment.astype(F32), pad_mask.astype(F32)]
    back = []
    for k in range(1, TAPS):
        earlier = jnp.pad(segment, ((0, 0), (k, 0)), constant_values=-1)[:, :length]
        back.append(earlier == segment)
    rows += [b.astype(F32) for b in back]
    blocks = segment.reshape(seqs, length // CHUNK, CHUNK)
    tail = blocks[:, :, CHUNK - 1 :]
    previous = jnp.pad(tail, ((0, 0), (1, 0), (0, 0)), constant_values=-1)[:, :-1]
    rows.append((blocks == previous).reshape(seqs, length).astype(F32))
    rows.append((blocks == tail).reshape(seqs, length).astype(F32))
    rows.append(jnp.zeros_like(rows[0]))
    for k in range(1, TAPS):
        later = jnp.pad(segment, ((0, 0), (0, k)), constant_values=-1)[:, k:]
        rows.append((later == segment).astype(F32))
    rows += [jnp.zeros_like(rows[0])] * (AUX - len(rows))
    return jnp.stack(rows, axis=1)


def gather_tokens(own, n, me):
    if n != 2:
        return lax.all_gather(own, "tensor", axis=1, tiled=True)
    other = lax.ppermute(own, "tensor", [(0, 1), (1, 0)])
    seqs, here, width = own.shape
    full = jnp.zeros((seqs, 2 * here, width), own.dtype)
    full = lax.dynamic_update_slice(full, own, (0, me * here, 0))
    return lax.dynamic_update_slice(full, other, (0, (1 - me) * here, 0))


def scatter_sum(make, size, n, me, dim):
    if n != 2:
        blocks = [make(i * size) for i in range(n)]
        return lax.psum_scatter(jnp.concatenate(blocks, axis=dim), "tensor", scatter_dimension=dim, tiled=True)
    away = lax.ppermute(make((1 - me) * size).astype(BF), "tensor", [(0, 1), (1, 0)])
    return make(me * size) + away.astype(F32)


def swap_sum(value, n):
    if n != 2:
        return lax.psum(value, "tensor")
    return value + lax.ppermute(value, "tensor", [(0, 1), (1, 0)])


def body(
    hidden, pre_gain, zx_weight, bc_weight, step_weight, conv_x_weight, conv_x_bias, conv_bc_weight, conv_bc_bias,
    step_bias, decay_log, skip_gain, norm_gain, out_weight, segment_ids, pad_mask, grad_out,
):
    n = lax.axis_size("tensor")
    me = lax.axis_index("tensor")
    heads = step_weight.shape[1]
    inner = heads * HEADDIM
    inner_all = inner * n
    here = hidden.shape[1]
    width = hidden.shape[2]
    maps_here = 2 * STATE // n

    zx_all = lax.all_gather(zx_weight, "dp", axis=0, tiled=True)
    small_all = lax.all_gather(jnp.concatenate([bc_weight, step_weight], axis=1), "dp", axis=0, tiled=True)
    out_all = lax.all_gather(out_weight.T, "dp", axis=0, tiled=True)
    bc_all, step_all = small_all[:, : 2 * STATE], small_all[:, 2 * STATE :]

    hidden_f = hidden.astype(F32)
    inv_rms = lax.rsqrt(jnp.mean(hidden_f * hidden_f, axis=-1, keepdims=True) + epsilon)
    normed = gather_tokens((hidden_f * inv_rms * pre_gain).astype(BF), n, me)
    cotangent = gather_tokens(grad_out, n, me)

    aux = doc_flags(segment_ids, pad_mask)
    cw = jnp.concatenate(
        [conv_x_weight, conv_x_bias[None], jnp.repeat(skip_gain, HEADDIM)[None], norm_gain[None], jnp.zeros((1, inner), F32)]
    )
    cbw = jnp.concatenate([conv_bc_weight, conv_bc_bias[None], jnp.zeros((3, 2 * STATE), F32)])
    rate = -jnp.exp(decay_log)
    hp = jnp.broadcast_to(jnp.stack([step_bias, rate])[:, :, None], (2, heads, 128))

    zx = jnp.einsum("stp,py->sty", normed, zx_all, preferred_element_type=F32).astype(BF)
    bc = jnp.einsum("stp,py->sty", normed, bc_all, preferred_element_type=F32).astype(BF)
    raw = jnp.einsum("stp,ph->sht", normed, step_all, preferred_element_type=F32)
    g = jnp.einsum("str,rc->stc", cotangent, out_all, preferred_element_type=F32).astype(BF)

    mixed, gated, cv, pre, cbc, pbc, st, stat = mixer_forward(zx, bc, raw, aux, g, cw, cbw, hp)
    stat = swap_sum(stat, n)
    gate_rms = lax.rsqrt(stat[:, 0] / inner_all + epsilon)
    back = jnp.stack([gate_rms, gate_rms**3 * (stat[:, 1] / inner_all)] + [jnp.zeros_like(gate_rms)] * 6, axis=1)

    normed_out = (gated.astype(F32) * gate_rms[..., None] * norm_gain).astype(BF)

    def out_part(start):
        rows = lax.dynamic_slice_in_dim(normed_out, start, here, axis=1)
        return jnp.einsum("stc,rc->str", rows, out_all, preferred_element_type=F32)

    output = (hidden_f + scatter_sum(out_part, here, n, me, 1)).astype(BF)
    out_grad = jnp.einsum("str,stc->rc", cotangent, normed_out, preferred_element_type=F32).astype(BF)
    grad_out_weight = lax.psum_scatter(out_grad, "dp", scatter_dimension=0, tiled=True).astype(F32).T

    gzx, gbc, gstep, gch, gmap, ghead = mixer_backward(
        zx, bc, raw, aux, g, mixed, cv, pre, cbc, pbc, st, back, cw, cbw, hp
    )
    gstep = gstep.astype(BF)
    gbc_own = scatter_sum(
        lambda start: lax.dynamic_slice_in_dim(gbc, start, maps_here, axis=2), maps_here, n, me, 2
    ).astype(BF)
    bc_own = lax.dynamic_slice_in_dim(bc_all, me * maps_here, maps_here, axis=1)

    def in_part(start):
        cut = lambda rows, dim: lax.dynamic_slice_in_dim(rows, start, here, axis=dim)
        return (
            jnp.einsum("sty,py->stp", cut(gzx, 1), zx_all, preferred_element_type=F32)
            + jnp.einsum("sty,py->stp", cut(gbc_own, 1), bc_own, preferred_element_type=F32)
            + jnp.einsum("sht,ph->stp", cut(gstep, 2), step_all, preferred_element_type=F32)
        )

    grad_normed = scatter_sum(in_part, here, n, me, 1)
    zx_grad = jnp.einsum("stp,sty->py", normed, gzx, preferred_element_type=F32).astype(BF)
    small_grad = jnp.concatenate(
        [
            jnp.einsum("stp,sty->py", normed, gbc_own, preferred_element_type=F32),
            jnp.einsum("stp,sht->ph", normed, gstep, preferred_element_type=F32),
        ],
        axis=1,
    ).astype(BF)
    grad_zx_weight = lax.psum_scatter(zx_grad, "dp", scatter_dimension=0, tiled=True).astype(F32)
    small_rows = lax.psum_scatter(small_grad, "dp", scatter_dimension=0, tiled=True).astype(F32)
    grad_bc_weight = lax.all_gather(small_rows[:, :maps_here], "tensor", axis=1, tiled=True)
    grad_step_weight = small_rows[:, maps_here:]

    scaled_in = hidden_f * inv_rms
    grad_pre = jnp.sum(scaled_in * grad_normed, axis=(0, 1))
    gain_grad = grad_normed * pre_gain
    grad_hidden = (
        grad_out.astype(F32)
        + inv_rms * gain_grad
        - hidden_f * inv_rms**3 * jnp.mean(hidden_f * gain_grad, axis=-1, keepdims=True)
    ).astype(BF)

    head_sums = jnp.sum(ghead, axis=-1)
    skip_sums = jnp.sum(gch[5].reshape(heads, HEADDIM), axis=-1)
    flat = jnp.concatenate(
        [gmap[:5].reshape(-1), grad_pre, gch[:5].reshape(-1), gch[6], head_sums.reshape(-1), skip_sums]
    )
    flat = lax.psum(flat, "dp")
    shared_size = 5 * 2 * STATE + width
    shared = swap_sum(flat[:shared_size], n)
    shared_map = shared[: 5 * 2 * STATE].reshape(5, 2 * STATE)
    rest = flat[shared_size:]
    channel = rest[: 6 * inner].reshape(6, inner)
    per_head = rest[6 * inner :].reshape(3, heads)
    return (
        output, grad_hidden, shared[5 * 2 * STATE :], grad_zx_weight, grad_bc_weight, grad_step_weight,
        channel[:4], channel[4], shared_map[:4], shared_map[4], per_head[0], per_head[1], per_head[2],
        channel[5], grad_out_weight,
    )


def solution(mesh):
    placed = (
        P("dp", "tensor", None), P(), P("dp", "tensor"), P("dp", None), P("dp", "tensor"), P(None, "tensor"),
        P("tensor"), P(), P(), P("tensor"), P("tensor"), P("tensor"), P("tensor"), P("tensor", "dp"),
        P("dp", None), P("dp", None), P("dp", "tensor", None),
    )
    return jax.shard_map(
        body,
        mesh=mesh,
        in_specs=placed,
        out_specs=(
            P("dp", "tensor", None), P("dp", "tensor", None), P(), P("dp", "tensor"), P("dp", None), P("dp", "tensor"),
            P(None, "tensor"), P("tensor"), P(), P(), P("tensor"), P("tensor"), P("tensor"), P("tensor"),
            P("tensor", "dp"),
        ),
        check_vma=False,
    )
```

time: 1010 us -> 397 us (0.39); the launches traced: 999 us -> 396 us
  waiting for transfers between devices: 305 us -> 126 us
  matrix products: 204 us -> 53.5 us
  local copies, waits for them, and re-layouts: 175 us -> 35.3 us
  other arithmetic: 127 us -> 13.6 us
  blocking collectives: 159 us -> 95.6 us
  Pallas kernels: 0 us -> 48.5 us
  loops' own time: 12.7 us -> 0 us
    reduce_scatter x6 -> x2, waiting for transfers between devices: 260 us -> 46.8 us  [the longest x1 46.8 us: body(): lax.psum_scatter(zx_grad, 'dp', scatter_dimension=0, tiled=True).astype(F32)]
    dot_general x67 -> x16, matrix products: 203 us -> 53.5 us  [the longest x1 9.33 us: body(): jnp.einsum('stp,py->sty', normed, zx_all, preferred_element_type=F32)]
    psum x4 -> x1, blocking collectives: 108 us -> 58 us  [body(): flat = lax.psum(flat, 'dp')]
    pallas_call x0 -> x2, Pallas kernels: none -> 48.5 us  [the longest x1 30.3 us: mixer_backward(): pl.pallas_call(functools.partial(backward_kernel, heads), grid=(seqs, chu...]
    transpose x5 -> x0, local copies, waits for them, and re-layouts: 39 us -> none  [the longest x3 23.3 us: state_scan(): jnp.moveaxis(pieces, 0, 1)]
    reduce_sum x10 -> x2, other arithmetic: 34.4 us -> 0.71 us  [the longest x1 0.63 us: body(): skip_sums = jnp.sum(gch[5].reshape(heads, HEADDIM), axis=-1)]
    convert_element_type x5 -> x1, local copies, waits for them, and re-layouts: 25 us -> 0.04 us  [scatter_sum(): make((1 - me) * size).astype(BF)]
    squeeze x24 -> x0, local copies, waits for them, and re-layouts: 23.4 us -> none  [state_scan(): lax.scan(jax.checkpoint(advance), start, (to_blocks(values_in), to_blocks...]
  transfers between devices with their start and end apart: 12 -> 12, of which waited for: 7 -> 6; matrix products, arithmetic and copies ran while one was open for 29% -> 18% of each run, Pallas kernels for 0% -> 0%
where the time goes in v1:
time: 397 us; the launch traced here: 396 us
  waiting for transfers between devices  126 us (32%)
  blocking collectives  95.6 us (24%)
  matrix products  53.5 us (13%)
  Pallas kernels  48.5 us (12%)
  local copies, waits for them, and re-layouts  35.3 us (9%)
  between operations  14.3 us (4%)
  other arithmetic  13.6 us (3%)
  starting transfers between devices  9.79 us (2%)
    psum x1, blocking collectives, body(): flat = lax.psum(flat, 'dp')  58 us
    reduce_scatter x1, waiting for transfers between devices, body(): lax.psum_scatter(zx_grad, 'dp', scatter_dimension=0, tiled=True).astype(F32)  46.8 us
    all_gather x1, waiting for transfers between devices, body(): zx_all = lax.all_gather(zx_weight, 'dp', axis=0, tiled=True)  39.9 us
    pallas_call x1, Pallas kernels, mixer_backward(): pl.pallas_call(functools.partial(backward_kernel, heads), grid=(seqs, chu...  30.3 us
    all_gather x1, blocking collectives, body(): lax.all_gather(jnp.concatenate([bc_weight, step_weight], axis=1), 'dp', a...  24.4 us
    unnamed x6, waiting for transfers between devices  20.7 us
    unnamed x98, local copies, waits for them, and re-layouts  19.6 us
    pallas_call x1, Pallas kernels, mixer_forward(): pl.pallas_call(functools.partial(forward_kernel, heads), grid=(seqs, chun...  18.3 us
  transfers between devices with their start and end apart: 12, of which 6 were waited for; matrix products, arithmetic and copies ran while one was open for 18% of the time, Pallas kernels for 0%

profile of v1, /device:TPU:0, one launch (start us, length us, event | category | flops | bytes accessed | tf_op | source)
XLA Modules:
  0.0 396.4 jit_solution(18422340335204453358)
XLA Ops:
  7.2 0.7 all-gather.5.cloned.1.call-update
  8.0 0.7 all-gather.3.cloned.1.call-update
  8.7 3.0 collective-permute-start.1
  11.8 1.6 fusion.9
  14.4 1.3 bitcast_dynamic-update-slice_fusion.3
  16.9 24.4 %all_gather.13 = bf16[1024,272]{1,0:T(8,128)(2,1)S(1)} all-gather(bf16[64,272]{1,0:T(8,128)(2,1)S(1)} %pad_maximum_fusion.1), channel_id=1, replica_groups=mesh['dp'=16,'tensor'=2] {'dp'}, dimensions={0}, use_global_device_ids=true | all-gather | bytes 591872 | tf_op jit(solution)/shard_map/all_gather | solution.py:485
  41.3 1.7 broadcast.104.clone.1
  42.9 2.3 bitcast_dynamic-update-slice_fusion.1
  45.2 12.5 %collective-permute-done = bf16[1,512,1024]{2,1,0:T(8,128)(2,1)} collective-permute-done((bf16[1,512,1024]{2,1,0:T(8,128)(2,1)}, bf16[1,512,1024]{2,1,0:T(8,128)(2,1)}, u32[]{:S(2)}, u32[]{:S(2)}) %collective-permute-start) | collective-permute-done | bytes 1048608 | tf_op jit(solution)/shard_map/ppermute | solution.py:450
  57.7 1.3 bitcast_dynamic-update-slice_fusion.2
  59.0 0.7 convolution_bitcast_fusion.raw_ref
  59.7 0.7 fusion.28.bc_ref
  60.5 2.3 bitcast_dynamic-update-slice_fusion
  62.8 4.7 %convert_bitcast_fusion.1.g_ref = bf16[1,1024,1024]{2,1,0:T(8,128)(2,1)S(1)} fusion(bf16[1024,1024]{1,0:T(8,128)(2,1)} %bitcast_dynamic-update-slice_fusion, bf16[1024,1024]{1,0:T(8,128)(2,1)} %all-gather.5.cloned.1.call-done), kind=kOutput, calls=%fused_computation.31 | convolution fusion | flops 2148532224 | bytes 6291456 | tf_op jit(solution)/shard_map/str,rc->stc/dot_general | solution.py:505
  67.5 39.9 %all-gather.3.cloned.1.call-done = bf16[1024,2048]{1,0:T(8,128)(2,1)} async-done(((bf16[64,2048]{1,0:T(8,128)(2,1)}), bf16[1024,2048]{1,0:T(8,128)(2,1)}) %all-gather.3.cloned.1.call-update) | async-done | bytes 4194320 | tf_op jit(solution)/shard_map/all_gather | solution.py:484
  107.4 9.3 %convert_bitcast_fusion.zx_ref = bf16[1,1024,2048]{2,1,0:T(8,128)(2,1)} fusion(bf16[1024,1024]{1,0:T(8,128)(2,1)} %copy-done.12, bf16[1024,2048]{1,0:T(8,128)(2,1)} %all-gather.3.cloned.1.call-done), kind=kOutput, calls=%fused_computation.3 | convolution fusion | flops 4297064448 | bytes 10485760 | tf_op jit(solution)/shard_map/stp,py->sty/dot_general | solution.py:502
  116.8 18.3 %mixer_forward.1 = (bf16[1,1024,1024]{2,1,0:T(8,128)(2,1)S(1)}, bf16[1,1024,1024]{2,1,0:T(8,128)(2,1)S(1)}, bf16[1,1024,1024]{2,1,0:T(8,128)(2,1)S(1)}, bf16[1,1...) custom-call(bf16[1,1024,2048]{2,1,0:T(8,128)(2,1)} %convert_bitcast_, ...), custom_call_target="tpu_custom_call" | custom-call | tf_op jit(solution)/shard_map/mixer_forward/pallas_call | solution.py:359
  135.2 1.3 copy-done
  136.5 1.4 copy-done.2
  137.9 1.3 copy-done.4
  139.2 1.3 copy-done.6
  140.6 1.3 copy-done.8
  141.9 0.8 copy-done.10
  142.7 1.5 collective-permute-start.2
  144.3 2.4 collective-permute-done.2
  146.7 1.6 copy-done.1
  148.3 1.6 copy-done.3
  149.9 1.6 copy-done.5
  151.5 1.6 copy-done.7
  153.1 1.0 copy-done.11
  154.1 30.3 %mixer_backward.1 = (bf16[1,1024,2048]{2,1,0:T(8,128)(2,1)}, f32[1,1024,256]{2,1,0:T(8,128)S(1)}, f32[1,16,1024]{2,1,0:T(8,128)S(1)}, f32[8,1024]{1,0:T(8,128)S(...) custom-call(bf16[1,1024,2048]{2,1,0:T(8,128)(2,1)} %convert_bitcast_fusion.zx_ref, ...), custom_call_target="tpu_custom_call" | custom-call | tf_op jit(solution)/shard_map/mixer_backward/pallas_call | solution.py:395
  184.4 1.5 collective-permute-start.4
  186.0 1.9 multiply_convert_fusion
  188.2 3.5 collective-permute-done.4
  192.6 1.0 copy.38
  193.7 5.9 %fusion.23 = bf16[1024,1024]{1,0:T(8,128)(2,1)} fusion(bf16[1024,1024]{1,0:T(8,128)(2,1)} %bitcast_dynamic-update-slice_fusion, bf16[1,1024,1024]{2,1,0:T(8,128)(2,1)} %multiply_convert_fusion), kind=kOutput, calls=%fused_computation.32 | convolution fusion | flops 2148532224 | bytes 6291456 | tf_op jit(solution)/shard_map/str,stc->rc/dot_general | solution.py:519
  199.6 8.6 %fusion.2 = bf16[1024,2048]{1,0:T(8,128)(2,1)} fusion(bf16[1024,1024]{1,0:T(8,128)(2,1)S(1)} %copy-done.13, bf16[1,1024,2048]{2,1,0:T(8,128)(2,1)} %get-tuple-element.37), kind=kOutput, calls=%fused_computation.9 | convolution fusion | flops 4297064448 | bytes 10485760 | tf_op jit(solution)/shard_map/stp,sty->py/dot_general | solution.py:540
  208.3 1.1 copy-done.17
  209.5 0.6 reshape.266
  210.2 0.6 reshape.268
  210.8 0.6 slice_reduce_fusion
  211.5 0.6 reduce_sum.49
  212.1 4.0 %fusion.27 = bf16[1,512,1024]{2,1,0:T(8,128)(2,1)} fusion(bf16[1024,1024]{1,0:T(8,128)(2,1)} %all-gather.5.cloned.1.call-done, bf16[1,1024,1024]{2,1,0:T(8,128)(2,1)S(1)} %copy-done.21, s32[]{:T(128)S(6)} %select_n.9), kind=kOutput, calls=%fused_computation.35 | convolution fusion | flops 1074266112 | bytes 4194308 | tf_op jit(solution)/shard_map/stc,rc->str/dot_general | solution.py:516
  216.1 1.5 collective-permute-start.3
  217.6 4.0 fusion.17
  222.1 1.5 fusion.26
  224.6 3.7 fusion.19
  228.8 19.3 %reduce-scatter.10.cloned.1.call-done = bf16[64,144]{1,0:T(8,128)(2,1)} async-done(((bf16[1024,144]{1,0:T(8,128)(2,1)}), bf16[64,144]{1,0:T(8,128)(2,1)}) %reduce-scatter.10.cloned.1.call-update) | async-done | bytes 18448
  248.0 0.7 slice.165
  248.8 0.7 copy.42
  249.4 0.7 slice.164
  250.2 13.2 %all_gather.15 = f32[64,256]{0,1:T(8,128)S(1)} all-gather(f32[64,128]{0,1:T(8,128)S(1)} %copy.41), channel_id=1, replica_groups=mesh['dp'=16,'tensor'=2] {'tensor'}, dimensions={1}, use_global_device_ids=true | all-gather | bytes 98304 | tf_op jit(solution)/shard_map/all_gather | solution.py:550
  263.4 0.7 copy.37
  264.2 4.8 %fusion.10 = bf16[1,512,1024]{2,1,0:T(8,128)(2,1)} fusion(bf16[1,512,1024]{2,1,0:T(8,128)(2,1)S(1)} %copy-done.15, bf16[1,512,1024]{2,1,0:T(8,128)(2,1)} %collective-permute-done.3, bf16[1024,1024]{1,0:T(8,128)(2,1)} %all-gather.5.cloned.1.call-done, bf16[1,1024,1024]{2,1,0:T(8,128)(2,1)} %multiply_convert_fusion, s32[]{:T(128)S(6)} %select_n.8), kind=kOutput, calls=%fused_computation.15 | convolution fusion | flops 1076363264 | bytes 6291460 | tf_op jit(solution)/shard_map/stc,rc->str/dot_general | solution.py:516
  269.0 3.8 fusion.8
  272.9 58.0 %psum.7 = f32[8496]{0:T(1024)S(1)} all-reduce(f32[8496]{0:T(1024)S(1)} %concatenate.19), channel_id=1, replica_groups=mesh['dp'=16,'tensor'=2] {'dp'}, use_global_device_ids=true, to_apply=%region_5.6 | all-reduce | flops 8496 | bytes 67968 | tf_op jit(solution)/shard_map/psum | solution.py:567
  330.9 1.5 collective-permute-start.6
  332.4 0.6 fusion.72
  333.0 3.7 fusion.13
  337.2 0.6 slice.149
  339.0 0.6 slice.152
  339.6 1.6 convert_bitcast_fusion.2
  341.3 46.8 %reduce-scatter.6.cloned.1.call-done = bf16[64,2048]{1,0:T(8,128)(2,1)} async-done(((bf16[1024,2048]{1,0:T(8,128)(2,1)}), bf16[64,2048]{1,0:T(8,128)(2,1)}) %reduce-scatter.6.cloned.1.call-update) | async-done | bytes 262160 | tf_op jit(solution)/shard_map/reduce_scatter | solution.py:548
  388.1 1.8 convert_element_type.124
  (146 shorter events, 7.9 us)
Async XLA Ops:
  7.2 7.0 %copy-start.24 = (f32[1024]{0:T(1024)S(1)}, f32[1024]{0:T(1024)}, u32[]{:S(2)}) copy-start(f32[1024]{0:T(1024)} %param.18) | copy-start | bytes 12292
  7.2 55.6 %all-gather.5.cloned.1.call-start = ((), (), s32[]{:S(2)}) async-start(), calls=%async_computation.4 | async-start | bytes 2228224 | tf_op jit(solution)/shard_map/all_gather | solution.py:486
  7.9 99.5 %all-gather.3.cloned.1.call-start = ((), (), s32[]{:S(2)}) async-start(), calls=%async_computation.3 | async-start | bytes 4456448 | tf_op jit(solution)/shard_map/all_gather | solution.py:484
  8.7 239.4 %reduce-scatter.10.cloned.1.call-start = ((), (), s32[]{:S(2)}) async-start(), calls=%async_computation.7 | async-start | bytes 557056
  8.7 51.7 %collective-permute-start.1 = (bf16[1,512,1024]{2,1,0:T(8,128)(2,1)}, bf16[1,512,1024]{2,1,0:T(8,128)(2,1)}, u32[]{:S(2)}, u32[]{:S(2)}) collective-permute-start(bf16[1,512,1024]{2,1,0:T(8,128)(2,1)} %param.33), channel_id=1, source_target_pairs={{0,1},{1,0},{2,3},{3,2},{4,5},{5,4},{6,7},{7,6},{8,9},{9,8},{10,11... | collective-permute-start | bytes 3145736 | tf_op jit(solution)/shard_map/ppermute | solution.py:450
  11.8 2.5 copy-start.14
  13.9 1.7 copy-start.26
  14.2 1.5 copy-start.25
  14.2 1.7 copy-start.37
  14.2 2.0 copy-start.45
  14.3 2.0 copy-start.41
  14.3 2.1 copy-start.34
  14.3 2.3 copy-start.31
  14.3 2.3 copy-start.32
  14.3 2.3 copy-start.35
  14.3 2.5 copy-start.42
  14.3 2.5 copy-start.28
  14.3 2.5 copy-start.36
  14.4 2.5 copy-start.39
  15.7 42.0 %collective-permute-start = (bf16[1,512,1024]{2,1,0:T(8,128)(2,1)}, bf16[1,512,1024]{2,1,0:T(8,128)(2,1)}, u32[]{:S(2)}, u32[]{:S(2)}) collective-permute-start(bf16[1,512,1024]{2,1,0:T(8,128)(2,1)} %get-tuple-element.78), channel_id=1, source_target_pairs={{0,1},{1,0},{2,3},{3,2},{4,5},{5,4},{6,7},{7,6},{8,9},{9,8},{10,11... | collective-permute-start | bytes 3145736 | tf_op jit(solution)/shard_map/ppermute | solution.py:450
  41.3 18.4 %copy-start.16 = (bf16[1024,272]{1,0:T(8,128)(2,1)}, bf16[1024,272]{1,0:T(8,128)(2,1)S(1)}, u32[]{:S(2)}) copy-start(bf16[1024,272]{1,0:T(8,128)(2,1)S(1)} %all_gather.13) | copy-start | bytes 1671172
  59.0 1.4 copy-start.12
  135.1 1.3 copy-start
  136.5 1.4 copy-start.2
  137.9 1.3 copy-start.4
  139.2 1.4 copy-start.6
  140.6 1.3 copy-start.8
  141.9 0.8 copy-start.10
  142.7 3.9 collective-permute-start.2
  146.7 1.6 copy-start.1
  148.3 1.6 copy-start.3
  149.9 1.6 copy-start.5
  151.5 1.6 copy-start.7
  153.1 1.0 copy-start.11
  154.1 31.8 %copy-start.9 = (bf16[1,1024,1024]{2,1,0:T(8,128)(2,1)S(1)}, bf16[1,1024,1024]{2,1,0:T(8,128)(2,1)}, u32[]{:S(2)}) copy-start(bf16[1,1024,1024]{2,1,0:T(8,128)(2,1)} %copy-done.8) | copy-start | bytes 6291460
  184.4 7.4 %collective-permute-start.4 = (bf16[1,1024,128]{2,1,0:T(8,128)(2,1)S(1)}, bf16[1,1024,128]{2,1,0:T(8,128)(2,1)S(1)}, u32[]{:S(2)}, u32[]{:S(2)}) collective-permute-start(bf16[1,1024,128]{2,1,0:T(8,128)(2,1)S(1)} %dynamic-slice_convert_fusion), channel_id=1, source_target_pairs={{0,1},{1,0},{2,3},{3,2},{4,5},{5,4},{6,7},{7,6},{8,9},{9,8},{10,11... | collective-permute-start | bytes 786440 | tf_op jit(solution)/shard_map/ppermute | solution.py:461
  186.0 1.9 copy-start.13
  191.9 0.7 copy-start.22
  193.6 146.0 %reduce-scatter.8.cloned.1.call-start = ((), (), s32[]{:S(2)}) async-start(), calls=%async_computation.6 | async-start | bytes 2228224 | tf_op jit(solution)/shard_map/reduce_scatter | solution.py:520
  199.6 188.5 %reduce-scatter.6.cloned.1.call-start = ((), (), s32[]{:S(2)}) async-start(), calls=%async_computation.5 | async-start | bytes 4456448 | tf_op jit(solution)/shard_map/reduce_scatter | solution.py:548
  208.3 1.1 copy-start.17
  208.3 3.8 copy-start.21
  209.5 12.1 %copy-start.19 = (bf16[1024,256]{1,0:T(8,128)(2,1)}, bf16[1024,256]{1,0:T(8,128)(2,1)S(1)}, u32[]{:S(2)}) copy-start(bf16[1024,256]{1,0:T(8,128)(2,1)S(1)} %slice.158) | copy-start | bytes 1572868
  212.1 5.5 %copy-start.43 = (bf16[1024,2048]{1,0:T(8,128)(2,1)S(1)}, bf16[1024,2048]{1,0:T(8,128)(2,1)}, u32[]{:S(2)}) copy-start(bf16[1024,2048]{1,0:T(8,128)(2,1)} %all-gather.3.cloned.1.call-done) | copy-start | bytes 12582916
  216.1 5.5 %copy-start.23 = (bf16[1,1024,128]{2,1,0:T(8,128)(2,1)S(1)}, bf16[1,1024,128]{2,1,0:T(8,128)(2,1)}, u32[]{:S(2)}) copy-start(bf16[1,1024,128]{2,1,0:T(8,128)(2,1)} %copy-done.22) | copy-start | bytes 786436
  216.1 48.0 %collective-permute-start.3 = (bf16[1,512,1024]{2,1,0:T(8,128)(2,1)}, bf16[1,512,1024]{2,1,0:T(8,128)(2,1)}, u32[]{:S(2)}, u32[]{:S(2)}) collective-permute-start(bf16[1,512,1024]{2,1,0:T(8,128)(2,1)} %fusion.27), channel_id=1, source_target_pairs={{0,1},{1,0},{2,3},{3,2},{4,5},{5,4},{6,7},{7,6},{8,9},{9,8},{10,11... | collective-permute-start | bytes 3145736 | tf_op jit(solution)/shard_map/ppermute | solution.py:461
  222.0 2.6 copy-start.44
  223.6 4.8 %copy-start.20 = (bf16[1024,256]{1,0:T(8,128)(2,1)S(1)}, bf16[1024,256]{1,0:T(8,128)(2,1)}, u32[]{:S(2)}) copy-start(bf16[1024,256]{1,0:T(8,128)(2,1)} %copy-done.19) | copy-start | bytes 1572868
  223.6 45.4 %collective-permute-start.5 = (bf16[1,512,1024]{2,1,0:T(8,128)(2,1)}, bf16[1,512,1024]{2,1,0:T(8,128)(2,1)}, u32[]{:S(2)}, u32[]{:S(2)}) collective-permute-start(bf16[1,512,1024]{2,1,0:T(8,128)(2,1)} %fusion.26), channel_id=1, source_target_pairs={{0,1},{1,0},{2,3},{3,2},{4,5},{5,4},{6,7},{7,6},{8,9},{9,8},{10,11... | collective-permute-start | bytes 3145736 | tf_op jit(solution)/shard_map/ppermute | solution.py:461
  228.3 35.8 %copy-start.15 = (bf16[1,512,1024]{2,1,0:T(8,128)(2,1)S(1)}, bf16[1,512,1024]{2,1,0:T(8,128)(2,1)}, u32[]{:S(2)}) copy-start(bf16[1,512,1024]{2,1,0:T(8,128)(2,1)} %param.17) | copy-start | bytes 3145732
  264.2 4.8 %copy-start.18 = (f32[512,1024]{1,0:T(8,128)S(1)}, f32[512,1024]{1,0:T(8,128)}, u32[]{:S(2)}) copy-start(f32[512,1024]{1,0:T(8,128)} %fusion.19) | copy-start | bytes 6291460
  264.2 4.8 %copy-start.27 = (f32[512]{0:T(512)S(1)}, f32[512]{0:T(512)}, u32[]{:S(2)}) copy-start(f32[512]{0:T(512)} %copy-done.26) | copy-start | bytes 6148
  269.0 3.8 copy-start.29
  269.0 3.8 copy-start.30
  269.0 3.8 copy-start.38
  269.0 3.8 copy-start.40
  269.0 64.0 %copy-start.33 = (f32[512]{0:T(512)S(1)}, f32[512]{0:T(512)}, u32[]{:S(2)}) copy-start(f32[512]{0:T(512)} %get-tuple-element.96) | copy-start | bytes 6148
  330.9 7.0 %collective-permute-start.6 = (f32[2304]{0:T(1024)S(1)}, f32[2304]{0:T(1024)S(1)}, u32[]{:S(2)}, u32[]{:S(2)}) collective-permute-start(f32[2304]{0:T(1024)S(1)} %slice.162), channel_id=1, source_target_pairs={{0,1},{1,0},{2,3},{3,2},{4,5},{5,4},{6,7},{7,6},{8,9},{9,8},{10,11... | collective-permute-start | bytes 27656 | tf_op jit(solution)/shard_map/ppermute | solution.py:468
Sparse Core Ops, SparseCore 0:
  10.2 45.5 all-gather.4
  57.9 49.4 all-gather.2
  193.7 54.2 reduce-scatter.9
  252.1 60.7 reduce-scatter.7
  316.6 71.4 reduce-scatter.5

commit v2 on v1

v2 whole, which is shorter than its diff:
```python
import functools
import jax
import jax.numpy as jnp
from jax import lax
from jax.experimental import pallas as pl
from jax.experimental.pallas import tpu as pltpu
from jax.sharding import PartitionSpec as P

HEADDIM = 64
STATE = 128
CHUNK = 128
TAPS = 4
HALO = 8
AUX = 16
LOG2E = 1.4426950408889634
FAR = -1e30
BLOCK = 256
VMEM_LIMIT = 44 * 1024 * 1024
epsilon = 1e-05
BF = jnp.bfloat16
F32 = jnp.float32


def sigmoid(v):
    return 0.5 * jnp.tanh(0.5 * v) + 0.5


def split3(v):
    a = v.astype(BF)
    r = v - a.astype(F32)
    b = r.astype(BF)
    c = (r - b.astype(F32)).astype(BF)
    return a, b, c


def dot_nn(a, b):
    return lax.dot_general(a, b, (((1,), (0,)), ((), ())), preferred_element_type=F32)


def dot_nt(a, b):
    return lax.dot_general(a, b, (((1,), (1,)), ((), ())), preferred_element_type=F32)


def exact_dot(v, ones):
    rows = v.shape[0]
    out = dot_nn(jnp.concatenate(split3(v), axis=0), ones)
    return out[:rows] + out[rows : 2 * rows] + out[2 * rows :]


def iota2(shape, dim):
    return lax.broadcasted_iota(jnp.int32, shape, dim)


def pieces(raw, bias, rate, aux, tri):
    pad = aux[1:2]
    pre = raw + bias
    soft = jnp.maximum(pre, 0.0) + jnp.log1p(jnp.exp(-jnp.abs(pre)))
    dt = soft * pad
    cum = exact_dot(dt * rate, tri) * LOG2E
    carried = jnp.exp2(cum) * aux[5:6]
    toward = jnp.exp2(cum[:, CHUNK - 1 : CHUNK] - cum) * aux[6:7]
    return dt, cum, carried, toward


def expander(heads, inner, place):
    row = lax.rem(iota2((256, inner), 0), 128)
    head = lax.div(iota2((256, inner), 1), HEADDIM)
    return jnp.where(row == head + place, 1.0, 0.0).astype(BF)


def collector(inner, place):
    head = lax.div(iota2((inner, 128), 0), HEADDIM)
    lane = iota2((inner, 128), 1)
    return jnp.where(lane == head + place, 1.0, 0.0).astype(BF)


def hi_lo(cols):
    hi = cols.astype(BF)
    return jnp.concatenate([hi, (cols - hi.astype(F32)).astype(BF)], axis=1)


def compact(rows_list):
    used = sum(r.shape[0] for r in rows_list)
    if used < 128:
        rows_list = list(rows_list) + [jnp.zeros((128 - used, CHUNK), F32)]
    return jnp.concatenate(rows_list, axis=0).T


def split_pair(first, second, low):
    gate = jnp.where(low, first, pltpu.roll(second, HEADDIM, 1))
    value = jnp.where(low, pltpu.roll(first, HEADDIM, 1), second)
    return gate, value


def forward_kernel(
    heads, tok_ref, w_ref, aux_ref, cw_ref, cbw_ref, hp_ref,
    pz_ref, raw_ref, mixed_ref, gated_ref, cv_ref, pre_ref, cbc_ref, pbc_ref, st_ref, stat_ref,
    state, ubuf, bbuf, vd, yint, expand, tri_ref,
):
    inner = heads * HEADDIM
    pairs = heads // 2
    wide = 2 * inner
    first = (pl.program_id(0) == 0) & (pl.program_id(1) == 0)

    @pl.when(first)
    def _():
        for i, place in enumerate((AUX + heads, AUX + 2 * heads, AUX + 3 * heads)):
            expand[i] = expander(heads, inner, place)
        tri_ref[...] = jnp.where(iota2((CHUNK, CHUNK), 0) <= iota2((CHUNK, CHUNK), 1), 1.0, 0.0).astype(BF)

    @pl.when(pl.program_id(1) == 0)
    def _():
        state[...] = jnp.zeros_like(state)
        ubuf[0:HALO] = jnp.zeros((HALO, inner), F32)
        bbuf[0:HALO] = jnp.zeros((HALO, 2 * STATE), F32)

    tok = tok_ref[0]
    side = dot_nn(tok, w_ref[:, wide:])
    raw_ref[0] = side[:, 2 * STATE :].T[0:heads]
    pz_ref[0, :, wide:] = side[:, : 2 * STATE].astype(BF)
    for p in range(pairs):
        pz_ref[0, :, 256 * p : 256 * p + 256] = dot_nn(tok, w_ref[:, 256 * p : 256 * p + 256]).astype(BF)

    def chunk_step(step, carry):
        here = pl.ds(pl.multiple_of(step * CHUNK, CHUNK), CHUNK)
        aux = aux_ref[0, :, here]
        raw = raw_ref[0, :, here]
        bc = pz_ref[0, here, wide:]
        dt, cum, carried, toward = pieces(raw, hp_ref[0], hp_ref[1], aux, tri_ref[...])
        cols = compact([aux, cum, dt, carried, toward])
        both = hi_lo(cols)
        dtx = dot_nn(both, expand[0])
        carx = dot_nn(both, expand[1])
        towx = dot_nn(both, expand[2])
        pad = cols[:, 1:2]
        same = [None] + [cols[:, 1 + k : 2 + k] for k in range(1, TAPS)]
        low = iota2((CHUNK, 128), 1) < HEADDIM

        bbuf[HALO:] = bc.astype(F32) * pad
        maps = cbw_ref[TAPS : TAPS + 1] + cbw_ref[0:1] * bbuf[HALO:]
        for k in range(1, TAPS):
            maps = maps + cbw_ref[k : k + 1] * (same[k] * bbuf[HALO - k : HALO - k + CHUNK])
        pbc_ref[0, here] = maps.astype(BF)
        maps = (maps * sigmoid(maps)).astype(BF)
        cbc_ref[0, here] = maps
        bbuf[0:HALO] = bbuf[CHUNK : CHUNK + HALO]
        keys, queries = maps[:, :STATE], maps[:, STATE:]
        scores = dot_nt(queries, keys)
        keys_t = keys.astype(F32).T.astype(BF)

        for p in range(pairs):
            s = slice(128 * p, 128 * p + 128)
            x0 = pz_ref[0, here, 256 * p : 256 * p + 128].astype(F32)
            x1 = pz_ref[0, here, 256 * p + 128 : 256 * p + 256].astype(F32)
            value = jnp.where(low, pltpu.roll(x0, HEADDIM, 1), x1)
            ubuf[HALO:, s] = value * pad
            pre = cw_ref[TAPS : TAPS + 1, s] + cw_ref[0:1, s] * ubuf[HALO:, s]
            for k in range(1, TAPS):
                pre = pre + cw_ref[k : k + 1, s] * (same[k] * ubuf[HALO - k : HALO - k + CHUNK, s])
            pre_ref[0, here, s] = pre.astype(BF)
            cv = (pre * sigmoid(pre)).astype(BF)
            cv_ref[0, here, s] = cv
            vd[:, s] = (cv.astype(F32) * dtx[:, s]).astype(BF)
        ubuf[0:HALO] = ubuf[CHUNK : CHUNK + HALO]

        old = state[...]
        old_b = old.astype(BF)
        st_ref[0, step] = old_b
        yint[...] = dot_nn(queries, old_b) * carx
        state[...] = carx[CHUNK - 1 : CHUNK] * old + dot_nn(keys_t, (vd[...].astype(F32) * towx).astype(BF))

        inside = (iota2((CHUNK, CHUNK), 0) >= iota2((CHUNK, CHUNK), 1)) & (cols[:, 0:1] == aux[0:1])
        fence = jnp.where(inside, 0.0, FAR)
        squares = jnp.zeros((CHUNK, 128), F32)
        for p in range(pairs):
            s = slice(128 * p, 128 * p + 128)
            mix = []
            for h in (2 * p, 2 * p + 1):
                decay = jnp.exp2(cols[:, AUX + h : AUX + h + 1] - cum[h : h + 1] + fence)
                mix.append((scores * decay).astype(BF))
            v = vd[:, s]
            zero = jnp.zeros_like(v)
            stacked = jnp.concatenate([jnp.where(low, v, zero), jnp.where(low, zero, v)], axis=0)
            y = dot_nn(jnp.concatenate(mix, axis=1), stacked)
            mixed = y + yint[:, s] + cw_ref[5:6, s] * cv_ref[0, here, s].astype(F32)
            x0 = pz_ref[0, here, 256 * p : 256 * p + 128].astype(F32)
            x1 = pz_ref[0, here, 256 * p + 128 : 256 * p + 256].astype(F32)
            gate = jnp.where(low, x0, pltpu.roll(x1, HEADDIM, 1))
            gated = mixed * (gate * sigmoid(gate))
            mixed_ref[0, here, s] = mixed.astype(BF)
            gated_ref[0, here, s] = (gated * cw_ref[6:7, s]).astype(BF)
            squares = squares + gated * gated
        lane = iota2((CHUNK, 128), 1)
        sums = jnp.where(lane == 0, jnp.sum(squares, axis=1, keepdims=True), 0.0)
        stat_ref[0, :, here] = sums.T[0:8]
        return carry

    lax.fori_loop(0, BLOCK // CHUNK, chunk_step, 0)


def backward_kernel(
    heads, pz_ref, raw_ref, aux_ref, cot_ref, mixed_ref, cv_ref, pre_ref, cbc_ref, pbc_ref,
    st_ref, stat_ref, cw_ref, cbw_ref, hp_ref, out_ref, w_ref, tok_ref,
    ge_ref, dg_ref, gch_ref, gmap_ref, ghead_ref, gpre_ref,
    g_s, dstate, cbuf, dbuf, vd, gm_s, gmc_s, ggate_s, cs_s, bs_s, expand, collect, tri_ref, suf_ref,
):
    inner = heads * HEADDIM
    pairs = heads // 2
    wide = 2 * inner
    first = (pl.program_id(0) == 0) & (pl.program_id(1) == 0)

    @pl.when(first)
    def _():
        for i, place in enumerate((AUX + heads, AUX + 2 * heads, AUX + 3 * heads)):
            expand[i] = expander(heads, inner, place)
        collect[0] = collector(inner, heads)
        collect[1] = collector(inner, 2 * heads)
        r, c = iota2((CHUNK, CHUNK), 0), iota2((CHUNK, CHUNK), 1)
        tri_ref[...] = jnp.where(r <= c, 1.0, 0.0).astype(BF)
        suf_ref[...] = jnp.where(r >= c, 1.0, 0.0).astype(BF)
        gch_ref[...] = jnp.zeros_like(gch_ref)
        gmap_ref[...] = jnp.zeros_like(gmap_ref)
        ghead_ref[...] = jnp.zeros_like(ghead_ref)
        gpre_ref[...] = jnp.zeros_like(gpre_ref)

    @pl.when(pl.program_id(1) == 0)
    def _():
        dstate[...] = jnp.zeros_like(dstate)
        cbuf[CHUNK:] = jnp.zeros((HALO, inner), F32)
        dbuf[CHUNK:] = jnp.zeros((HALO, 2 * STATE), F32)

    g_s[...] = dot_nn(cot_ref[0], out_ref[...])

    def chunk_step(step, carry):
        here = pl.ds(pl.multiple_of(BLOCK - CHUNK - step * CHUNK, CHUNK), CHUNK)
        aux = aux_ref[0, :, here]
        rate = hp_ref[1]
        dt, cum, carried, toward = pieces(raw_ref[0, :, here], hp_ref[0], rate, aux, tri_ref[...])
        cols = compact([aux, cum, dt, carried, toward, stat_ref[0, :, here]])
        both = hi_lo(cols)
        dtx = dot_nn(both, expand[0])
        carx = dot_nn(both, expand[1])
        towx = dot_nn(both, expand[2])
        pad = cols[:, 1:2]
        ahead = [None] + [cols[:, 7 + k : 8 + k] for k in range(1, TAPS)]
        base = AUX + 4 * heads
        rms, pull = cols[:, base : base + 1], cols[:, base + 1 : base + 2]
        low = iota2((CHUNK, 128), 1) < HEADDIM
        maps = cbc_ref[0, here]
        keys, queries = maps[:, :STATE], maps[:, STATE:]
        queries_t = queries.astype(F32).T.astype(BF)
        scores_t = dot_nt(keys, queries)

        for p in range(pairs):
            s = slice(128 * p, 128 * p + 128)
            x0 = pz_ref[0, here, 256 * p : 256 * p + 128].astype(F32)
            x1 = pz_ref[0, here, 256 * p + 128 : 256 * p + 256].astype(F32)
            gate = jnp.where(low, x0, pltpu.roll(x1, HEADDIM, 1))
            sig = sigmoid(gate)
            act = gate * sig
            mixed = mixed_ref[0, here, s].astype(F32)
            gated = mixed * act
            g = g_s[here, s]
            grad_gated = rms * (g * cw_ref[6:7, s]) - gated * pull
            gm = grad_gated * act
            ggate_s[:, s] = (grad_gated * mixed * (sig * (1.0 + gate * (1.0 - sig)))).astype(BF)
            gm_s[:, s] = gm.astype(BF)
            gmc_s[:, s] = (gm * carx[:, s]).astype(BF)
            cv = cv_ref[0, here, s].astype(F32)
            vd[:, s] = (cv * dtx[:, s]).astype(BF)
            gch_ref[5:6, s] += jnp.sum(gm * cv, axis=0, keepdims=True)
            gch_ref[6:7, s] += jnp.sum(gated * rms * g, axis=0, keepdims=True)

        ds = dstate[...]
        ds_b = ds.astype(BF)
        st = st_ref[0, BLOCK // CHUNK - 1 - step]
        gmc = gmc_s[...]
        cs = dot_nn(queries, st)
        bs = dot_nn(keys, ds_b) * towx
        bs_s[...] = bs
        reach = dot_nn((gmc.astype(F32) * cs).astype(BF), collect[1])
        reach = reach + dot_nn((bs * cv_ref[0, here].astype(F32)).astype(BF), collect[0])
        grad_q = dot_nt(gmc, st)
        grad_k = dot_nt((vd[...].astype(F32) * towx).astype(BF), ds_b)
        keep = carx[CHUNK - 1 : CHUNK]
        held = jnp.sum(st.astype(F32) * ds, axis=0, keepdims=True) * keep
        dstate[...] = keep * ds + dot_nn(queries_t, gmc)

        inside = (iota2((CHUNK, CHUNK), 0) <= iota2((CHUNK, CHUNK), 1)) & (cols[:, 0:1] == aux[0:1])
        fence = jnp.where(inside, 0.0, FAR)
        grad_scores_t = jnp.zeros((CHUNK, CHUNK), F32)
        lane = iota2((CHUNK, 128), 1)
        gathered = reach
        row_sums = []
        for p in range(pairs):
            s = slice(128 * p, 128 * p + 128)
            gm_b = gm_s[:, s]
            zero = jnp.zeros_like(gm_b)
            gm_two = jnp.concatenate([jnp.where(low, gm_b, zero), jnp.where(low, zero, gm_b)], axis=0)
            near = dot_nt(vd[:, s], gm_two)
            mix = []
            for j in range(2):
                h = 2 * p + j
                decay = jnp.exp2(cum[h : h + 1] - cols[:, AUX + h : AUX + h + 1] + fence)
                mix.append((scores_t * decay).astype(BF))
                weighed = decay * near[:, CHUNK * j : CHUNK * j + CHUNK]
                grad_scores_t = grad_scores_t + weighed
                pairs_g = weighed * scores_t
                row_sums.append(jnp.sum(pairs_g, axis=0, keepdims=True))
                gathered = jnp.where(lane == h, jnp.sum(pairs_g, axis=1, keepdims=True), gathered)
            z = dot_nn(jnp.concatenate(mix, axis=1), gm_two)
            gm = gm_b.astype(F32)
            grad_v = cw_ref[5:6, s] * gm + dtx[:, s] * (z + bs_s[:, s])
            x0 = pz_ref[0, here, 256 * p : 256 * p + 128].astype(F32)
            x1 = pz_ref[0, here, 256 * p + 128 : 256 * p + 256].astype(F32)
            u = jnp.where(low, pltpu.roll(x0, HEADDIM, 1), x1) * pad
            pre = pre_ref[0, here, s].astype(F32)
            sig = sigmoid(pre)
            c = grad_v * (sig * (1.0 + pre * (1.0 - sig)))
            cbuf[0:CHUNK, s] = c
            gu = cw_ref[0:1, s] * c
            gch_ref[4:5, s] += jnp.sum(c, axis=0, keepdims=True)
            gch_ref[0:1, s] += jnp.sum(c * u, axis=0, keepdims=True)
            for k in range(1, TAPS):
                shifted = ahead[k] * cbuf[k : k + CHUNK, s]
                gu = gu + cw_ref[k : k + 1, s] * shifted
                gch_ref[k : k + 1, s] += jnp.sum(shifted * u, axis=0, keepdims=True)
            gu = gu * pad
            ggate = ggate_s[:, s].astype(F32)
            ge_ref[0, here, 256 * p : 256 * p + 128] = jnp.where(low, ggate, pltpu.roll(gu, HEADDIM, 1)).astype(BF)
            ge_ref[0, here, 256 * p + 128 : 256 * p + 256] = jnp.where(low, pltpu.roll(ggate, HEADDIM, 1), gu).astype(BF)
        cbuf[CHUNK:] = cbuf[0:HALO]

        gst = grad_scores_t.astype(BF)
        grad_k = grad_k + dot_nn(gst, queries)
        grad_q = grad_q + dot_nn(grad_scores_t.T.astype(BF), keys)
        pbc = pbc_ref[0, here].astype(F32)
        sig = sigmoid(pbc)
        c = jnp.concatenate([grad_k, grad_q], axis=1) * (sig * (1.0 + pbc * (1.0 - sig)))
        dbuf[0:CHUNK] = c
        u = pz_ref[0, here, wide:].astype(F32) * pad
        gu = cbw_ref[0:1] * c
        gmap_ref[4:5] += jnp.sum(c, axis=0, keepdims=True)
        gmap_ref[0:1] += jnp.sum(c * u, axis=0, keepdims=True)
        for k in range(1, TAPS):
            shifted = ahead[k] * dbuf[k : k + CHUNK]
            gu = gu + cbw_ref[k : k + 1] * shifted
            gmap_ref[k : k + 1] += jnp.sum(shifted * u, axis=0, keepdims=True)
        ge_ref[0, here, wide : wide + 2 * STATE] = (gu * pad).astype(BF)
        dbuf[CHUNK:] = dbuf[0:HALO]

        across = gathered.T
        col_sum = across[0:heads]
        kx = across[heads : 2 * heads]
        rint = across[2 * heads : 3 * heads]
        row_sum = jnp.concatenate(row_sums, axis=0)
        k_all = kx * dt
        held_head = exact_dot(jnp.broadcast_to(held, (16, inner)), collect[0])
        held_col = jnp.broadcast_to(held_head[0:1], (CHUNK, 128)).T[heads : 2 * heads]
        diff = row_sum + rint - col_sum - k_all
        grad_a = exact_dot(diff, suf_ref[...]) + jnp.sum(k_all, axis=1, keepdims=True) + held_col
        direct = jnp.where(dt > 0.0, col_sum / jnp.where(dt > 0.0, dt, 1.0), 0.0)
        grad_dt = direct + kx + rate * grad_a
        graw = grad_dt * aux[1:2] * sigmoid(raw_ref[0, :, here] + hp_ref[0])
        ge_ref[0, here, wide + 2 * STATE :] = compact([graw]).astype(BF)
        ghead_ref[0] += graw
        ghead_ref[1] += rate * dt * grad_a
        return carry

    lax.fori_loop(0, BLOCK // CHUNK, chunk_step, 0)
    dg = dot_nt(ge_ref[0], w_ref[...])
    dg_ref[0] = dg.astype(BF)
    gpre_ref[0:1] += jnp.sum(dg * tok_ref[0].astype(F32), axis=0, keepdims=True)


def whole_once(*shape):
    return pl.BlockSpec(shape, lambda s, c: (0,) * len(shape), pipeline_mode=pl.Buffered(1))


def mixer_forward(tok, weights, aux, cw, cbw, hp):
    seqs, length, width = tok.shape
    heads, inner = hp.shape[1], cw.shape[1]
    wide = 2 * inner + 2 * STATE
    chunks = length // CHUNK
    token = lambda size: pl.BlockSpec((1, BLOCK, size), lambda s, c: (s, c, 0))
    row = lambda high: pl.BlockSpec((1, high, BLOCK), lambda s, c: (s, 0, c))
    sds = jax.ShapeDtypeStruct
    return pl.pallas_call(
        functools.partial(forward_kernel, heads),
        grid=(seqs, length // BLOCK),
        in_specs=[
            token(width), whole_once(*weights.shape), row(AUX),
            whole_once(8, inner), whole_once(8, 2 * STATE), whole_once(2, heads, 128),
        ],
        out_specs=[
            token(wide), row(heads), token(inner), token(inner), token(inner), token(inner), token(2 * STATE),
            token(2 * STATE), pl.BlockSpec((1, BLOCK // CHUNK, STATE, inner), lambda s, c: (s, c, 0, 0)), row(8),
        ],
        out_shape=[
            sds((seqs, length, wide), BF), sds((seqs, heads, length), F32),
            sds((seqs, length, inner), BF), sds((seqs, length, inner), BF), sds((seqs, length, inner), BF),
            sds((seqs, length, inner), BF), sds((seqs, length, 2 * STATE), BF), sds((seqs, length, 2 * STATE), BF),
            sds((seqs, chunks, STATE, inner), BF), sds((seqs, 8, length), F32),
        ],
        scratch_shapes=[
            pltpu.VMEM((STATE, inner), F32), pltpu.VMEM((HALO + CHUNK, inner), F32),
            pltpu.VMEM((HALO + CHUNK, 2 * STATE), F32), pltpu.VMEM((CHUNK, inner), BF),
            pltpu.VMEM((CHUNK, inner), F32), pltpu.VMEM((3, 256, inner), BF), pltpu.VMEM((CHUNK, CHUNK), BF),
        ],
        compiler_params=pltpu.CompilerParams(vmem_limit_bytes=VMEM_LIMIT),
        name="mixer_forward",
    )(tok, weights, aux, cw, cbw, hp)


def mixer_backward(pz, raw, aux, cot, mixed, cv, pre, cbc, pbc, st, stat, cw, cbw, hp, out_all, weights, tok):
    seqs, length, width = cot.shape
    heads, inner = hp.shape[1], cw.shape[1]
    last = length // BLOCK - 1
    token = lambda size: pl.BlockSpec((1, BLOCK, size), lambda s, c: (s, last - c, 0))
    row = lambda high: pl.BlockSpec((1, high, BLOCK), lambda s, c: (s, 0, last - c))
    whole = lambda *shape: pl.BlockSpec(shape, lambda s, c: (0,) * len(shape))
    sds = jax.ShapeDtypeStruct
    return pl.pallas_call(
        functools.partial(backward_kernel, heads),
        grid=(seqs, length // BLOCK),
        in_specs=[
            token(pz.shape[2]), row(heads), row(AUX), token(width), token(inner), token(inner),
            token(inner), token(2 * STATE), token(2 * STATE),
            pl.BlockSpec((1, BLOCK // CHUNK, STATE, inner), lambda s, c: (s, last - c, 0, 0)), row(8),
            whole_once(8, inner), whole_once(8, 2 * STATE), whole_once(2, heads, 128),
            whole_once(*out_all.shape), whole_once(*weights.shape), token(width),
        ],
        out_specs=[
            token(weights.shape[1]), token(width),
            whole(8, inner), whole(8, 2 * STATE), whole(2, heads, 128), whole(8, width),
        ],
        out_shape=[
            sds((seqs, length, weights.shape[1]), BF), sds((seqs, length, width), BF),
            sds((8, inner), F32), sds((8, 2 * STATE), F32), sds((2, heads, 128), F32), sds((8, width), F32),
        ],
        scratch_shapes=[
            pltpu.VMEM((BLOCK, inner), F32),
            pltpu.VMEM((STATE, inner), F32), pltpu.VMEM((CHUNK + HALO, inner), F32),
            pltpu.VMEM((CHUNK + HALO, 2 * STATE), F32), pltpu.VMEM((CHUNK, inner), BF),
            pltpu.VMEM((CHUNK, inner), BF), pltpu.VMEM((CHUNK, inner), BF), pltpu.VMEM((CHUNK, inner), BF),
            pltpu.VMEM((CHUNK, inner), F32), pltpu.VMEM((CHUNK, inner), F32),
            pltpu.VMEM((3, 256, inner), BF), pltpu.VMEM((2, inner, 128), BF),
            pltpu.VMEM((CHUNK, CHUNK), BF), pltpu.VMEM((CHUNK, CHUNK), BF),
        ],
        compiler_params=pltpu.CompilerParams(vmem_limit_bytes=VMEM_LIMIT),
        name="mixer_backward",
    )(pz, raw, aux, cot, mixed, cv, pre, cbc, pbc, st, stat, cw, cbw, hp, out_all, weights, tok)


def out_kernel(gn_ref, cot_ref, out_ref, stat_ref, y_ref, stat_out_ref):
    y = dot_nt(gn_ref[0], out_ref[...])
    y_ref[0] = y.astype(BF)
    cross = jnp.sum(y * cot_ref[0].astype(F32), axis=1, keepdims=True)
    row = jnp.broadcast_to(cross, (cross.shape[0], 128)).T[0:8]
    stat_out_ref[0] = jnp.where(iota2(row.shape, 0) == 1, row, stat_ref[0])


def out_project(gn, cot, out_all, stat):
    seqs, length, inner = gn.shape
    width = cot.shape[2]
    size = 256
    token = lambda last: pl.BlockSpec((1, size, last), lambda s, c: (s, c, 0))
    row = pl.BlockSpec((1, 8, size), lambda s, c: (s, 0, c))
    sds = jax.ShapeDtypeStruct
    return pl.pallas_call(
        out_kernel,
        grid=(seqs, length // size),
        in_specs=[token(inner), token(width), whole_once(*out_all.shape), row],
        out_specs=[token(width), row],
        out_shape=[sds((seqs, length, width), BF), sds((seqs, 8, length), F32)],
        compiler_params=pltpu.CompilerParams(vmem_limit_bytes=VMEM_LIMIT),
        name="out_project",
    )(gn, cot, out_all, stat)


def doc_flags(segment, pad_mask):
    seqs, length = segment.shape
    position = lax.broadcasted_iota(jnp.int32, segment.shape, 1)
    rows = [segment.astype(F32), pad_mask.astype(F32)]
    back = []
    for k in range(1, TAPS):
        earlier = jnp.pad(segment, ((0, 0), (k, 0)), constant_values=-1)[:, :length]
        back.append(earlier == segment)
    rows += [b.astype(F32) for b in back]
    blocks = segment.reshape(seqs, length // CHUNK, CHUNK)
    tail = blocks[:, :, CHUNK - 1 :]
    previous = jnp.pad(tail, ((0, 0), (1, 0), (0, 0)), constant_values=-1)[:, :-1]
    rows.append((blocks == previous).reshape(seqs, length).astype(F32))
    rows.append((blocks == tail).reshape(seqs, length).astype(F32))
    rows.append(jnp.zeros_like(rows[0]))
    for k in range(1, TAPS):
        later = jnp.pad(segment, ((0, 0), (0, k)), constant_values=-1)[:, k:]
        rows.append((later == segment).astype(F32))
    rows += [jnp.zeros_like(rows[0])] * (AUX - len(rows))
    return jnp.stack(rows, axis=1)


MESH = pl.DeviceIdType.MESH


def factors(size):
    first = 4 if size % 8 == 0 else 1
    return first, size // (2 * first)


def gather_sites(first, second):
    return (2 + second) + (first - 1) * 2 * (1 + second) + (2 * first - 1) * (second - 1)


def gather_kernel(first, second, pair, arrays, *refs):
    own = refs[:arrays]
    tok = refs[arrays]
    full = refs[arrays + 1 : 2 * arrays + 1]
    tok_full = refs[2 * arrays + 1]
    send_sem, recv_sem, local_sem, tok_sem = refs[2 * arrays + 2 :]
    index = lax.axis_index("dp")
    me = lax.axis_index("tensor")
    a = lax.div(index, 2 * second)
    b = lax.rem(lax.div(index, 2), second)
    c = lax.rem(index, 2)
    at = lambda i, j, k: (i * second + j) * 2 + k
    sibling = at(a, b, 1 - c)
    has_up, has_down = a < first - 1, a > 0

    barrier = pltpu.get_barrier_semaphore()
    greet = lambda dp, t: pl.semaphore_signal(barrier, inc=1, device_id=(dp, t), device_id_type=MESH)
    greet(sibling, me)
    for j in range(1, second):
        greet(at(a, lax.rem(b + j, second), c), me)
    for i in range(1, first):
        greet(at(lax.rem(a + i, first), b, c), me)
    if pair:
        greet(index, 1 - me)
    pl.semaphore_wait(barrier, first + second - 1 + (1 if pair else 0))

    def place(which, shard):
        rows = own[which].shape[0]
        return full[which].at[pl.ds(pl.multiple_of(shard * rows, rows), rows)]

    def copies(site, shard, target, mine):
        return [
            pltpu.make_async_remote_copy(
                src_ref=own[w] if mine else place(w, shard),
                dst_ref=place(w, shard),
                send_sem=send_sem.at[w, site],
                recv_sem=recv_sem.at[w, shard],
                device_id=(target, me),
                device_id_type=MESH,
            )
            for w in range(arrays)
        ]

    sites = []

    def send(valid, shard, target, mine=False):
        site = len(sites)
        sites.append((valid, shard, target, mine))

        def start():
            for copy in copies(site, shard, target, mine):
                copy.start()

        start() if valid is None else pl.when(valid)(start)

    def arrived(shard):
        for copy in copies(0, shard, sibling, False):
            copy.wait_recv()

    def both(left, right):
        return right if left is None else left & right

    if pair:
        here = tok.shape[1]
        token_copy = pltpu.make_async_remote_copy(
            src_ref=tok,
            dst_ref=tok_full.at[:, pl.ds(pl.multiple_of(me * here, here), here)],
            send_sem=tok_sem.at[0],
            recv_sem=tok_sem.at[1],
            device_id=(index, 1 - me),
            device_id_type=MESH,
        )
        token_copy.start()
        token_local = pltpu.make_async_copy(
            tok, tok_full.at[:, pl.ds(pl.multiple_of(me * here, here), here)], tok_sem.at[2]
        )
        token_local.start()
    send(has_up, index, at(a + 1, b, c), True)
    send(has_down, index, at(a - 1, b, c), True)
    for j in range(1, second):
        send(None, index, at(a, lax.rem(b + j, second), c), True)
    send(None, index, sibling, True)
    local = [pltpu.make_async_copy(own[w], place(w, index), local_sem.at[w]) for w in range(arrays)]
    for copy in local:
        copy.start()

    steps = [(None, index)]
    for s in range(1, first):
        below, above = a - s >= 0, a + s < first
        steps += [(below, a - s), (above, a + s)]
        for valid, other, onward, target in (
            (below, a - s, has_up, at(a + 1, b, c)),
            (above, a + s, has_down, at(a - 1, b, c)),
        ):
            shard = at(other, b, c)
            pl.when(valid)(functools.partial(arrived, shard))
            send(valid & onward, shard, target)
            for j in range(1, second):
                send(valid, shard, at(a, lax.rem(b + j, second), c))
            send(valid, shard, sibling)
    for j in range(1, second):
        column = lax.rem(b + j, second)
        for s, (valid, other) in enumerate(steps):
            shard = at(a if s == 0 else other, column, c)
            arrived(shard) if valid is None else pl.when(valid)(functools.partial(arrived, shard))
            send(valid, shard, sibling)
    for i in range(first):
        for j in range(second):
            arrived(at(i, j, 1 - c))
    for site, (valid, shard, target, mine) in enumerate(sites):

        def finish(site=site, shard=shard, target=target, mine=mine):
            for copy in copies(site, shard, target, mine):
                copy.wait_send()

        finish() if valid is None else pl.when(valid)(finish)
    for copy in local:
        copy.wait()
    if pair:
        token_copy.wait()
        token_local.wait()


def gather_all(shards, tokens, size, n):
    first, second = factors(size)
    pair = n == 2
    arrays = len(shards)
    any_space = pl.BlockSpec(memory_space=pl.ANY)
    sds = jax.ShapeDtypeStruct
    seqs, here, width = tokens.shape
    out_shape = [sds((size * s.shape[0], s.shape[1]), s.dtype) for s in shards]
    out_shape.append(sds((seqs, 2 * here, width) if pair else (8, 128), tokens.dtype))
    *full, tok_full = pl.pallas_call(
        functools.partial(gather_kernel, first, second, pair, arrays),
        in_specs=[any_space] * arrays + [pl.BlockSpec(memory_space=pltpu.VMEM)],
        out_specs=[any_space] * (arrays + 1),
        out_shape=out_shape,
        scratch_shapes=[
            pltpu.SemaphoreType.DMA((arrays, gather_sites(first, second))),
            pltpu.SemaphoreType.DMA((arrays, size)),
            pltpu.SemaphoreType.DMA((arrays,)),
            pltpu.SemaphoreType.DMA((3,)),
        ],
        compiler_params=pltpu.CompilerParams(collective_id=0, has_side_effects=True),
        name="gather_all",
    )(*shards, tokens)
    return full, tok_full if pair else lax.all_gather(tokens, "tensor", axis=1, tiled=True)


def reduce_kernel(
    first, second, pair, shared, part_ref, flat_ref, out_ref, sum_ref,
    core_buf, x_buf, z_buf, y_flat, core_flat, x_flat, z_flat, stage,
    core_send, core_recv, x_send, x_recv, z_send, z_recv, flat_send, flat_recv,
):
    index = lax.axis_index("dp")
    me = lax.axis_index("tensor")
    a = lax.div(index, 2 * second)
    b = lax.rem(lax.div(index, 2), second)
    c = lax.rem(index, 2)
    rows = out_ref.shape[0]
    at = lambda i, j, k: (i * second + j) * 2 + k
    around = lambda i: lax.rem(a + i, first)
    aside = lambda j: lax.rem(b + j, second)
    sibling = at(a, b, 1 - c)
    columns = [at(a, aside(j), c) for j in range(1, second)]
    lines = [at(around(i), b, c) for i in range(1, first)]

    barrier = pltpu.get_barrier_semaphore()
    greet = lambda dp, t: pl.semaphore_signal(barrier, inc=1, device_id=(dp, t), device_id_type=MESH)
    for other in [sibling] + columns + lines:
        greet(other, me)
    if pair:
        greet(index, 1 - me)
    pl.semaphore_wait(barrier, first + second - 1 + (1 if pair else 0))

    started = []

    def send(src, dst, ss, rs, target, tensor=me):
        copy = pltpu.make_async_remote_copy(
            src_ref=src, dst_ref=dst, send_sem=ss, recv_sem=rs, device_id=(target, tensor), device_id_type=MESH
        )
        copy.start()
        started.append(copy)

    def arrived(dst, rs):
        pltpu.make_async_remote_copy(
            src_ref=dst, dst_ref=dst, send_sem=core_send.at[0], recv_sem=rs,
            device_id=(sibling, me), device_id_type=MESH,
        ).wait_recv()

    def block(i, j, k):
        return part_ref.at[pl.ds(pl.multiple_of(at(i, j, k) * rows, rows), rows)]

    order = [around(i) for i in range(1, first)] + [a]
    slot = lambda i, j: i * second + j
    if pair:
        send(flat_ref.at[0:shared], y_flat, flat_send.at[0], flat_recv.at[0], index, 1 - me)
    for j in list(range(1, second)) + [0]:
        for i in order:
            s = slot(i, aside(j))
            send(block(i, aside(j), 1 - c), core_buf.at[s], core_send.at[s], core_recv.at[s], sibling)
    if pair:
        arrived(y_flat, flat_recv.at[0])
        stage[0, 0:shared] = flat_ref[0:shared] + y_flat[...]
    else:
        stage[0, 0:shared] = flat_ref[0:shared]
    stage[0, shared:] = flat_ref[shared:]
    send(stage.at[0], core_flat, flat_send.at[1], flat_recv.at[1], sibling)
    for j in range(1, second):
        for i in order:
            s = slot(i, aside(j))
            arrived(core_buf.at[s], core_recv.at[s])
            core_buf[s] = (block(i, aside(j), c)[...].astype(F32) + core_buf[s].astype(F32)).astype(BF)
            t = i * (second - 1) + (second - j - 1)
            send(core_buf.at[s], x_buf.at[t], x_send.at[i * (second - 1) + j - 1], x_recv.at[t], at(a, aside(j), c))
    arrived(core_flat, flat_recv.at[1])
    stage[1] = stage[0] + core_flat[...]
    x_flat[b] = stage[1]
    for j in range(1, second):
        send(stage.at[1], x_flat.at[b], flat_send.at[1 + j], flat_recv.at[2 + b], at(a, aside(j), c))
    for n, i in enumerate(order):
        s = slot(i, b)
        arrived(core_buf.at[s], core_recv.at[s])
        total = block(i, b, c)[...].astype(F32) + core_buf[s].astype(F32)
        for j in range(1, second):
            t = i * (second - 1) + j - 1
            arrived(x_buf.at[t], x_recv.at[t])
            total = total + x_buf[t].astype(F32)
        if n < first - 1:
            core_buf[s] = total.astype(BF)
            send(core_buf.at[s], z_buf.at[a], z_send.at[n], z_recv.at[a], at(i, b, c))
        else:
            out_ref[...] = total
    for j in range(1, second):
        arrived(x_flat.at[aside(j)], flat_recv.at[2 + aside(j)])
    total = x_flat[0]
    for j in range(1, second):
        total = total + x_flat[j]
    stage[2] = total
    z_flat[a] = total
    for i in range(1, first):
        send(stage.at[2], z_flat.at[a], flat_send.at[second + i], flat_recv.at[2 + second + a], at(around(i), b, c))
    for i in range(1, first):
        arrived(z_buf.at[around(i)], z_recv.at[around(i)])
        out_ref[...] = out_ref[...] + z_buf[around(i)].astype(F32)
    for i in range(1, first):
        arrived(z_flat.at[around(i)], flat_recv.at[2 + second + around(i)])
    total = z_flat[0]
    for i in range(1, first):
        total = total + z_flat[i]
    sum_ref[...] = total
    for copy in started:
        copy.wait_send()


def reduce_all(part, flat, shared, size, n):
    first, second = factors(size)
    pair = n == 2
    if not pair:
        flat = jnp.concatenate([lax.psum(flat[:shared], "tensor"), flat[shared:]])
    rows, width = part.shape[0] // size, part.shape[1]
    sds = jax.ShapeDtypeStruct
    vmem = pl.BlockSpec(memory_space=pltpu.VMEM)
    blocks = first * second
    return pl.pallas_call(
        functools.partial(reduce_kernel, first, second, pair, shared),
        in_specs=[vmem, vmem],
        out_specs=[vmem, vmem],
        out_shape=[sds((rows, width), F32), sds(flat.shape, F32)],
        scratch_shapes=[
            pltpu.VMEM((blocks, rows, width), BF),
            pltpu.VMEM((first * max(second - 1, 1), rows, width), BF),
            pltpu.VMEM((first, rows, width), BF),
            pltpu.VMEM((shared, flat.shape[1]), F32),
            pltpu.VMEM(flat.shape, F32),
            pltpu.VMEM((second,) + flat.shape, F32),
            pltpu.VMEM((first,) + flat.shape, F32),
            pltpu.VMEM((3,) + flat.shape, F32),
            pltpu.SemaphoreType.DMA((blocks,)),
            pltpu.SemaphoreType.DMA((blocks,)),
            pltpu.SemaphoreType.DMA((first * max(second - 1, 1),)),
            pltpu.SemaphoreType.DMA((first * max(second - 1, 1),)),
            pltpu.SemaphoreType.DMA((first,)),
            pltpu.SemaphoreType.DMA((first,)),
            pltpu.SemaphoreType.DMA((1 + first + second,)),
            pltpu.SemaphoreType.DMA((2 + first + second,)),
        ],
        compiler_params=pltpu.CompilerParams(collective_id=1, has_side_effects=True, vmem_limit_bytes=VMEM_LIMIT),
        name="reduce_all",
    )(part, flat)


def gather_tokens(own, n, me):
    if n != 2:
        return lax.all_gather(own, "tensor", axis=1, tiled=True)
    other = lax.ppermute(own, "tensor", [(0, 1), (1, 0)])
    seqs, here, width = own.shape
    full = jnp.zeros((seqs, 2 * here, width), own.dtype)
    full = lax.dynamic_update_slice(full, own, (0, me * here, 0))
    return lax.dynamic_update_slice(full, other, (0, (1 - me) * here, 0))


def scatter_sum(make, size, n, me, dim):
    if n != 2:
        blocks = [make(i * size) for i in range(n)]
        return lax.psum_scatter(jnp.concatenate(blocks, axis=dim), "tensor", scatter_dimension=dim, tiled=True)
    away = lax.ppermute(make((1 - me) * size).astype(BF), "tensor", [(0, 1), (1, 0)])
    return make(me * size) + away.astype(F32)


def swap_sum(value, n):
    if n != 2:
        return lax.psum(value, "tensor")
    return value + lax.ppermute(value, "tensor", [(0, 1), (1, 0)])


def body(
    hidden, pre_gain, zx_weight, bc_weight, step_weight, conv_x_weight, conv_x_bias, conv_bc_weight, conv_bc_bias,
    step_bias, decay_log, skip_gain, norm_gain, out_weight, segment_ids, pad_mask, grad_out,
):
    n = lax.axis_size("tensor")
    me = lax.axis_index("tensor")
    heads = step_weight.shape[1]
    inner = heads * HEADDIM
    inner_all = inner * n
    here = hidden.shape[1]
    width = hidden.shape[2]
    size = lax.axis_size("dp")
    hidden_f = hidden.astype(F32)
    inv_rms = lax.rsqrt(jnp.mean(hidden_f * hidden_f, axis=-1, keepdims=True) + epsilon)
    normed_own = (hidden_f * inv_rms * pre_gain).astype(BF)
    shard = jnp.concatenate(
        [zx_weight, bc_weight, step_weight, jnp.zeros((zx_weight.shape[0], 128 - heads), BF)], axis=1
    )
    (weights,), normed = gather_all([shard], normed_own, size, n)
    out_own, cot_own, normed = lax.optimization_barrier((out_weight.T, grad_out, normed))
    out_all = lax.all_gather(out_own, "dp", axis=0, tiled=True)
    cot = gather_tokens(cot_own, n, me)

    aux = doc_flags(segment_ids, pad_mask)
    cw = jnp.concatenate(
        [conv_x_weight, conv_x_bias[None], jnp.repeat(skip_gain, HEADDIM)[None], norm_gain[None], jnp.zeros((1, inner), F32)]
    )
    cbw = jnp.concatenate([conv_bc_weight, conv_bc_bias[None], jnp.zeros((3, 2 * STATE), F32)])
    rate = -jnp.exp(decay_log)
    hp = jnp.broadcast_to(jnp.stack([step_bias, rate])[:, :, None], (2, heads, 128))

    pz, raw, mixed, gn, cv, pre, cbc, pbc, st, stat = mixer_forward(normed, weights, aux, cw, cbw, hp)
    y, stat = out_project(gn, cot, out_all, stat)
    stat = swap_sum(stat, n)
    gate_rms = lax.rsqrt(stat[:, 0] / inner_all + epsilon)
    back = jnp.stack([gate_rms, gate_rms**3 * (stat[:, 1] / inner_all)] + [jnp.zeros_like(gate_rms)] * 6, axis=1)
    y, back = lax.optimization_barrier((y, back))

    part = lambda rows: lambda start: lax.dynamic_slice_in_dim(rows, start, here, axis=1).astype(F32)
    rms_own = lax.dynamic_slice_in_dim(gate_rms, me * here, here, axis=1)[..., None]
    output = (hidden_f + rms_own * scatter_sum(part(y), here, n, me, 1)).astype(BF)
    cot_scaled = (cot.astype(F32) * gate_rms[..., None]).astype(BF)
    out_grad = jnp.einsum("str,stc->rc", cot_scaled, gn, preferred_element_type=F32).astype(BF)
    grad_out_weight = lax.psum_scatter(out_grad, "dp", scatter_dimension=0, tiled=True).astype(F32).T

    ge, dg, gch, gmap, ghead, gpre = mixer_backward(
        pz, raw, aux, cot, mixed, cv, pre, cbc, pbc, st, back, cw, cbw, hp, out_all, weights, normed
    )
    grad_normed = scatter_sum(part(dg), here, n, me, 1)
    weight_grad = jnp.einsum("stp,sty->py", normed, ge, preferred_element_type=F32).astype(BF)

    def rows_of(*vectors):
        flat = jnp.concatenate([v.reshape(-1) for v in vectors])
        rows = -(-flat.shape[0] // 8192) * 8
        return jnp.pad(flat, (0, rows * 1024 - flat.shape[0])).reshape(rows, 1024)

    shared = rows_of(gmap[:5], gpre[0] / pre_gain)
    skip_sums = jnp.sum(gch[5].reshape(heads, HEADDIM), axis=-1)
    flat = jnp.concatenate([shared, rows_of(gch[:5], gch[6], jnp.sum(ghead, axis=-1), skip_sums)])
    own_rows, flat = reduce_all(weight_grad, flat, shared.shape[0], size, n)
    wide = 2 * inner
    grad_zx_weight = own_rows[:, :wide]
    grad_step_weight = own_rows[:, wide + 2 * STATE :][:, :heads]
    grad_bc_weight = swap_sum(own_rows[:, wide : wide + 2 * STATE], n)

    gain_grad = grad_normed * pre_gain
    grad_hidden = (
        grad_out.astype(F32)
        + inv_rms * gain_grad
        - hidden_f * inv_rms**3 * jnp.mean(hidden_f * gain_grad, axis=-1, keepdims=True)
    ).astype(BF)

    sums = flat[: shared.shape[0]].reshape(-1)
    shared_map = sums[: 5 * 2 * STATE].reshape(5, 2 * STATE)
    grad_pre = sums[5 * 2 * STATE :][:width]
    rest = flat[shared.shape[0] :].reshape(-1)
    channel = rest[: 6 * inner].reshape(6, inner)
    per_head = rest[6 * inner :][: 3 * heads].reshape(3, heads)
    return (
        output, grad_hidden, grad_pre, grad_zx_weight, grad_bc_weight, grad_step_weight,
        channel[:4], channel[4], shared_map[:4], shared_map[4], per_head[0], per_head[1], per_head[2],
        channel[5], grad_out_weight,
    )


def solution(mesh):
    placed = (
        P("dp", "tensor", None), P(), P("dp", "tensor"), P("dp", None), P("dp", "tensor"), P(None, "tensor"),
        P("tensor"), P(), P(), P("tensor"), P("tensor"), P("tensor"), P("tensor"), P("tensor", "dp"),
        P("dp", None), P("dp", None), P("dp", "tensor", None),
    )
    return jax.shard_map(
        body,
        mesh=mesh,
        in_specs=placed,
        out_specs=(
            P("dp", "tensor", None), P("dp", "tensor", None), P(), P("dp", "tensor"), P("dp", None), P("dp", "tensor"),
            P(None, "tensor"), P("tensor"), P(), P(), P("tensor"), P("tensor"), P("tensor"), P("tensor"),
            P("tensor", "dp"),
        ),
        check_vma=False,
    )
```

time: 397 us -> 267 us (0.67)
  Pallas kernels: 48.5 us -> 168 us
  waiting for transfers between devices: 126 us -> 25 us
  blocking collectives: 95.6 us -> 0 us
  matrix products: 53.5 us -> 12.2 us
  local copies, waits for them, and re-layouts: 35.3 us -> 26.9 us
    pallas_call x2 -> x5, Pallas kernels: 48.5 us -> 168 us  [the longest x1 55.7 us: reduce_all(): pl.pallas_call(functools.partial(reduce_kernel, first, second, pair, shar...]
    psum x1 -> x0, blocking collectives: 58 us -> none  [body(): flat = lax.psum(flat, 'dp')]
    reduce_scatter x1 -> x0, waiting for transfers between devices: 46.8 us -> none  [body(): lax.psum_scatter(zx_grad, 'dp', scatter_dimension=0, tiled=True).astype(F32)]
    dot_general x16 -> x2, matrix products: 53.5 us -> 12.2 us  [the longest x1 8.35 us: body(): jnp.einsum('stp,sty->py', normed, ge, preferred_element_type=F32).astype(BF)]
    all_gather x2 -> x0, blocking collectives: 37.6 us -> none  [the longest x1 24.4 us: body(): lax.all_gather(jnp.concatenate([bc_weight, step_weight], axis=1), 'dp', a...]
    all_gather x2 -> x1, waiting for transfers between devices: 39.9 us -> 3.65 us  [body(): out_all = lax.all_gather(out_own, 'dp', axis=0, tiled=True)]
    unnamed x6 -> x2, waiting for transfers between devices: 20.7 us -> 0.03 us
    ppermute x2, waiting for transfers between devices: 2.36 us -> 21.4 us  [swap_sum(): return value + lax.ppermute(value, 'tensor', [(0, 1), (1, 0)])]
  transfers between devices with their start and end apart: 12 -> 7, of which waited for: 6 -> 3; matrix products, arithmetic and copies ran while one was open for 18% -> 11% of each run, Pallas kernels for 0% -> 47%
where the time goes in v2:
time: 267 us; the launch traced here: 266 us
  Pallas kernels  168 us (63%)
  local copies, waits for them, and re-layouts  26.9 us (10%)
  waiting for transfers between devices  25 us (9%)
  between operations  14.5 us (5%)
  other arithmetic  12.7 us (5%)
  matrix products  12.2 us (5%)
  starting transfers between devices  6.69 us (3%)
    pallas_call x1, Pallas kernels, reduce_all(): pl.pallas_call(functools.partial(reduce_kernel, first, second, pair, shar...  55.7 us
    pallas_call x1, Pallas kernels, mixer_backward(): pl.pallas_call(functools.partial(backward_kernel, heads), grid=(seqs, len...  43.1 us
    pallas_call x1, Pallas kernels, gather_all(): pl.pallas_call(functools.partial(gather_kernel, first, second, pair, arra...  38.8 us
    pallas_call x1, Pallas kernels, mixer_forward(): pl.pallas_call(functools.partial(forward_kernel, heads), grid=(seqs, leng...  27 us
    ppermute x2, waiting for transfers between devices, swap_sum(): return value + lax.ppermute(value, 'tensor', [(0, 1), (1, 0)])  21.4 us
    unnamed x63, local copies, waits for them, and re-layouts  13.4 us
    dot_general x1, matrix products, body(): jnp.einsum('stp,sty->py', normed, ge, preferred_element_type=F32).astype(BF)  8.35 us
  transfers between devices with their start and end apart: 7, of which 3 were waited for; matrix products, arithmetic and copies ran while one was open for 11% of the time, Pallas kernels for 47%

profile of v2, /device:TPU:0, one launch (start us, length us, event | category | flops | bytes accessed | tf_op | source)
XLA Modules:
  0.0 266.1 jit_solution(10705042707275061541)
XLA Ops:
  7.2 1.5 fusion.1
  8.8 0.8 copy.32
  9.7 2.6 fusion.3.refs_1_
  12.3 0.8 concatenate.18.refs_0_
  13.1 38.8 %gather_all.1 = (bf16[1024,2432]{1,0:T(8,128)(2,1)}, bf16[1,1024,1024]{2,1,0:T(8,128)(2,1)}) custom-call(bf16[64,2432]{1,0:T(8,128)(2,1)} %concatenate.18.refs_0_, bf16[1,512,1024]{2,1,0:T(8,128)(2,1)} %fusion.3.refs_1_), custom_call_target="tpu_custom_call" | custom-call | tf_op jit(solution)/shard_map/gather_all/pallas_call | solution.py:647
  51.9 0.0 reduce-scatter.2.cloned.1.call-start
  52.0 1.6 collective-permute-start
  53.6 0.1 slice.128
  53.7 0.1 copy.35
  53.8 0.1 broadcast_in_dim.38
  53.9 0.1 broadcast_in_dim_reshape.3
  53.9 0.1 pad.57.clone
  54.1 0.1 slice_bitcast_fusion.2
  54.2 0.1 eq.49
  54.2 0.1 eq.52
  54.3 0.1 fusion.30
  54.4 0.1 stack.92.aux_ref
  54.6 0.1 maximum_maximum_fusion.cbw_ref
  54.7 0.1 broadcast_in_dim.43.hp_ref
  54.8 27.0 %mixer_forward.1 = (bf16[1,1024,2304]{2,1,0:T(8,128)(2,1)}, f32[1,16,1024]{2,1,0:T(8,128)S(1)}, bf16[1,1024,1024]{2,1,0:T(8,128)(2,1)S(1)}, bf16[1,1024,1024]{2,...) custom-call(bf16[1,1024,1024]{2,1,0:T(8,128)(2,1)} %get-tuple-elemen, ...), custom_call_target="tpu_custom_call" | custom-call | tf_op jit(solution)/shard_map/mixer_forward/pallas_call | solution.py:388
  81.7 1.4 copy-done.10
  83.1 1.3 copy-done.11
  84.5 0.3 broadcast_in_dim.44
  84.7 2.1 constant_dynamic-update-slice_fusion.1
  86.9 1.3 constant_dynamic-update-slice_fusion.cot_ref
  88.2 3.6 %all-gather.2.cloned.1.call-done.out_ref = bf16[1024,1024]{1,0:T(8,128)(2,1)} async-done(((bf16[64,1024]{1,0:T(8,128)(2,1)}), bf16[1024,1024]{1,0:T(8,128)(2,1)}) %all-gather.2.cloned.1.call-update) | async-done | bytes 2097168 | tf_op jit(solution)/shard_map/all_gather | solution.py:851
  91.9 1.6 copy-done
  93.5 1.6 copy-done.12
  95.1 3.5 %out_project.1 = (bf16[1,1024,1024]{2,1,0:T(8,128)(2,1)S(1)}, f32[1,8,1024]{2,1,0:T(8,128)S(1)}) custom-call(bf16[1,1024,1024]{2,1,0:T(8,128)(2,1)S(1)} %copy-done.12, bf16[1,1024,1024]{2,1,0:T(8,128)(2,1)S(1)} %constant_dynamic-update-slice_fusion.cot_ref, bf16[1024,1024]{1,0:T(8,128)(2,1)S(1)} %copy-done, f32[1,8,1024]{2,1,0:T(8,128)S(1)} %get-tuple-element.48.stat_ref), custom_call_target="tpu_custom_call" | custom-call | tf_op jit(solution)/shard_map/out_project/pallas_call | solution.py:470
  98.5 1.4 copy-done.3
  99.9 1.5 collective-permute-start.1
  101.4 0.1 pad.51.clone
  101.4 2.4 collective-permute-done.1
  103.8 3.9 %fusion.15 = bf16[1024,1024]{1,0:T(8,128)(2,1)} fusion(bf16[1,1024,1024]{2,1,0:T(8,128)(2,1)S(1)} %copy-done.12, bf16[1,1024,1024]{2,1,0:T(8,128)(2,1)S(1)} %constant_dynamic-update-slice_fusion.cot_ref, f32[1024]{0:T(1024)S(1)} %bitcast.75), kind=kOutput, calls=%fused_computation.22 | convolution fusion | flops 2151677952 | bytes 6295552 | tf_op jit(solution)/shard_map/str,stc->rc/dot_general | solution.py:873
  107.7 0.1 pad_maximum_fusion.1.stat_ref
  107.8 1.6 copy-done.7
  109.4 1.6 copy-done.9
  111.0 43.1 %mixer_backward.1 = (bf16[1,1024,2432]{2,1,0:T(8,128)(2,1)}, bf16[1,1024,1024]{2,1,0:T(8,128)(2,1)S(1)}, f32[8,1024]{1,0:T(8,128)S(1)}, f32[8,256]{1,0:T(8,128)S...) custom-call(bf16[1,1024,2304]{2,1,0:T(8,128)(2,1)} %get-tuple-element.52.pz_ref, ...), custom_call_target="tpu_custom_call" | custom-call | tf_op jit(solution)/shard_map/mixer_backward/pallas_call | solution.py:423
  154.1 1.3 copy-done.1
  155.4 0.1 reduce_sum.38
  155.5 0.1 reshape.212
  155.6 0.1 reshape_squeeze.3
  155.7 0.1 reduce_sum.39
  155.8 0.1 concatenate.22
  155.9 2.4 constant_dynamic-slice_fusion
  158.3 1.5 collective-permute-start.3
  159.8 8.4 %convolution_convert_fusion.part_ref = bf16[1024,2432]{1,0:T(8,128)(2,1)S(1)} fusion(bf16[1,1024,2432]{2,1,0:T(8,128)(2,1)} %get-tuple-element.62, bf16[1,1024,1024]{2,1,0:T(8,128)(2,1)S(1)} %copy-done.14), kind=kOutput, calls=%fused_computation | convolution fusion | flops 5102764032 | bytes 12058624 | tf_op jit(solution)/shard_map/stp,sty->py/dot_general | solution.py:880
  168.2 55.7 %reduce_all.1 = (f32[64,2432]{1,0:T(8,128)S(1)}, f32[16,1024]{1,0:T(8,128)S(1)}) custom-call(bf16[1024,2432]{1,0:T(8,128)(2,1)S(1)} %convolution_convert_fusion.part_ref, f32[16,1024]{1,0:T(8,128)S(1)} %pad_maximum_fusion.flat_ref), custom_call_target="tpu_custom_call" | custom-call | tf_op jit(solution)/shard_map/reduce_all/pallas_call | solution.py:779
  223.9 1.0 constant_dynamic-slice_fusion.1
  225.0 1.5 collective-permute-start.2
  226.5 0.6 fusion.32
  227.1 0.6 slice.147
  227.8 0.6 slice.161
  228.3 0.6 slice.160
  228.9 0.8 slice.144
  229.8 0.6 slice.150
  230.4 0.7 copy.34
  231.0 0.5 collective-permute-start.4
  231.5 0.6 fusion.33
  232.1 19.0 %collective-permute-done.4 = f32[64,256]{1,0:T(8,128)S(1)} collective-permute-done((f32[64,256]{1,0:T(8,128)S(1)}, f32[64,256]{1,0:T(8,128)S(1)}, u32[]{:S(2)}, u32[]{:S(2)}) %collective-permute-start.4) | collective-permute-done | bytes 65568 | tf_op jit(solution)/shard_map/ppermute | solution.py:828
  251.1 0.6 slice_add_fusion
  251.7 2.1 fusion.8
  253.9 3.8 %fusion.7 = (bf16[1,512,1024]{2,1,0:T(8,128)(2,1)}, bf16[1,512,1024]{2,1,0:T(8,128)(2,1)}) fusion(bf16[1,512,1024]{2,1,0:T(8,128)(2,1)S(1)} %copy-done.13, bf16[1,512,1024]{2,1,0:T(8,128)(2,1)} %param.33, bf16[1,512,1024]{2,1,0:T(8,128)(2,1)} %collective-permute-done.3, f32[512]{0:T(512)S(1)} %broadcast_multiply_fusion, f32[512]{0:T(512)S(1)} %get-tuple-element.104, ...), kind=kLoop, calls=%fused_computation.14 | loop fusion | flops 9437184 | bytes 8400900 | tf_op jit(solution)/shard_map/convert_element_type | solution.py:901
  257.6 1.6 convert_bitcast_fusion
  (86 shorter events, 0.4 us)
Async XLA Ops:
  7.2 5.1 %copy-start.18 = (bf16[64,256]{1,0:T(8,128)(2,1)S(1)}, bf16[64,256]{1,0:T(8,128)(2,1)}, u32[]{:S(2)}) copy-start(bf16[64,256]{1,0:T(8,128)(2,1)} %param.20) | copy-start | bytes 98308
  7.2 5.1 %copy-start.15 = (bf16[64,2048]{1,0:T(8,128)(2,1)S(1)}, bf16[64,2048]{1,0:T(8,128)(2,1)}, u32[]{:S(2)}) copy-start(bf16[64,2048]{1,0:T(8,128)(2,1)} %param.19) | copy-start | bytes 786436
  7.2 84.7 %all-gather.2.cloned.1.call-start = ((), (), s32[]{:S(2)}) async-start(), calls=%async_computation.1 | async-start | bytes 2228224 | tf_op jit(solution)/shard_map/all_gather | solution.py:851
  9.6 44.0 %copy-start.17 = (s32[1,1024]{1,0:T(1,128)S(1)}, s32[1,1024]{1,0:T(1,128)}, u32[]{:S(2)}) copy-start(s32[1,1024]{1,0:T(1,128)} %param.31) | copy-start | bytes 12292
  9.6 44.0 %copy-start.23 = (s32[1,1024]{1,0:T(1,128)S(1)}, s32[1,1024]{1,0:T(1,128)}, u32[]{:S(2)}) copy-start(s32[1,1024]{1,0:T(1,128)} %param.32) | copy-start | bytes 12292
  9.6 44.2 %copy-start.25 = (f32[16]{0:T(128)S(1)}, f32[16]{0:T(128)}, u32[]{:S(2)}) copy-start(f32[16]{0:T(128)} %param.28) | copy-start | bytes 196
  9.6 44.4 %copy-start.19 = (f32[4,1024]{1,0:T(4,128)S(1)}, f32[4,1024]{1,0:T(4,128)}, u32[]{:S(2)}) copy-start(f32[4,1024]{1,0:T(4,128)} %param.22) | copy-start | bytes 49156
  9.6 44.4 %copy-start.20 = (f32[1024]{0:T(1024)S(1)}, f32[1024]{0:T(1024)}, u32[]{:S(2)}) copy-start(f32[1024]{0:T(1024)} %param.23) | copy-start | bytes 12292
  9.6 44.4 %copy-start.21 = (f32[1024]{0:T(1024)S(1)}, f32[1024]{0:T(1024)}, u32[]{:S(2)}) copy-start(f32[1024]{0:T(1024)} %param.29) | copy-start | bytes 12292
  9.6 44.9 %copy-start.27 = (f32[16]{0:T(128)S(1)}, f32[16]{0:T(128)}, u32[]{:S(2)}) copy-start(f32[16]{0:T(128)} %param.27) | copy-start | bytes 196
  9.7 44.9 %copy-start.26 = (f32[16]{0:T(128)S(1)}, f32[16]{0:T(128)}, u32[]{:S(2)}) copy-start(f32[16]{0:T(128)} %param.26) | copy-start | bytes 196
  9.7 44.9 %copy-start.22 = (f32[4,256]{1,0:T(4,128)S(1)}, f32[4,256]{1,0:T(4,128)}, u32[]{:S(2)}) copy-start(f32[4,256]{1,0:T(4,128)} %param.24) | copy-start | bytes 12292
  9.7 44.9 %copy-start.24 = (f32[256]{0:T(256)S(1)}, f32[256]{0:T(256)}, u32[]{:S(2)}) copy-start(f32[256]{0:T(256)} %param.25) | copy-start | bytes 3076
  51.9 205.7 %reduce-scatter.2.cloned.1.call-start = ((), (), s32[]{:S(2)}) async-start(), calls=%async_computation.2 | async-start | bytes 2228224 | tf_op jit(solution)/shard_map/reduce_scatter | solution.py:874
  52.0 34.9 %collective-permute-start = (bf16[1,512,1024]{2,1,0:T(8,128)(2,1)}, bf16[1,512,1024]{2,1,0:T(8,128)(2,1)}, u32[]{:S(2)}, u32[]{:S(2)}) collective-permute-start(bf16[1,512,1024]{2,1,0:T(8,128)(2,1)} %param.33), channel_id=1, source_target_pairs={{0,1},{1,0},{2,3},{3,2},{4,5},{5,4},{6,7},{7,6},{8,9},{9,8},{10,11... | collective-permute-start | bytes 3145736 | tf_op jit(solution)/shard_map/ppermute | solution.py:810
  81.7 1.4 copy-start.10
  83.1 1.3 copy-start.11
  84.4 2.4 copy-start.6
  84.4 2.4 copy-start.8
  91.9 1.6 copy-start
  93.5 1.6 copy-start.12
  98.5 1.4 copy-start.3
  99.9 3.9 %collective-permute-start.1 = (f32[1,8,1024]{2,1,0:T(8,128)S(1)}, f32[1,8,1024]{2,1,0:T(8,128)S(1)}, u32[]{:S(2)}, u32[]{:S(2)}) collective-permute-start(f32[1,8,1024]{2,1,0:T(8,128)S(1)} %get-tuple-element.49), channel_id=1, source_target_pairs={{0,1},{1,0},{2,3},{3,2},{4,5},{5,4},{6,7},{7,6},{8,9},{9,8},{10,11... | collective-permute-start | bytes 98312 | tf_op jit(solution)/shard_map/ppermute | solution.py:828
  107.8 1.6 copy-start.7
  109.4 1.6 copy-start.9
  111.0 44.6 %copy-start.16 = (f32[1024]{0:T(1024)S(1)}, f32[1024]{0:T(1024)}, u32[]{:S(2)}) copy-start(f32[1024]{0:T(1024)} %param.18) | copy-start | bytes 12292
  154.1 1.3 copy-start.1
  155.4 4.4 %copy-start.14 = (bf16[1,1024,1024]{2,1,0:T(8,128)(2,1)S(1)}, bf16[1,1024,1024]{2,1,0:T(8,128)(2,1)}, u32[]{:S(2)}) copy-start(bf16[1,1024,1024]{2,1,0:T(8,128)(2,1)} %get-tuple-element.43.tok_ref) | copy-start | bytes 6291460
  158.3 93.5 %collective-permute-start.3 = (bf16[1,512,1024]{2,1,0:T(8,128)(2,1)}, bf16[1,512,1024]{2,1,0:T(8,128)(2,1)}, u32[]{:S(2)}, u32[]{:S(2)}) collective-permute-start(bf16[1,512,1024]{2,1,0:T(8,128)(2,1)} %constant_dynamic-slice_fusion), channel_id=1, source_target_pairs={{0,1},{1,0},{2,3},{3,2},{4,5},{5,4},{6,7},{7,6},{8,9},{9,8},{10,11... | collective-permute-start | bytes 3145736 | tf_op jit(solution)/shard_map/ppermute | solution.py:821
  168.2 55.8 %copy-start.4 = (bf16[1,1024,1024]{2,1,0:T(8,128)(2,1)S(1)}, bf16[1,1024,1024]{2,1,0:T(8,128)(2,1)}, u32[]{:S(2)}) copy-start(bf16[1,1024,1024]{2,1,0:T(8,128)(2,1)} %copy-done.3) | copy-start | bytes 6291460
  223.9 27.8 %copy-start.2 = (bf16[1,1024,1024]{2,1,0:T(8,128)(2,1)S(1)}, bf16[1,1024,1024]{2,1,0:T(8,128)(2,1)}, u32[]{:S(2)}) copy-start(bf16[1,1024,1024]{2,1,0:T(8,128)(2,1)} %copy-done.1) | copy-start | bytes 6291460
  225.0 28.9 %collective-permute-start.2 = (bf16[1,512,1024]{2,1,0:T(8,128)(2,1)}, bf16[1,512,1024]{2,1,0:T(8,128)(2,1)}, u32[]{:S(2)}, u32[]{:S(2)}) collective-permute-start(bf16[1,512,1024]{2,1,0:T(8,128)(2,1)} %constant_dynamic-slice_fusion.1), channel_id=1, source_target_pairs={{0,1},{1,0},{2,3},{3,2},{4,5},{5,4},{6,7},{7,6},{8,9},{9,8},{10,11... | collective-permute-start | bytes 3145736 | tf_op jit(solution)/shard_map/ppermute | solution.py:821
  231.0 22.8 %copy-start.5 = (bf16[1,1024,1024]{2,1,0:T(8,128)(2,1)S(1)}, bf16[1,1024,1024]{2,1,0:T(8,128)(2,1)}, u32[]{:S(2)}) copy-start(bf16[1,1024,1024]{2,1,0:T(8,128)(2,1)} %copy-done.3) | copy-start | bytes 6291460
  231.0 22.8 %copy-start.13 = (bf16[1,512,1024]{2,1,0:T(8,128)(2,1)S(1)}, bf16[1,512,1024]{2,1,0:T(8,128)(2,1)}, u32[]{:S(2)}) copy-start(bf16[1,512,1024]{2,1,0:T(8,128)(2,1)} %param.17) | copy-start | bytes 3145732
  231.0 20.1 %collective-permute-start.4 = (f32[64,256]{1,0:T(8,128)S(1)}, f32[64,256]{1,0:T(8,128)S(1)}, u32[]{:S(2)}, u32[]{:S(2)}) collective-permute-start(f32[64,256]{1,0:T(8,128)S(1)} %slice.145), channel_id=1, source_target_pairs={{0,1},{1,0},{2,3},{3,2},{4,5},{5,4},{6,7},{7,6},{8,9},{9,8},{10,11... | collective-permute-start | bytes 196616 | tf_op jit(solution)/shard_map/ppermute | solution.py:828
Sparse Core Ops, SparseCore 0:
  52.1 39.7 all-gather.1
  107.9 60.2 reduce-scatter.1

commit v3 on v2

--- a/solution.py
+++ b/solution.py
@@ -15,7 +15,7 @@
 LOG2E = 1.4426950408889634
 FAR = -1e30
 BLOCK = 256
-VMEM_LIMIT = 44 * 1024 * 1024
+VMEM_LIMIT = 58 * 1024 * 1024
 epsilon = 1e-05
 BF = jnp.bfloat16
 F32 = jnp.float32
@@ -661,28 +661,34 @@
     return full, tok_full if pair else lax.all_gather(tokens, "tensor", axis=1, tiled=True)
 
 
+PIECES = 2
+
+
 def reduce_kernel(
-    first, second, pair, shared, part_ref, flat_ref, out_ref, sum_ref,
-    core_buf, x_buf, z_buf, y_flat, core_flat, x_flat, z_flat, stage,
-    core_send, core_recv, x_send, x_recv, z_send, z_recv, flat_send, flat_recv,
+    first, second, pair, fused, shared, tok_ref, ge_ref, flat_ref, dg_ref, hidden_ref, cot_ref, gain_ref,
+    out_ref, sum_ref, gh_ref,
+    part_buf, core_buf, x_buf, z_buf, acc, dg_buf, y_flat, core_flat, x_flat, z_flat, stage,
+    core_send, core_recv, x_send, x_recv, z_send, z_recv, flat_send, flat_recv, dg_sem,
 ):
     index = lax.axis_index("dp")
     me = lax.axis_index("tensor")
     a = lax.div(index, 2 * second)
     b = lax.rem(lax.div(index, 2), second)
     c = lax.rem(index, 2)
-    rows = out_ref.shape[0]
+    rows = out_ref.shape[0] // PIECES
     at = lambda i, j, k: (i * second + j) * 2 + k
     around = lambda i: lax.rem(a + i, first)
     aside = lambda j: lax.rem(b + j, second)
     sibling = at(a, b, 1 - c)
-    columns = [at(a, aside(j), c) for j in range(1, second)]
-    lines = [at(around(i), b, c) for i in range(1, first)]
+    part_ref = part_buf if fused else ge_ref
 
     barrier = pltpu.get_barrier_semaphore()
     greet = lambda dp, t: pl.semaphore_signal(barrier, inc=1, device_id=(dp, t), device_id_type=MESH)
-    for other in [sibling] + columns + lines:
-        greet(other, me)
+    greet(sibling, me)
+    for j in range(1, second):
+        greet(at(a, aside(j), c), me)
+    for i in range(1, first):
+        greet(at(around(i), b, c), me)
     if pair:
         greet(index, 1 - me)
     pl.semaphore_wait(barrier, first + second - 1 + (1 if pair else 0))
@@ -702,17 +708,49 @@
             device_id=(sibling, me), device_id_type=MESH,
         ).wait_recv()
 
-    def block(i, j, k):
-        return part_ref.at[pl.ds(pl.multiple_of(at(i, j, k) * rows, rows), rows)]
-
-    order = [around(i) for i in range(1, first)] + [a]
-    slot = lambda i, j: i * second + j
+    def block(i, j, k, q):
+        return part_ref.at[pl.ds(pl.multiple_of((at(i, j, k) * PIECES + q) * rows, rows), rows)]
+
+    if first == 4:
+        near = jnp.minimum(a, 3 - a)
+        order = [jnp.where(a < 2, d, 3 - d) for d in (3 + 0 * a, 2 - 2 * near, 1 + near)] + [a]
+    else:
+        order = [a]
+    slot = lambda i, j, q: (i * second + j) * PIECES + q
+    pieces_of = [(n, i, q) for n, i in enumerate(order) for q in range(PIECES)]
+
     if pair:
         send(flat_ref.at[0:shared], y_flat, flat_send.at[0], flat_recv.at[0], index, 1 - me)
-    for j in list(range(1, second)) + [0]:
-        for i in order:
-            s = slot(i, aside(j))
-            send(block(i, aside(j), 1 - c), core_buf.at[s], core_send.at[s], core_recv.at[s], sibling)
+        here = hidden_ref.shape[1]
+        own_rows = pl.ds(pl.multiple_of(me * here, here), here)
+        away_rows = pl.ds(pl.multiple_of((1 - me) * here, here), here)
+        send(dg_ref.at[:, away_rows], dg_buf, dg_sem.at[0], dg_sem.at[1], index, 1 - me)
+
+    def produce(i, j):
+        if fused:
+            there = pl.ds(pl.multiple_of(at(i, aside(j), 0) * rows * PIECES, 128), 2 * rows * PIECES)
+            part_buf[there] = lax.dot_general(
+                tok_ref[:, there], ge_ref[...], (((0,), (0,)), ((), ())), preferred_element_type=F32
+            ).astype(BF)
+        for q in range(PIECES):
+            s = slot(i, aside(j), q)
+            send(block(i, aside(j), 1 - c, q), core_buf.at[s], core_send.at[s], core_recv.at[s], sibling)
+
+    def cross_over(i, j):
+        for q in range(PIECES):
+            s = slot(i, aside(j), q)
+            arrived(core_buf.at[s], core_recv.at[s])
+            core_buf[s] = (block(i, aside(j), c, q)[...].astype(F32) + core_buf[s].astype(F32)).astype(BF)
+            t = (i * (second - 1) + second - j - 1) * PIECES + q
+            u = (i * (second - 1) + j - 1) * PIECES + q
+            send(core_buf.at[s], x_buf.at[t], x_send.at[u], x_recv.at[t], at(a, aside(j), c))
+
+    work = [(i, j) for j in list(range(1, second)) + [0] for i in order]
+    for n, (i, j) in enumerate(work):
+        produce(i, j)
+        if n >= 1 and work[n - 1][1] > 0:
+            cross_over(*work[n - 1])
+
     if pair:
         arrived(y_flat, flat_recv.at[0])
         stage[0, 0:shared] = flat_ref[0:shared] + y_flat[...]
@@ -720,31 +758,36 @@
         stage[0, 0:shared] = flat_ref[0:shared]
     stage[0, shared:] = flat_ref[shared:]
     send(stage.at[0], core_flat, flat_send.at[1], flat_recv.at[1], sibling)
-    for j in range(1, second):
-        for i in order:
-            s = slot(i, aside(j))
-            arrived(core_buf.at[s], core_recv.at[s])
-            core_buf[s] = (block(i, aside(j), c)[...].astype(F32) + core_buf[s].astype(F32)).astype(BF)
-            t = i * (second - 1) + (second - j - 1)
-            send(core_buf.at[s], x_buf.at[t], x_send.at[i * (second - 1) + j - 1], x_recv.at[t], at(a, aside(j), c))
     arrived(core_flat, flat_recv.at[1])
     stage[1] = stage[0] + core_flat[...]
     x_flat[b] = stage[1]
     for j in range(1, second):
         send(stage.at[1], x_flat.at[b], flat_send.at[1 + j], flat_recv.at[2 + b], at(a, aside(j), c))
-    for n, i in enumerate(order):
-        s = slot(i, b)
+
+    for n, i, q in pieces_of:
+        s = slot(i, b, q)
         arrived(core_buf.at[s], core_recv.at[s])
-        total = block(i, b, c)[...].astype(F32) + core_buf[s].astype(F32)
+        total = block(i, b, c, q)[...].astype(F32) + core_buf[s].astype(F32)
         for j in range(1, second):
-            t = i * (second - 1) + j - 1
+            t = (i * (second - 1) + j - 1) * PIECES + q
             arrived(x_buf.at[t], x_recv.at[t])
             total = total + x_buf[t].astype(F32)
         if n < first - 1:
-            core_buf[s] = total.astype(BF)
-            send(core_buf.at[s], z_buf.at[a], z_send.at[n], z_recv.at[a], at(i, b, c))
+            down = jnp.where(i > a, 0, 1)
+            z = (down * first + i) * PIECES + q
+            acc[...] = total
+
+            @pl.when(jnp.where(i > a, a, first - 1 - a) > 0)
+            def _():
+                arrived(z_buf.at[z], z_recv.at[z])
+                acc[...] = acc[...] + z_buf[z].astype(F32)
+
+            core_buf[s] = acc[...].astype(BF)
+            send(
+                core_buf.at[s], z_buf.at[z], z_send.at[n * PIECES + q], z_recv.at[z], at(a + 1 - 2 * down, b, c)
+            )
         else:
-            out_ref[...] = total
+            out_ref[q * rows : (q + 1) * rows] = total
     for j in range(1, second):
         arrived(x_flat.at[aside(j)], flat_recv.at[2 + aside(j)])
     total = x_flat[0]
@@ -754,9 +797,36 @@
     z_flat[a] = total
     for i in range(1, first):
         send(stage.at[2], z_flat.at[a], flat_send.at[second + i], flat_recv.at[2 + second + a], at(around(i), b, c))
-    for i in range(1, first):
-        arrived(z_buf.at[around(i)], z_recv.at[around(i)])
-        out_ref[...] = out_ref[...] + z_buf[around(i)].astype(F32)
+
+    if pair:
+        arrived(dg_buf, dg_sem.at[1])
+        size = 128
+
+        def norm_rows(step, carry):
+            seq, cut = lax.div(step, here // size), lax.rem(step, here // size)
+            mine = pl.ds(pl.multiple_of(cut * size, size), size)
+            full = pl.ds(pl.multiple_of(me * here + cut * size, size), size)
+            hid = hidden_ref[seq, mine].astype(F32)
+            inv = lax.rsqrt(jnp.mean(hid * hid, axis=-1, keepdims=True) + epsilon)
+            gain = (dg_ref[seq, full].astype(F32) + dg_buf[seq, mine].astype(F32)) * gain_ref[0:1]
+            pull = inv * inv * inv * jnp.mean(hid * gain, axis=-1, keepdims=True)
+            gh_ref[seq, mine] = (cot_ref[seq, mine].astype(F32) + inv * gain - hid * pull).astype(BF)
+            return carry
+
+        lax.fori_loop(0, hidden_ref.shape[0] * (here // size), norm_rows, 0)
+    else:
+        gh_ref[...] = jnp.zeros_like(gh_ref)
+
+    for q in range(PIECES):
+        cut_rows = slice(q * rows, (q + 1) * rows)
+        for down, there in ((0, a), (1, first - 1 - a)):
+            z = (down * first + a) * PIECES + q
+
+            @pl.when(there > 0)
+            def _(z=z, cut_rows=cut_rows):
+                arrived(z_buf.at[z], z_recv.at[z])
+                out_ref[cut_rows] = out_ref[cut_rows] + z_buf[z].astype(F32)
+
     for i in range(1, first):
         arrived(z_flat.at[around(i)], flat_recv.at[2 + second + around(i)])
     total = z_flat[0]
@@ -767,41 +837,51 @@
         copy.wait_send()
 
 
-def reduce_all(part, flat, shared, size, n):
+def reduce_all(tok, ge, flat, shared, dg, hidden, cot_own, pre_gain, size, n):
     first, second = factors(size)
     pair = n == 2
+    seqs, length, depth = tok.shape
+    width = ge.shape[2]
+    rows = depth // size
+    fused = (2 * rows) % 128 == 0
     if not pair:
         flat = jnp.concatenate([lax.psum(flat[:shared], "tensor"), flat[shared:]])
-    rows, width = part.shape[0] // size, part.shape[1]
+        dg, hidden, cot_own = [jnp.zeros((1, 16, depth), BF)] * 3
+    if fused:
+        tok, ge = tok.reshape(seqs * length, depth), ge.reshape(seqs * length, width)
+    else:
+        ge = jnp.einsum("stp,sty->py", tok, ge, preferred_element_type=F32).astype(BF)
+        tok = tok[0, :16]
     sds = jax.ShapeDtypeStruct
     vmem = pl.BlockSpec(memory_space=pltpu.VMEM)
-    blocks = first * second
+    blocks = first * second * PIECES
+    columns = first * max(second - 1, 1) * PIECES
+    lines = 2 * first * PIECES
+    cut = rows // PIECES
+    dma = pltpu.SemaphoreType.DMA
     return pl.pallas_call(
-        functools.partial(reduce_kernel, first, second, pair, shared),
-        in_specs=[vmem, vmem],
-        out_specs=[vmem, vmem],
-        out_shape=[sds((rows, width), F32), sds(flat.shape, F32)],
+        functools.partial(reduce_kernel, first, second, pair, fused, shared),
+        in_specs=[vmem] * 7,
+        out_specs=[vmem] * 3,
+        out_shape=[sds((rows, width), F32), sds(flat.shape, F32), sds(hidden.shape, BF)],
         scratch_shapes=[
-            pltpu.VMEM((blocks, rows, width), BF),
-            pltpu.VMEM((first * max(second - 1, 1), rows, width), BF),
-            pltpu.VMEM((first, rows, width), BF),
+            pltpu.VMEM((depth, width) if fused else (16, 128), BF),
+            pltpu.VMEM((blocks, cut, width), BF),
+            pltpu.VMEM((columns, cut, width), BF),
+            pltpu.VMEM((lines, cut, width), BF),
+            pltpu.VMEM((cut, width), F32),
+            pltpu.VMEM(hidden.shape, BF),
             pltpu.VMEM((shared, flat.shape[1]), F32),
             pltpu.VMEM(flat.shape, F32),
             pltpu.VMEM((second,) + flat.shape, F32),
             pltpu.VMEM((first,) + flat.shape, F32),
             pltpu.VMEM((3,) + flat.shape, F32),
-            pltpu.SemaphoreType.DMA((blocks,)),
-            pltpu.SemaphoreType.DMA((blocks,)),
-            pltpu.SemaphoreType.DMA((first * max(second - 1, 1),)),
-            pltpu.SemaphoreType.DMA((first * max(second - 1, 1),)),
-            pltpu.SemaphoreType.DMA((first,)),
-            pltpu.SemaphoreType.DMA((first,)),
-            pltpu.SemaphoreType.DMA((1 + first + second,)),
-            pltpu.SemaphoreType.DMA((2 + first + second,)),
+            dma((blocks,)), dma((blocks,)), dma((columns,)), dma((columns,)),
+            dma((first * PIECES,)), dma((lines,)), dma((1 + first + second,)), dma((2 + first + second,)), dma((2,)),
         ],
         compiler_params=pltpu.CompilerParams(collective_id=1, has_side_effects=True, vmem_limit_bytes=VMEM_LIMIT),
         name="reduce_all",
-    )(part, flat)
+    )(tok, ge, flat, dg, hidden, cot_own, jnp.broadcast_to(pre_gain[None], (8, depth)))
 
 
 def gather_tokens(own, n, me):
@@ -876,8 +956,7 @@
     ge, dg, gch, gmap, ghead, gpre = mixer_backward(
         pz, raw, aux, cot, mixed, cv, pre, cbc, pbc, st, back, cw, cbw, hp, out_all, weights, normed
     )
-    grad_normed = scatter_sum(part(dg), here, n, me, 1)
-    weight_grad = jnp.einsum("stp,sty->py", normed, ge, preferred_element_type=F32).astype(BF)
+    ge, output = lax.optimization_barrier((ge, output))
 
     def rows_of(*vectors):
         flat = jnp.concatenate([v.reshape(-1) for v in vectors])
@@ -887,18 +966,21 @@
     shared = rows_of(gmap[:5], gpre[0] / pre_gain)
     skip_sums = jnp.sum(gch[5].reshape(heads, HEADDIM), axis=-1)
     flat = jnp.concatenate([shared, rows_of(gch[:5], gch[6], jnp.sum(ghead, axis=-1), skip_sums)])
-    own_rows, flat = reduce_all(weight_grad, flat, shared.shape[0], size, n)
+    own_rows, flat, grad_hidden = reduce_all(
+        normed, ge, flat, shared.shape[0], dg, hidden, grad_out, pre_gain, size, n
+    )
     wide = 2 * inner
     grad_zx_weight = own_rows[:, :wide]
     grad_step_weight = own_rows[:, wide + 2 * STATE :][:, :heads]
     grad_bc_weight = swap_sum(own_rows[:, wide : wide + 2 * STATE], n)
 
-    gain_grad = grad_normed * pre_gain
-    grad_hidden = (
-        grad_out.astype(F32)
-        + inv_rms * gain_grad
-        - hidden_f * inv_rms**3 * jnp.mean(hidden_f * gain_grad, axis=-1, keepdims=True)
-    ).astype(BF)
+    if n != 2:
+        gain_grad = scatter_sum(part(dg), here, n, me, 1) * pre_gain
+        grad_hidden = (
+            grad_out.astype(F32)
+            + inv_rms * gain_grad
+            - hidden_f * inv_rms**3 * jnp.mean(hidden_f * gain_grad, axis=-1, keepdims=True)
+        ).astype(BF)
 
     sums = flat[: shared.shape[0]].reshape(-1)
     shared_map = sums[: 5 * 2 * STATE].reshape(5, 2 * STATE)

time: 267 us -> 237 us (0.89)
  waiting for transfers between devices: 25 us -> 7.37 us
  matrix products: 12.2 us -> 5.42 us
  Pallas kernels: 168 us -> 165 us
    ppermute x2, waiting for transfers between devices: 21.4 us -> 2.65 us  [swap_sum(): return value + lax.ppermute(value, 'tensor', [(0, 1), (1, 0)])]
    pallas_call x1, Pallas kernels: 55.7 us -> 46.7 us  [reduce_all(): pl.pallas_call(functools.partial(reduce_kernel, first, second, pair, fuse...]
    unnamed x63 -> x46, local copies, waits for them, and re-layouts: 13.4 us -> 5.03 us
    dot_general x1 -> x0, matrix products: 8.35 us -> none  [body(): jnp.einsum('stp,sty->py', normed, ge, preferred_element_type=F32).astype(BF)]
    pallas_call x1, Pallas kernels: 3.45 us -> 7.05 us  [out_project(): pl.pallas_call(out_kernel, grid=(seqs, length // size), in_specs=[token(i...]
  transfers between devices with their start and end apart: 7 -> 6, of which waited for: 3 -> 2; matrix products, arithmetic and copies ran while one was open for 11% -> 12% of each run, Pallas kernels for 47% -> 51%
where the time goes in v3:
time: 237 us; the launch traced here: 236 us
  Pallas kernels  165 us (70%)
  local copies, waits for them, and re-layouts  24.4 us (10%)
  between operations  14.4 us (6%)
  other arithmetic  13.7 us (6%)
  waiting for transfers between devices  7.37 us (3%)
  matrix products  5.42 us (2%)
  starting transfers between devices  5.13 us (2%)
    pallas_call x1, Pallas kernels, reduce_all(): pl.pallas_call(functools.partial(reduce_kernel, first, second, pair, fuse...  46.7 us
    pallas_call x1, Pallas kernels, mixer_backward(): pl.pallas_call(functools.partial(backward_kernel, heads), grid=(seqs, len...  44.9 us
    pallas_call x1, Pallas kernels, gather_all(): pl.pallas_call(functools.partial(gather_kernel, first, second, pair, arra...  38.8 us
    pallas_call x1, Pallas kernels, mixer_forward(): pl.pallas_call(functools.partial(forward_kernel, heads), grid=(seqs, leng...  27.8 us
    pallas_call x1, Pallas kernels, out_project(): pl.pallas_call(out_kernel, grid=(seqs, length // size), in_specs=[token(i...  7.05 us
    dot_general x1, matrix products, body(): jnp.einsum('str,stc->rc', cot_scaled, gn, preferred_element_type=F32)  5.42 us
    unnamed x46, local copies, waits for them, and re-layouts  5.03 us
  transfers between devices with their start and end apart: 6, of which 2 were waited for; matrix products, arithmetic and copies ran while one was open for 12% of the time, Pallas kernels for 51%

profile of v3, /device:TPU:0, one launch (start us, length us, event | category | flops | bytes accessed | tf_op | source)
XLA Modules:
  0.0 235.7 jit_solution(2760102504172394603)
XLA Ops:
  7.2 1.5 fusion
  8.8 0.8 copy.32
  9.7 2.6 %fusion.2.refs_1_ = bf16[1,512,1024]{2,1,0:T(8,128)(2,1)} fusion(bf16[1,512,1024]{2,1,0:T(8,128)(2,1)} %hidden_ref.1, f32[1024]{0:T(1024)} %param.18, f32[512]{0:T(512)S(1)} %add_rsqrt_fusion), kind=kLoop, calls=%fused_computation.6 | loop fusion | flops 2097152 | bytes 2103296 | tf_op jit(solution)/shard_map/convert_element_type | solution.py:925
  12.3 0.8 concatenate.18.refs_0_
  13.1 38.8 %gather_all.1 = (bf16[1024,2432]{1,0:T(8,128)(2,1)}, bf16[1,1024,1024]{2,1,0:T(8,128)(2,1)}) custom-call(bf16[64,2432]{1,0:T(8,128)(2,1)} %concatenate.18.refs_0_, bf16[1,512,1024]{2,1,0:T(8,128)(2,1)} %fusion.2.refs_1_), custom_call_target="tpu_custom_call" | custom-call | tf_op jit(solution)/shard_map/gather_all/pallas_call | solution.py:647
  52.0 1.6 collective-permute-start
  53.7 0.1 slice.128
  53.7 0.1 copy.35
  53.8 0.1 broadcast_in_dim.42
  53.9 0.1 broadcast_in_dim_reshape.3
  54.0 0.1 pad.57.clone
  54.1 0.6 concatenate.19.cw_ref
  54.7 0.1 slice_bitcast_fusion.2
  54.8 0.1 eq.49
  54.9 0.1 eq.52
  54.9 0.1 fusion.24
  55.1 1.3 stack.92.aux_ref
  56.4 0.7 maximum_maximum_fusion.cbw_ref
  57.1 0.7 broadcast_in_dim.47.hp_ref
  57.8 27.8 %mixer_forward.1 = (bf16[1,1024,2304]{2,1,0:T(8,128)(2,1)}, f32[1,16,1024]{2,1,0:T(8,128)}, bf16[1,1024,1024]{2,1,0:T(8,128)(2,1)}, bf16[1,1024,1024]{2,1,0:T(8,...) custom-call(bf16[1,1024,1024]{2,1,0:T(8,128)(2,1)} %get-tuple-elemen, ...), custom_call_target="tpu_custom_call" | custom-call | tf_op jit(solution)/shard_map/mixer_forward/pallas_call | solution.py:388
  85.5 0.3 broadcast_in_dim.48
  85.8 0.1 constant_dynamic-update-slice_fusion.1
  85.9 1.3 constant_dynamic-update-slice_fusion.cot_ref
  87.3 4.7 %all-gather.2.cloned.1.call-done.out_ref = bf16[1024,1024]{1,0:T(8,128)(2,1)} async-done(((bf16[64,1024]{1,0:T(8,128)(2,1)}), bf16[1024,1024]{1,0:T(8,128)(2,1)}) %all-gather.2.cloned.1.call-update) | async-done | bytes 2097168 | tf_op jit(solution)/shard_map/all_gather | solution.py:931
  92.0 7.0 %out_project.1 = (bf16[1,1024,1024]{2,1,0:T(8,128)(2,1)}, f32[1,8,1024]{2,1,0:T(8,128)}) custom-call(bf16[1,1024,1024]{2,1,0:T(8,128)(2,1)} %get-tuple-element.57.gn_ref, bf16[1,1024,1024]{2,1,0:T(8,128)(2,1)} %copy-done, bf16[1024,1024]{1,0:T(8,128)(2,1)} %all-gather.2.cloned.1.call-done.out_ref, f32[1,8,1024]{2,1,0:T(8,128)} %get-tuple-element.59.stat_ref), custom_call_target="tpu_custom_call" | custom-call | tf_op jit(solution)/shard_map/out_project/pallas_call | solution.py:470
  99.0 1.5 collective-permute-start.1
  100.5 2.6 %collective-permute-done.1 = f32[1,8,1024]{2,1,0:T(8,128)S(1)} collective-permute-done((f32[1,8,1024]{2,1,0:T(8,128)}, f32[1,8,1024]{2,1,0:T(8,128)S(1)}, u32[]{:S(2)}, u32[]{:S(2)}) %collective-permute-start.1) | collective-permute-done | bytes 32800 | tf_op jit(solution)/shard_map/ppermute | solution.py:908
  103.2 0.8 add.79
  104.0 5.4 %fusion.9 = bf16[1024,1024]{1,0:T(8,128)(2,1)} fusion(bf16[1,1024,1024]{2,1,0:T(8,128)(2,1)S(1)} %copy-done.3, bf16[1,1024,1024]{2,1,0:T(8,128)(2,1)} %copy-done, f32[1024]{0:T(1024)S(1)} %bitcast.72), kind=kOutput, calls=%fused_computation.12 | convolution fusion | flops 2151677952 | bytes 6295552 | tf_op jit(solution)/shard_map/str,stc->rc/dot_general | solution.py:953
  109.4 0.1 pad.51.clone
  109.5 0.7 pad_maximum_fusion.1.stat_ref
  110.2 0.8 copy-done.4
  111.0 1.0 constant_dynamic-slice_fusion
  112.0 1.5 collective-permute-start.2
  113.5 44.9 %mixer_backward.1 = (bf16[1,1024,2432]{2,1,0:T(8,128)(2,1)}, bf16[1,1024,1024]{2,1,0:T(8,128)(2,1)}, f32[8,1024]{1,0:T(8,128)}, f32[8,256]{1,0:T(8,128)}, f32[2,16,128]{2,1,0:T(8,128)}, /*index=5*/f32[8,1024]{1,0:T(8,128)}) custom-call(bf16[1,1024,2304]{2,1,0:T(8,128)(2,1)} %get-tuple-element.48.pz_ref, f32[1,16,1024]{2,1,0:T(8,128)} %get-tuple-element.49.raw_ref, ...), custom_call_target="tpu_custom_call" | custom-call | tf_op jit(solution)/shard_map/mixer_backward/pallas_call | solution.py:423
  158.4 0.7 reshape.192
  159.1 0.8 reduce_sum.28
  159.9 0.1 reshape.195
  160.0 0.8 slice.138
  160.8 0.9 slice_reduce_fusion.1
  161.7 0.1 reshape_squeeze.3
  161.7 0.1 reduce_sum.29
  161.9 0.8 reshape.194
  162.6 0.1 concatenate.22
  162.8 0.6 pad_maximum_fusion.flat_ref
  163.4 2.7 %fusion.3 = bf16[1,512,1024]{2,1,0:T(8,128)(2,1)} fusion(bf16[1,512,1024]{2,1,0:T(8,128)(2,1)S(1)} %copy-done.1, bf16[1,512,1024]{2,1,0:T(8,128)(2,1)} %collective-permute-done.2, bf16[1,1024,1024]{2,1,0:T(8,128)(2,1)S(1)} %copy-done.4, s32[]{:T(128)S(6)} %select_n.4, f32[512]{0:T(512)S(1)} %bitcast.78), kind=kLoop, calls=%fused_computation.7 | loop fusion | flops 3670016 | bytes 4196356 | tf_op jit(solution)/shard_map/convert_element_type | solution.py:951
  166.1 0.6 broadcast_in_dim.49.gain_ref
  166.7 46.7 %reduce_all.1 = (f32[64,2432]{1,0:T(8,128)}, f32[16,1024]{1,0:T(8,128)}, bf16[1,512,1024]{2,1,0:T(8,128)(2,1)}) custom-call(bf16[1024,1024]{1,0:T(8,128)(2,1)} %bitcast.65, bf16[1024,2432]{1,0:T(8,128)(2,1)} %bitcast.66, f32[16,1024]{1,0:T(8,128)} %pad_maximum_fusion.flat_ref, bf16[1,1024,1024]{2,1,0:T(8,128)(2,1)} %get-tuple-element.71.dg_ref, ...), custom_call_target="tpu_custom_call" | custom-call | tf_op jit(solution)/shard_map/reduce_all/pallas_call | solution.py:862
  213.4 0.9 slice_bitcast_fusion.1
  214.3 0.8 slice.145
  215.1 0.5 collective-permute-start.3
  215.6 1.4 fusion.26
  217.0 0.8 slice_bitcast_fusion
  217.8 0.6 fusion.27
  218.4 1.4 slice.147
  219.8 0.6 slice.161
  220.3 0.6 slice.160
  220.9 0.8 slice.146
  221.7 1.9 slice.144
  223.6 0.6 slice.150
  224.2 0.7 copy.34
  224.8 1.5 slice_add_fusion
  226.3 1.6 convert_bitcast_fusion
  227.9 1.0 copy.45
  (64 shorter events, 0.4 us)
Async XLA Ops:
  7.2 5.1 %copy-start.9 = (bf16[64,256]{1,0:T(8,128)(2,1)S(1)}, bf16[64,256]{1,0:T(8,128)(2,1)}, u32[]{:S(2)}) copy-start(bf16[64,256]{1,0:T(8,128)(2,1)} %param.20) | copy-start | bytes 98308
  7.2 5.1 %copy-start.6 = (bf16[64,2048]{1,0:T(8,128)(2,1)S(1)}, bf16[64,2048]{1,0:T(8,128)(2,1)}, u32[]{:S(2)}) copy-start(bf16[64,2048]{1,0:T(8,128)(2,1)} %param.19) | copy-start | bytes 786436
  7.2 84.8 %all-gather.2.cloned.1.call-start = ((), (), s32[]{:S(2)}) async-start(), calls=%async_computation.1 | async-start | bytes 2228224 | tf_op jit(solution)/shard_map/all_gather | solution.py:931
  9.6 42.4 %copy-start.2 = (bf16[1,512,1024]{2,1,0:T(8,128)(2,1)S(1)}, bf16[1,512,1024]{2,1,0:T(8,128)(2,1)}, u32[]{:S(2)}) copy-start(bf16[1,512,1024]{2,1,0:T(8,128)(2,1)} %cot_ref.1) | copy-start | bytes 3145732
  9.6 44.1 %copy-start.8 = (s32[1,1024]{1,0:T(1,128)S(1)}, s32[1,1024]{1,0:T(1,128)}, u32[]{:S(2)}) copy-start(s32[1,1024]{1,0:T(1,128)} %param.31) | copy-start | bytes 12292
  9.6 44.0 %copy-start.14 = (s32[1,1024]{1,0:T(1,128)S(1)}, s32[1,1024]{1,0:T(1,128)}, u32[]{:S(2)}) copy-start(s32[1,1024]{1,0:T(1,128)} %param.32) | copy-start | bytes 12292
  9.6 44.2 %copy-start.16 = (f32[16]{0:T(128)S(1)}, f32[16]{0:T(128)}, u32[]{:S(2)}) copy-start(f32[16]{0:T(128)} %param.28) | copy-start | bytes 196
  9.6 44.4 %copy-start.10 = (f32[4,1024]{1,0:T(4,128)S(1)}, f32[4,1024]{1,0:T(4,128)}, u32[]{:S(2)}) copy-start(f32[4,1024]{1,0:T(4,128)} %param.22) | copy-start | bytes 49156
  9.6 44.4 %copy-start.11 = (f32[1024]{0:T(1024)S(1)}, f32[1024]{0:T(1024)}, u32[]{:S(2)}) copy-start(f32[1024]{0:T(1024)} %param.23) | copy-start | bytes 12292
  9.6 44.4 %copy-start.12 = (f32[1024]{0:T(1024)S(1)}, f32[1024]{0:T(1024)}, u32[]{:S(2)}) copy-start(f32[1024]{0:T(1024)} %param.29) | copy-start | bytes 12292
  9.7 46.7 %copy-start.18 = (f32[16]{0:T(128)S(1)}, f32[16]{0:T(128)}, u32[]{:S(2)}) copy-start(f32[16]{0:T(128)} %param.27) | copy-start | bytes 196
  9.7 46.7 %copy-start.17 = (f32[16]{0:T(128)S(1)}, f32[16]{0:T(128)}, u32[]{:S(2)}) copy-start(f32[16]{0:T(128)} %param.26) | copy-start | bytes 196
  9.7 46.8 %copy-start.13 = (f32[4,256]{1,0:T(4,128)S(1)}, f32[4,256]{1,0:T(4,128)}, u32[]{:S(2)}) copy-start(f32[4,256]{1,0:T(4,128)} %param.24) | copy-start | bytes 12292
  9.7 46.7 %copy-start.15 = (f32[256]{0:T(256)S(1)}, f32[256]{0:T(256)}, u32[]{:S(2)}) copy-start(f32[256]{0:T(256)} %param.25) | copy-start | bytes 3076
  52.0 174.3 %reduce-scatter.2.cloned.1.call-start = ((), (), s32[]{:S(2)}) async-start(), calls=%async_computation.2 | async-start | bytes 2228224 | tf_op jit(solution)/shard_map/reduce_scatter | solution.py:954
  52.0 33.9 %collective-permute-start = (bf16[1,512,1024]{2,1,0:T(8,128)(2,1)S(1)}, bf16[1,512,1024]{2,1,0:T(8,128)(2,1)}, u32[]{:S(2)}, u32[]{:S(2)}) collective-permute-start(bf16[1,512,1024]{2,1,0:T(8,128)(2,1)S(1)} %copy-done.2), channel_id=1, source_target_pairs={{0,1},{1,0},{2,3},{3,2},{4,5},{5,4},{6,7},{7,6},{8,9},{9,8},{10,11... | collective-permute-start | bytes 3145736 | tf_op jit(solution)/shard_map/ppermute | solution.py:890
  87.3 4.7 %copy-start = (bf16[1,1024,1024]{2,1,0:T(8,128)(2,1)}, bf16[1,1024,1024]{2,1,0:T(8,128)(2,1)S(1)}, u32[]{:S(2)}) copy-start(bf16[1,1024,1024]{2,1,0:T(8,128)(2,1)S(1)} %constant_dynamic-update-slice_fusion.cot_ref) | copy-start | bytes 6291460
  92.0 12.0 %copy-start.3 = (bf16[1,1024,1024]{2,1,0:T(8,128)(2,1)S(1)}, bf16[1,1024,1024]{2,1,0:T(8,128)(2,1)}, u32[]{:S(2)}) copy-start(bf16[1,1024,1024]{2,1,0:T(8,128)(2,1)} %get-tuple-element.57.gn_ref) | copy-start | bytes 6291460
  99.0 4.1 %collective-permute-start.1 = (f32[1,8,1024]{2,1,0:T(8,128)}, f32[1,8,1024]{2,1,0:T(8,128)S(1)}, u32[]{:S(2)}, u32[]{:S(2)}) collective-permute-start(f32[1,8,1024]{2,1,0:T(8,128)} %get-tuple-element.61), channel_id=1, source_target_pairs={{0,1},{1,0},{2,3},{3,2},{4,5},{5,4},{6,7},{7,6},{8,9},{9,8},{10,11... | collective-permute-start | bytes 98312 | tf_op jit(solution)/shard_map/ppermute | solution.py:908
  109.4 1.6 copy-start.4
  112.0 51.4 %collective-permute-start.2 = (bf16[1,512,1024]{2,1,0:T(8,128)(2,1)}, bf16[1,512,1024]{2,1,0:T(8,128)(2,1)}, u32[]{:S(2)}, u32[]{:S(2)}) collective-permute-start(bf16[1,512,1024]{2,1,0:T(8,128)(2,1)} %constant_dynamic-slice_fusion), channel_id=1, source_target_pairs={{0,1},{1,0},{2,3},{3,2},{4,5},{5,4},{6,7},{7,6},{8,9},{9,8},{10,11... | collective-permute-start | bytes 3145736 | tf_op jit(solution)/shard_map/ppermute | solution.py:901
  113.5 47.3 %copy-start.7 = (f32[1024]{0:T(1024)S(1)}, f32[1024]{0:T(1024)}, u32[]{:S(2)}) copy-start(f32[1024]{0:T(1024)} %param.18) | copy-start | bytes 12292
  113.5 49.9 %copy-start.1 = (bf16[1,512,1024]{2,1,0:T(8,128)(2,1)S(1)}, bf16[1,512,1024]{2,1,0:T(8,128)(2,1)}, u32[]{:S(2)}) copy-start(bf16[1,512,1024]{2,1,0:T(8,128)(2,1)} %hidden_ref.1) | copy-start | bytes 3145732
  213.4 14.5 %copy-start.5 = (bf16[1,512,1024]{2,1,0:T(8,128)(2,1)S(1)}, bf16[1,512,1024]{2,1,0:T(8,128)(2,1)}, u32[]{:S(2)}) copy-start(bf16[1,512,1024]{2,1,0:T(8,128)(2,1)} %get-tuple-element.126) | copy-start | bytes 3145732
  215.1 9.7 %collective-permute-start.3 = (f32[64,256]{1,0:T(8,128)S(1)}, f32[64,256]{1,0:T(8,128)S(1)}, u32[]{:S(2)}, u32[]{:S(2)}) collective-permute-start(f32[64,256]{1,0:T(8,128)S(1)} %slice.145), channel_id=1, source_target_pairs={{0,1},{1,0},{2,3},{3,2},{4,5},{5,4},{6,7},{7,6},{8,9},{9,8},{10,11... | collective-permute-start | bytes 196616 | tf_op jit(solution)/shard_map/ppermute | solution.py:908
Sparse Core Ops, SparseCore 0:
  52.1 39.8 all-gather.1
  109.5 60.3 reduce-scatter.1

commit v4 on v2

v4 whole, which is shorter than its diff:
```python
import collections
import functools
import jax
import jax.numpy as jnp
from jax import lax
from jax.experimental import pallas as pl
from jax.experimental.pallas import tpu as pltpu
from jax.sharding import PartitionSpec as P

HEADDIM = 64
STATE = 128
CHUNK = 128
TAPS = 4
HALO = 8
AUX = 16
LOG2E = 1.4426950408889634
FAR = -1e30
BLOCK = 256
VMEM_LIMIT = 58 * 1024 * 1024
MESH = pl.DeviceIdType.MESH
PIECES = 2
epsilon = 1e-05
BF = jnp.bfloat16
F32 = jnp.float32


def sigmoid(v):
    return 0.5 * jnp.tanh(0.5 * v) + 0.5


def split3(v):
    a = v.astype(BF)
    r = v - a.astype(F32)
    b = r.astype(BF)
    c = (r - b.astype(F32)).astype(BF)
    return a, b, c


def dot_nn(a, b):
    return lax.dot_general(a, b, (((1,), (0,)), ((), ())), preferred_element_type=F32)


def dot_nt(a, b):
    return lax.dot_general(a, b, (((1,), (1,)), ((), ())), preferred_element_type=F32)


def exact_dot(v, ones):
    rows = v.shape[0]
    out = dot_nn(jnp.concatenate(split3(v), axis=0), ones)
    return out[:rows] + out[rows : 2 * rows] + out[2 * rows :]


def iota2(shape, dim):
    return lax.broadcasted_iota(jnp.int32, shape, dim)


def pieces(raw, bias, rate, aux, tri):
    pad = aux[1:2]
    pre = raw + bias
    soft = jnp.maximum(pre, 0.0) + jnp.log1p(jnp.exp(-jnp.abs(pre)))
    dt = soft * pad
    cum = exact_dot(dt * rate, tri) * LOG2E
    carried = jnp.exp2(cum) * aux[5:6]
    toward = jnp.exp2(cum[:, CHUNK - 1 : CHUNK] - cum) * aux[6:7]
    return dt, cum, carried, toward


def expander(heads, inner, place):
    row = lax.rem(iota2((256, inner), 0), 128)
    head = lax.div(iota2((256, inner), 1), HEADDIM)
    return jnp.where(row == head + place, 1.0, 0.0).astype(BF)


def collector(inner, place):
    head = lax.div(iota2((inner, 128), 0), HEADDIM)
    lane = iota2((inner, 128), 1)
    return jnp.where(lane == head + place, 1.0, 0.0).astype(BF)


def hi_lo(cols):
    hi = cols.astype(BF)
    return jnp.concatenate([hi, (cols - hi.astype(F32)).astype(BF)], axis=1)


def compact(rows_list):
    used = sum(r.shape[0] for r in rows_list)
    if used < 128:
        rows_list = list(rows_list) + [jnp.zeros((128 - used, CHUNK), F32)]
    return jnp.concatenate(rows_list, axis=0).T


def split_pair(first, second, low):
    gate = jnp.where(low, first, pltpu.roll(second, HEADDIM, 1))
    value = jnp.where(low, pltpu.roll(first, HEADDIM, 1), second)
    return gate, value


Place = collections.namedtuple("Place", ("first", "second", "pair", "fused", "steps", "length"))


def factors(size):
    first = 4 if size % 8 == 0 else 1
    return first, size // (2 * first)


class Spot:
    def __init__(self, place):
        self.first, self.second = place.first, place.second
        self.index = lax.axis_index("dp")
        self.me = lax.axis_index("tensor")
        self.a = lax.div(self.index, 2 * self.second)
        self.b = lax.rem(lax.div(self.index, 2), self.second)
        self.c = lax.rem(self.index, 2)

    def at(self, i, j, k):
        return (i * self.second + j) * 2 + k

    def around(self, i):
        return lax.rem(self.a + i, self.first)

    def aside(self, j):
        return lax.rem(self.b + j, self.second)

    @property
    def sibling(self):
        return self.at(self.a, self.b, 1 - self.c)

    def greet(self, pair):
        barrier = pltpu.get_barrier_semaphore()
        peers = [(self.sibling, self.me)]
        peers += [(self.at(self.a, self.aside(j), self.c), self.me) for j in range(1, self.second)]
        peers += [(self.at(self.around(i), self.b, self.c), self.me) for i in range(1, self.first)]
        if pair:
            peers.append((self.index, 1 - self.me))
        for peer in peers:
            pl.semaphore_signal(barrier, inc=1, device_id=peer, device_id_type=MESH)
        pl.semaphore_wait(barrier, len(peers))

    def copy(self, src, dst, ss, rs, target, tensor=None):
        return pltpu.make_async_remote_copy(
            src_ref=src, dst_ref=dst, send_sem=ss, recv_sem=rs,
            device_id=(target, self.me if tensor is None else tensor), device_id_type=MESH,
        )

    def arrived(self, dst, rs):
        self.copy(dst, dst, rs, rs, self.sibling).wait_recv()


def when(valid, run):
    def quiet():
        run()

    quiet() if valid is None else pl.when(valid)(quiet)


def gather_sites(first, second):
    return (2 + second) + (first - 1) * 2 * (1 + second) + (2 * first - 1) * (second - 1)


class LineGather:
    def __init__(self, spot, arrays, send_sem, recv_sem, local_sem):
        self.spot, self.arrays = spot, arrays
        self.send_sem, self.recv_sem, self.local_sem = send_sem, recv_sem, local_sem
        self.sites = []

    def rows(self, which, shard):
        own, full = self.arrays[which]
        rows = own.shape[0]
        return full.at[pl.ds(pl.multiple_of(shard * rows, rows), rows)]

    def copies(self, site, shard, target, mine=False):
        return [
            self.spot.copy(
                own if mine else self.rows(w, shard), self.rows(w, shard),
                self.send_sem.at[w, site], self.recv_sem.at[w, shard], target,
            )
            for w, (own, full) in enumerate(self.arrays)
        ]

    def send(self, valid, shard, target, mine=False):
        site = len(self.sites)
        self.sites.append((valid, shard, target, mine))
        when(valid and valid(), lambda: [copy.start() for copy in self.copies(site, shard(), target(), mine)])

    def arrive(self, valid, shard):
        def wait():
            for w in range(len(self.arrays)):
                self.spot.arrived(self.rows(w, shard), self.recv_sem.at[w, shard])

        when(valid, wait)

    def local(self):
        return [
            pltpu.make_async_copy(own, self.rows(w, self.spot.index), self.local_sem.at[w])
            for w, (own, full) in enumerate(self.arrays)
        ]

    def begin(self):
        s = self.spot
        self.send(lambda: s.a < s.first - 1, lambda: s.index, lambda: s.at(s.a + 1, s.b, s.c), True)
        self.send(lambda: s.a > 0, lambda: s.index, lambda: s.at(s.a - 1, s.b, s.c), True)
        for j in range(1, s.second):
            self.send(None, lambda: s.index, lambda j=j: s.at(s.a, s.aside(j), s.c), True)
        self.send(None, lambda: s.index, lambda: s.sibling, True)
        for copy in self.local():
            copy.start()

    def sides(self, hop):
        s = self.spot
        if hop == 0:
            return [(None, lambda: s.a, None, None)]
        return [
            (lambda: s.a - hop >= 0, lambda: s.a - hop, lambda: s.a < s.first - 1, lambda: s.at(s.a + 1, s.b, s.c)),
            (lambda: s.a + hop < s.first, lambda: s.a + hop, lambda: s.a > 0, lambda: s.at(s.a - 1, s.b, s.c)),
        ]

    def along(self, hop):
        s = self.spot
        for valid, origin, onward, target in self.sides(hop):
            shard = lambda origin=origin: s.at(origin(), s.b, s.c)
            self.arrive(valid(), shard())
            self.send(lambda valid=valid, onward=onward: valid() & onward(), shard, target)
            for j in range(1, s.second):
                self.send(valid, shard, lambda j=j: s.at(s.a, s.aside(j), s.c))
            self.send(valid, shard, lambda: s.sibling)

    def across(self, hop):
        s = self.spot
        for j in range(1, s.second):
            for valid, origin, onward, target in self.sides(hop):
                shard = lambda origin=origin, j=j: s.at(origin(), s.aside(j), s.c)
                self.arrive(valid and valid(), shard())
                self.send(valid, shard, lambda: s.sibling)

    def finish(self):
        s = self.spot
        for i in range(s.first):
            for j in range(s.second):
                self.arrive(None, s.at(i, j, 1 - s.c))
        for site, (valid, shard, target, mine) in enumerate(self.sites):
            when(
                valid and valid(),
                lambda site=site, shard=shard, target=target, mine=mine: [
                    copy.wait_send() for copy in self.copies(site, shard(), target(), mine)
                ],
            )
        for copy in self.local():
            copy.wait()


class TokenSwap:
    def __init__(self, spot, own, full, sem):
        self.spot, self.own, self.full, self.sem = spot, own, full, sem

    def target(self):
        here = self.own.shape[1]
        return self.full.at[:, pl.ds(pl.multiple_of(self.spot.me * here, here), here)]

    def remote(self):
        s = self.spot
        return s.copy(self.own, self.target(), self.sem.at[0], self.sem.at[1], s.index, 1 - s.me)

    def local(self):
        return pltpu.make_async_copy(self.own, self.target(), self.sem.at[2])

    def begin(self):
        self.remote().start()
        self.local().start()

    def finish(self):
        self.remote().wait()
        self.local().wait()


class HalfSwap:
    def __init__(self, spot, whole, away, sem):
        self.spot, self.whole, self.away, self.sem = spot, whole, away, sem

    def remote(self):
        s = self.spot
        here = self.away.shape[1]
        rows = self.whole.at[:, pl.ds(pl.multiple_of((1 - s.me) * here, here), here)]
        return s.copy(rows, self.away, self.sem.at[0], self.sem.at[1], s.index, 1 - s.me)

    def begin(self):
        self.remote().start()

    def finish(self):
        self.remote().wait()


class LineScatter:
    def __init__(
        self, spot, part, core_buf, x_buf, z_buf, out, core_send, core_recv, x_send, x_recv, z_send, z_recv, cuts=1
    ):
        self.spot, self.part, self.out, self.cuts = spot, part, out, cuts
        self.core_buf, self.x_buf, self.z_buf = core_buf, x_buf, z_buf
        self.sems = (core_send, core_recv, x_send, x_recv, z_send, z_recv)
        self.rows = out.shape[0] // cuts
        self.copies = []
        a = spot.a
        if spot.first == 4:
            near = jnp.minimum(a, 3 - a)
            self.order = [jnp.where(a < 2, d, 3 - d) for d in (3 + 0 * a, 2 - 2 * near, 1 + near)] + [a]
        else:
            self.order = [a]

    def block(self, i, j, k, q):
        rows = self.rows
        return self.part.at[pl.ds(pl.multiple_of((self.spot.at(i, j, k) * self.cuts + q) * rows, rows), rows)]

    def slot(self, i, j, q):
        return (i * self.spot.second + j) * self.cuts + q

    def start(self, make):
        make().start()
        self.copies.append(make)

    def give(self, n, j):
        s, i = self.spot, self.order[n]
        for q in range(self.cuts):

            def make(q=q):
                t = self.slot(i, s.aside(j), q)
                return s.copy(
                    self.block(i, s.aside(j), 1 - s.c, q), self.core_buf.at[t], self.sems[0].at[t],
                    self.sems[1].at[t], s.sibling,
                )

            self.start(make)

    def terms(self, n, j):
        rows = 2 * self.rows * self.cuts
        first_row = self.spot.at(self.order[n], self.spot.aside(j), 0) * self.rows * self.cuts
        return pl.ds(pl.multiple_of(first_row, rows), rows)

    def cross_over(self, n, j):
        s, i = self.spot, self.order[n]
        for q in range(self.cuts):
            t = self.slot(i, s.aside(j), q)
            s.arrived(self.core_buf.at[t], self.sems[1].at[t])
            own = self.block(i, s.aside(j), s.c, q)[...].astype(F32)
            self.core_buf[t] = (own + self.core_buf[t].astype(F32)).astype(BF)

            def make(q=q):
                t = self.slot(i, s.aside(j), q)
                there = (i * (s.second - 1) + s.second - j - 1) * self.cuts + q
                here = (i * (s.second - 1) + j - 1) * self.cuts + q
                return s.copy(
                    self.core_buf.at[t], self.x_buf.at[there], self.sems[2].at[here], self.sems[3].at[there],
                    s.at(s.a, s.aside(j), s.c),
                )

            self.start(make)

    def column_sum(self, n, q):
        s, i = self.spot, self.order[n]
        t = self.slot(i, s.b, q)
        s.arrived(self.core_buf.at[t], self.sems[1].at[t])
        total = self.block(i, s.b, s.c, q)[...].astype(F32) + self.core_buf[t].astype(F32)
        for j in range(1, s.second):
            u = (i * (s.second - 1) + j - 1) * self.cuts + q
            s.arrived(self.x_buf.at[u], self.sems[3].at[u])
            total = total + self.x_buf[u].astype(F32)
        return total

    def produce(self, make_terms, far):
        s = self.spot
        for j in range(1, s.second) if far else [0]:
            for n in range(s.first):
                make_terms(self.terms(n, j))
                self.give(n, j)

    def cross(self):
        for j in range(1, self.spot.second):
            for n in range(self.spot.first):
                self.cross_over(n, j)

    def along(self):
        s = self.spot
        for n in range(s.first):
            for q in range(self.cuts):
                total = self.column_sum(n, q)
                if n == s.first - 1:
                    self.out[q * self.rows : (q + 1) * self.rows] = total
                    continue
                self.core_buf[self.slot(self.order[n], s.b, q)] = total.astype(BF)

                def make(n=n, q=q):
                    z = s.a * self.cuts + q
                    return s.copy(
                        self.core_buf.at[self.slot(self.order[n], s.b, q)], self.z_buf.at[z],
                        self.sems[4].at[n * self.cuts + q], self.sems[5].at[z], s.at(self.order[n], s.b, s.c),
                    )

                self.start(make)

    def chain(self, acc):
        s = self.spot
        for n in range(s.first):
            for q in range(self.cuts):
                i = self.order[n]
                total = self.column_sum(n, q)
                if n == s.first - 1:
                    self.out[q * self.rows : (q + 1) * self.rows] = total
                    continue
                down = jnp.where(i > s.a, 0, 1)
                z = (down * s.first + i) * self.cuts + q
                acc[...] = total

                @pl.when(jnp.where(i > s.a, s.a, s.first - 1 - s.a) > 0)
                def _(z=z):
                    s.arrived(self.z_buf.at[z], self.sems[5].at[z])
                    acc[...] = acc[...] + self.z_buf[z].astype(F32)

                self.core_buf[self.slot(i, s.b, q)] = acc[...].astype(BF)

                def make(n=n, q=q, i=i, down=down, z=z):
                    return s.copy(
                        self.core_buf.at[self.slot(i, s.b, q)], self.z_buf.at[z],
                        self.sems[4].at[n * self.cuts + q], self.sems[5].at[z], s.at(s.a + 1 - 2 * down, s.b, s.c),
                    )

                self.start(make)

    def finish_chain(self):
        s = self.spot
        for q in range(self.cuts):
            cut = slice(q * self.rows, (q + 1) * self.rows)
            for down, there in ((0, s.a), (1, s.first - 1 - s.a)):
                z = (down * s.first + s.a) * self.cuts + q

                @pl.when(there > 0)
                def _(z=z, cut=cut):
                    s.arrived(self.z_buf.at[z], self.sems[5].at[z])
                    self.out[cut] = self.out[cut] + self.z_buf[z].astype(F32)

    def wait_sends(self):
        for make in self.copies:
            make().wait_send()

    def finish(self):
        s = self.spot
        for i in range(1, s.first):
            for q in range(self.cuts):
                z = s.around(i) * self.cuts + q
                s.arrived(self.z_buf.at[z], self.sems[5].at[z])
                cut = slice(q * self.rows, (q + 1) * self.rows)
                self.out[cut] = self.out[cut] + self.z_buf[z].astype(F32)
        self.wait_sends()


def forward_kernel(
    place, heads, tok_ref, w_ref, aux_ref, cw_ref, cbw_ref, hp_ref, cot_own, out_own,
    pz_ref, raw_ref, mixed_ref, gated_ref, cv_ref, pre_ref, cbc_ref, pbc_ref, st_ref, stat_ref, out_all, cot_full,
    state, ubuf, bbuf, vd, yint, expand, tri_ref, send_sem, recv_sem, local_sem, cot_sem,
):
    inner = heads * HEADDIM
    pairs = heads // 2
    wide = 2 * inner
    now = pl.program_id(0) * pl.num_programs(1) + pl.program_id(1)
    last = place.steps - 1
    first = now == 0
    spot = Spot(place)
    gather = LineGather(spot, [(out_own, out_all)], send_sem, recv_sem, local_sem)
    swap = TokenSwap(spot, cot_own, cot_full, cot_sem) if place.pair else None

    @pl.when(first)
    def _():
        spot.greet(place.pair)
        gather.begin()
        if swap:
            swap.begin()

    for hop in range(1, place.first):

        @pl.when(now == min(hop, last))
        def _(hop=hop):
            gather.along(hop)
            gather.across(hop - 1)

    @pl.when(first)
    def _():
        for i, place in enumerate((AUX + heads, AUX + 2 * heads, AUX + 3 * heads)):
            expand[i] = expander(heads, inner, place)
        tri_ref[...] = jnp.where(iota2((CHUNK, CHUNK), 0) <= iota2((CHUNK, CHUNK), 1), 1.0, 0.0).astype(BF)

    @pl.when(pl.program_id(1) == 0)
    def _():
        state[...] = jnp.zeros_like(state)
        ubuf[0:HALO] = jnp.zeros((HALO, inner), F32)
        bbuf[0:HALO] = jnp.zeros((HALO, 2 * STATE), F32)

    tok = tok_ref[0]
    side = dot_nn(tok, w_ref[:, wide:])
    raw_ref[0] = side[:, 2 * STATE :].T[0:heads]
    pz_ref[0, :, wide:] = side[:, : 2 * STATE].astype(BF)
    for p in range(pairs):
        pz_ref[0, :, 256 * p : 256 * p + 256] = dot_nn(tok, w_ref[:, 256 * p : 256 * p + 256]).astype(BF)

    def chunk_step(step, carry):
        here = pl.ds(pl.multiple_of(step * CHUNK, CHUNK), CHUNK)
        aux = aux_ref[0, :, here]
        raw = raw_ref[0, :, here]
        bc = pz_ref[0, here, wide:]
        dt, cum, carried, toward = pieces(raw, hp_ref[0], hp_ref[1], aux, tri_ref[...])
        cols = compact([aux, cum, dt, carried, toward])
        both = hi_lo(cols)
        dtx = dot_nn(both, expand[0])
        carx = dot_nn(both, expand[1])
        towx = dot_nn(both, expand[2])
        pad = cols[:, 1:2]
        same = [None] + [cols[:, 1 + k : 2 + k] for k in range(1, TAPS)]
        low = iota2((CHUNK, 128), 1) < HEADDIM

        bbuf[HALO:] = bc.astype(F32) * pad
        maps = cbw_ref[TAPS : TAPS + 1] + cbw_ref[0:1] * bbuf[HALO:]
        for k in range(1, TAPS):
            maps = maps + cbw_ref[k : k + 1] * (same[k] * bbuf[HALO - k : HALO - k + CHUNK])
        pbc_ref[0, here] = maps.astype(BF)
        maps = (maps * sigmoid(maps)).astype(BF)
        cbc_ref[0, here] = maps
        bbuf[0:HALO] = bbuf[CHUNK : CHUNK + HALO]
        keys, queries = maps[:, :STATE], maps[:, STATE:]
        scores = dot_nt(queries, keys)
        keys_t = keys.astype(F32).T.astype(BF)

        for p in range(pairs):
            s = slice(128 * p, 128 * p + 128)
            x0 = pz_ref[0, here, 256 * p : 256 * p + 128].astype(F32)
            x1 = pz_ref[0, here, 256 * p + 128 : 256 * p + 256].astype(F32)
            value = jnp.where(low, pltpu.roll(x0, HEADDIM, 1), x1)
            ubuf[HALO:, s] = value * pad
            pre = cw_ref[TAPS : TAPS + 1, s] + cw_ref[0:1, s] * ubuf[HALO:, s]
            for k in range(1, TAPS):
                pre = pre + cw_ref[k : k + 1, s] * (same[k] * ubuf[HALO - k : HALO - k + CHUNK, s])
            pre_ref[0, here, s] = pre.astype(BF)
            cv = (pre * sigmoid(pre)).astype(BF)
            cv_ref[0, here, s] = cv
            vd[:, s] = (cv.astype(F32) * dtx[:, s]).astype(BF)
        ubuf[0:HALO] = ubuf[CHUNK : CHUNK + HALO]

        old = state[...]
        old_b = old.astype(BF)
        st_ref[0, step] = old_b
        yint[...] = dot_nn(queries, old_b) * carx
        state[...] = carx[CHUNK - 1 : CHUNK] * old + dot_nn(keys_t, (vd[...].astype(F32) * towx).astype(BF))

        inside = (iota2((CHUNK, CHUNK), 0) >= iota2((CHUNK, CHUNK), 1)) & (cols[:, 0:1] == aux[0:1])
        fence = jnp.where(inside, 0.0, FAR)
        squares = jnp.zeros((CHUNK, 128), F32)
        for p in range(pairs):
            s = slice(128 * p, 128 * p + 128)
            mix = []
            for h in (2 * p, 2 * p + 1):
                decay = jnp.exp2(cols[:, AUX + h : AUX + h + 1] - cum[h : h + 1] + fence)
                mix.append((scores * decay).astype(BF))
            v = vd[:, s]
            zero = jnp.zeros_like(v)
            stacked = jnp.concatenate([jnp.where(low, v, zero), jnp.where(low, zero, v)], axis=0)
            y = dot_nn(jnp.concatenate(mix, axis=1), stacked)
            mixed = y + yint[:, s] + cw_ref[5:6, s] * cv_ref[0, here, s].astype(F32)
            x0 = pz_ref[0, here, 256 * p : 256 * p + 128].astype(F32)
            x1 = pz_ref[0, here, 256 * p + 128 : 256 * p + 256].astype(F32)
            gate = jnp.where(low, x0, pltpu.roll(x1, HEADDIM, 1))
            gated = mixed * (gate * sigmoid(gate))
            mixed_ref[0, here, s] = mixed.astype(BF)
            gated_ref[0, here, s] = (gated * cw_ref[6:7, s]).astype(BF)
            squares = squares + gated * gated
        lane = iota2((CHUNK, 128), 1)
        sums = jnp.where(lane == 0, jnp.sum(squares, axis=1, keepdims=True), 0.0)
        stat_ref[0, :, here] = sums.T[0:8]
        return carry

    lax.fori_loop(0, BLOCK // CHUNK, chunk_step, 0)

    @pl.when(now == last)
    def _():
        gather.across(place.first - 1)
        gather.finish()
        if swap:
            swap.finish()


def backward_kernel(
    place, heads, pz_ref, raw_ref, aux_ref, cot_ref, mixed_ref, cv_ref, pre_ref, cbc_ref, pbc_ref,
    st_ref, stat_ref, cw_ref, cbw_ref, hp_ref, out_ref, w_ref, tok_ref, y_ref, gn_all, cot_all, stat_all,
    ge_ref, dg_ref, flat_ref, y_away, grad_rows,
    g_s, dstate, cbuf, dbuf, vd, gm_s, gmc_s, ggate_s, bs_s, expand, collect, tri_ref, suf_ref, ghead_ref,
    normed_s, part_buf, core_buf, x_buf, z_buf, core_send, core_recv, x_send, x_recv, z_send, z_recv, y_sem,
):
    inner = heads * HEADDIM
    pairs = heads // 2
    wide = 2 * inner
    now = pl.program_id(0) * pl.num_programs(1) + pl.program_id(1)
    last = place.steps - 1
    first = now == 0
    gch_ref = flat_ref.at[8:16, 0:inner]
    gmap_ref = flat_ref.at[0:8, 0 : 2 * STATE]
    gpre_ref = flat_ref.at[5:6]
    spot = Spot(place)
    scatter = None
    if place.fused:
        scatter = LineScatter(
            spot, part_buf, core_buf, x_buf, z_buf, grad_rows, core_send, core_recv, x_send, x_recv, z_send, z_recv
        )

        def out_terms(there):
            part_buf[there] = lax.dot_general(
                cot_all[:, there], normed_s[...], (((0,), (0,)), ((), ())), preferred_element_type=F32
            ).astype(BF)

    if place.fused or place.pair:

        @pl.when(first)
        def _():
            spot.greet(place.pair)

    if place.pair:
        half = HalfSwap(spot, y_ref, y_away, y_sem)
        pl.when(first)(half.begin)

    if place.fused:

        @pl.when(first)
        def _():
            def scale(step, carry):
                rows = pl.ds(pl.multiple_of(step * CHUNK, CHUNK), CHUNK)
                seq = lax.div(step, place.length // CHUNK)
                there = pl.ds(pl.multiple_of(lax.rem(step, place.length // CHUNK) * CHUNK, CHUNK), CHUNK)
                rms_col = compact([stat_all[seq, :, there]])[:, 0:1]
                normed_s[rows] = (gn_all[rows].astype(F32) * rms_col).astype(BF)
                return carry

            lax.fori_loop(0, normed_s.shape[0] // CHUNK, scale, 0)
            scatter.produce(out_terms, True)

        @pl.when(now == min(1, last))
        def _():
            scatter.cross()
            scatter.produce(out_terms, False)

        @pl.when(now == min(2, last))
        def _():
            scatter.along()

    @pl.when(first)
    def _():
        for i, place in enumerate((AUX + heads, AUX + 2 * heads, AUX + 3 * heads)):
            expand[i] = expander(heads, inner, place)
        collect[0] = collector(inner, heads)
        collect[1] = collector(inner, 2 * heads)
        r, c = iota2((CHUNK, CHUNK), 0), iota2((CHUNK, CHUNK), 1)
        tri_ref[...] = jnp.where(r <= c, 1.0, 0.0).astype(BF)
        suf_ref[...] = jnp.where(r >= c, 1.0, 0.0).astype(BF)
        flat_ref[...] = jnp.zeros_like(flat_ref)
        ghead_ref[...] = jnp.zeros_like(ghead_ref)

    @pl.when(pl.program_id(1) == 0)
    def _():
        dstate[...] = jnp.zeros_like(dstate)
        cbuf[CHUNK:] = jnp.zeros((HALO, inner), F32)
        dbuf[CHUNK:] = jnp.zeros((HALO, 2 * STATE), F32)

    g_s[...] = dot_nn(cot_ref[0], out_ref[...])

    def chunk_step(step, carry):
        here = pl.ds(pl.multiple_of(BLOCK - CHUNK - step * CHUNK, CHUNK), CHUNK)
        aux = aux_ref[0, :, here]
        rate = hp_ref[1]
        dt, cum, carried, toward = pieces(raw_ref[0, :, here], hp_ref[0], rate, aux, tri_ref[...])
        cols = compact([aux, cum, dt, carried, toward, stat_ref[0, :, here]])
        both = hi_lo(cols)
        dtx = dot_nn(both, expand[0])
        carx = dot_nn(both, expand[1])
        towx = dot_nn(both, expand[2])
        pad = cols[:, 1:2]
        ahead = [None] + [cols[:, 7 + k : 8 + k] for k in range(1, TAPS)]
        base = AUX + 4 * heads
        rms, pull = cols[:, base : base + 1], cols[:, base + 1 : base + 2]
        low = iota2((CHUNK, 128), 1) < HEADDIM
        maps = cbc_ref[0, here]
        keys, queries = maps[:, :STATE], maps[:, STATE:]
        queries_t = queries.astype(F32).T.astype(BF)
        scores_t = dot_nt(keys, queries)

        for p in range(pairs):
            s = slice(128 * p, 128 * p + 128)
            x0 = pz_ref[0, here, 256 * p : 256 * p + 128].astype(F32)
            x1 = pz_ref[0, here, 256 * p + 128 : 256 * p + 256].astype(F32)
            gate = jnp.where(low, x0, pltpu.roll(x1, HEADDIM, 1))
            sig = sigmoid(gate)
            act = gate * sig
            mixed = mixed_ref[0, here, s].astype(F32)
            gated = mixed * act
            g = g_s[here, s]
            grad_gated = rms * (g * cw_ref[6:7, s]) - gated * pull
            gm = grad_gated * act
            ggate_s[:, s] = (grad_gated * mixed * (sig * (1.0 + gate * (1.0 - sig)))).astype(BF)
            gm_s[:, s] = gm.astype(BF)
            gmc_s[:, s] = (gm * carx[:, s]).astype(BF)
            cv = cv_ref[0, here, s].astype(F32)
            vd[:, s] = (cv * dtx[:, s]).astype(BF)
            gch_ref[5:6, s] += jnp.sum(gm * cv, axis=0, keepdims=True)
            gch_ref[6:7, s] += jnp.sum(gated * rms * g, axis=0, keepdims=True)

        ds = dstate[...]
        ds_b = ds.astype(BF)
        st = st_ref[0, BLOCK // CHUNK - 1 - step]
        gmc = gmc_s[...]
        cs = dot_nn(queries, st)
        bs = dot_nn(keys, ds_b) * towx
        bs_s[...] = bs
        reach = dot_nn((gmc.astype(F32) * cs).astype(BF), collect[1])
        reach = reach + dot_nn((bs * cv_ref[0, here].astype(F32)).astype(BF), collect[0])
        grad_q = dot_nt(gmc, st)
        grad_k = dot_nt((vd[...].astype(F32) * towx).astype(BF), ds_b)
        keep = carx[CHUNK - 1 : CHUNK]
        held = jnp.sum(st.astype(F32) * ds, axis=0, keepdims=True) * keep
        dstate[...] = keep * ds + dot_nn(queries_t, gmc)

        inside = (iota2((CHUNK, CHUNK), 0) <= iota2((CHUNK, CHUNK), 1)) & (cols[:, 0:1] == aux[0:1])
        fence = jnp.where(inside, 0.0, FAR)
        grad_scores_t = jnp.zeros((CHUNK, CHUNK), F32)
        lane = iota2((CHUNK, 128), 1)
        gathered = reach
        row_sums = []
        for p in range(pairs):
            s = slice(128 * p, 128 * p + 128)
            gm_b = gm_s[:, s]
            zero = jnp.zeros_like(gm_b)
            gm_two = jnp.concatenate([jnp.where(low, gm_b, zero), jnp.where(low, zero, gm_b)], axis=0)
            near = dot_nt(vd[:, s], gm_two)
            mix = []
            for j in range(2):
                h = 2 * p + j
                decay = jnp.exp2(cum[h : h + 1] - cols[:, AUX + h : AUX + h + 1] + fence)
                mix.append((scores_t * decay).astype(BF))
                weighed = decay * near[:, CHUNK * j : CHUNK * j + CHUNK]
                grad_scores_t = grad_scores_t + weighed
                pairs_g = weighed * scores_t
                row_sums.append(jnp.sum(pairs_g, axis=0, keepdims=True))
                gathered = jnp.where(lane == h, jnp.sum(pairs_g, axis=1, keepdims=True), gathered)
            z = dot_nn(jnp.concatenate(mix, axis=1), gm_two)
            gm = gm_b.astype(F32)
            grad_v = cw_ref[5:6, s] * gm + dtx[:, s] * (z + bs_s[:, s])
            x0 = pz_ref[0, here, 256 * p : 256 * p + 128].astype(F32)
            x1 = pz_ref[0, here, 256 * p + 128 : 256 * p + 256].astype(F32)
            u = jnp.where(low, pltpu.roll(x0, HEADDIM, 1), x1) * pad
            pre = pre_ref[0, here, s].astype(F32)
            sig = sigmoid(pre)
            c = grad_v * (sig * (1.0 + pre * (1.0 - sig)))
            cbuf[0:CHUNK, s] = c
            gu = cw_ref[0:1, s] * c
            gch_ref[4:5, s] += jnp.sum(c, axis=0, keepdims=True)
            gch_ref[0:1, s] += jnp.sum(c * u, axis=0, keepdims=True)
            for k in range(1, TAPS):
                shifted = ahead[k] * cbuf[k : k + CHUNK, s]
                gu = gu + cw_ref[k : k + 1, s] * shifted
                gch_ref[k : k + 1, s] += jnp.sum(shifted * u, axis=0, keepdims=True)
            gu = gu * pad
            ggate = ggate_s[:, s].astype(F32)
            ge_ref[0, here, 256 * p : 256 * p + 128] = jnp.where(low, ggate, pltpu.roll(gu, HEADDIM, 1)).astype(BF)
            ge_ref[0, here, 256 * p + 128 : 256 * p + 256] = jnp.where(low, pltpu.roll(ggate, HEADDIM, 1), gu).astype(BF)
        cbuf[CHUNK:] = cbuf[0:HALO]

        gst = grad_scores_t.astype(BF)
        grad_k = grad_k + dot_nn(gst, queries)
        grad_q = grad_q + dot_nn(grad_scores_t.T.astype(BF), keys)
        pbc = pbc_ref[0, here].astype(F32)
        sig = sigmoid(pbc)
        c = jnp.concatenate([grad_k, grad_q], axis=1) * (sig * (1.0 + pbc * (1.0 - sig)))
        dbuf[0:CHUNK] = c
        u = pz_ref[0, here, wide:].astype(F32) * pad
        gu = cbw_ref[0:1] * c
        gmap_ref[4:5] += jnp.sum(c, axis=0, keepdims=True)
        gmap_ref[0:1] += jnp.sum(c * u, axis=0, keepdims=True)
        for k in range(1, TAPS):
            shifted = ahead[k] * dbuf[k : k + CHUNK]
            gu = gu + cbw_ref[k : k + 1] * shifted
            gmap_ref[k : k + 1] += jnp.sum(shifted * u, axis=0, keepdims=True)
        ge_ref[0, here, wide : wide + 2 * STATE] = (gu * pad).astype(BF)
        dbuf[CHUNK:] = dbuf[0:HALO]

        across = gathered.T
        col_sum = across[0:heads]
        kx = across[heads : 2 * heads]
        rint = across[2 * heads : 3 * heads]
        row_sum = jnp.concatenate(row_sums, axis=0)
        k_all = kx * dt
        held_head = exact_dot(jnp.broadcast_to(held, (16, inner)), collect[0])
        held_col = jnp.broadcast_to(held_head[0:1], (CHUNK, 128)).T[heads : 2 * heads]
        diff = row_sum + rint - col_sum - k_all
        grad_a = exact_dot(diff, suf_ref[...]) + jnp.sum(k_all, axis=1, keepdims=True) + held_col
        direct = jnp.where(dt > 0.0, col_sum / jnp.where(dt > 0.0, dt, 1.0), 0.0)
        grad_dt = direct + kx + rate * grad_a
        graw = grad_dt * aux[1:2] * sigmoid(raw_ref[0, :, here] + hp_ref[0])
        ge_ref[0, here, wide + 2 * STATE :] = compact([graw]).astype(BF)
        ghead_ref[0] += graw
        ghead_ref[1] += rate * dt * grad_a
        return carry

    lax.fori_loop(0, BLOCK // CHUNK, chunk_step, 0)
    dg = dot_nt(ge_ref[0], w_ref[...])
    dg_ref[0] = dg.astype(BF)
    gpre_ref[...] += jnp.sum(dg * tok_ref[0].astype(F32), axis=0, keepdims=True)

    @pl.when(now == last)
    def _():
        for i in range(2):
            sums = jnp.broadcast_to(jnp.sum(ghead_ref[i], axis=1, keepdims=True), (heads, 128))
            flat_ref[15:16, 128 * i : 128 * i + 128] = compact([sums])[0:1]
        if place.fused:
            scatter.finish()
        else:
            grad_rows[...] = jnp.zeros_like(grad_rows)
        if place.pair:
            half.finish()


def gather_kernel(
    place, heads, zx_ref, bc_ref, step_ref, hidden_ref, gain_ref, cxw_ref, cxb_ref, cbw_ref, cbb_ref, head_ref,
    ngain_ref, seg_ref, pad_ref,
    w_all, tok_full, aux_ref, cw_ref, cbw_out, hp_ref,
    shard, tok_own, square, send_sem, recv_sem, local_sem, tok_sem,
):
    inner = heads * HEADDIM
    wide = 2 * inner
    spot = Spot(place)
    rows = zx_ref.shape[0]
    shard[:, 0:wide] = zx_ref[...]
    shard[:, wide : wide + 2 * STATE] = bc_ref[...]
    square[...] = jnp.zeros_like(square)
    square[0:heads, 0:rows] = step_ref[...].astype(F32)
    shard[:, wide + 2 * STATE :] = square[...].T[0:rows].astype(BF)
    spot.greet(place.pair)
    gather = LineGather(spot, [(shard, w_all)], send_sem, recv_sem, local_sem)
    gather.begin()

    size = 64
    seqs, here = hidden_ref.shape[0], hidden_ref.shape[1]

    def norm_rows(step, carry):
        seq, cut = lax.div(step, here // size), lax.rem(step, here // size)
        mine = pl.ds(pl.multiple_of(cut * size, size), size)
        hid = hidden_ref[seq, mine].astype(F32)
        inv = lax.rsqrt(jnp.mean(hid * hid, axis=-1, keepdims=True) + epsilon)
        tok_own[seq, mine] = (hid * inv * gain_ref[...]).astype(BF)
        return carry

    lax.fori_loop(0, seqs * (here // size), norm_rows, 0)
    if place.pair:
        swap = TokenSwap(spot, tok_own, tok_full, tok_sem)
        swap.begin()
    else:
        copy = pltpu.make_async_copy(tok_own, tok_full, tok_sem.at[2])
        copy.start()

    square[...] = jnp.zeros_like(square)
    square[0:3, 0:heads] = head_ref[...]
    per_head = square[...].T
    hp_ref[0] = jnp.broadcast_to(per_head[0:heads, 0:1], (heads, 128))
    hp_ref[1] = jnp.broadcast_to(-jnp.exp(per_head[0:heads, 1:2]), (heads, 128))
    cw_ref[0:TAPS] = cxw_ref[...]
    cw_ref[TAPS : TAPS + 1] = cxb_ref[...]
    cw_ref[5:6] = exact_dot(square[0:16], expander(heads, inner, 0)[0:128])[2:3]
    cw_ref[6:7] = ngain_ref[...]
    cw_ref[7:8] = jnp.zeros((1, inner), F32)
    cbw_out[...] = jnp.zeros_like(cbw_out)
    cbw_out[0:TAPS] = cbw_ref[...]
    cbw_out[TAPS : TAPS + 1] = cbb_ref[...]

    length = place.length
    lane = iota2((8, length), 1)
    flag = lambda condition: jnp.where(condition, 1.0, 0.0)[0:1]
    for seq in range(aux_ref.shape[0]):
        seg = jnp.broadcast_to(seg_ref[seq : seq + 1], (8, length))
        aux_ref[seq] = jnp.zeros((AUX, length), F32)
        aux_ref[seq, 0:1] = seg[0:1].astype(F32)
        aux_ref[seq, 1:2] = pad_ref[seq : seq + 1].astype(F32)
        for k in range(1, TAPS):
            aux_ref[seq, 1 + k : 2 + k] = flag((pltpu.roll(seg, k, 1) == seg) & (lane >= k))
            aux_ref[seq, 7 + k : 8 + k] = flag((pltpu.roll(seg, length - k, 1) == seg) & (lane < length - k))
        before = jnp.full((8, CHUNK), -1, jnp.int32)
        for chunk in range(length // CHUNK):
            cut = slice(chunk * CHUNK, (chunk + 1) * CHUNK)
            block = seg[:, cut]
            tail = jnp.broadcast_to(block[:, CHUNK - 1 : CHUNK], (8, CHUNK))
            aux_ref[seq, 5:6, cut] = flag(block == before)
            aux_ref[seq, 6:7, cut] = flag(block == tail)
            before = tail

    gather.across(0) if place.first == 1 else None
    for hop in range(1, place.first):
        gather.along(hop)
        gather.across(hop - 1)
    if place.first > 1:
        gather.across(place.first - 1)
    gather.finish()
    swap.finish() if place.pair else copy.wait()


def out_kernel(place, inner_all, gn_ref, cot_ref, out_ref, stat_ref, y_ref, back_ref, sums, theirs, sem):
    seq, block = pl.program_id(0), pl.program_id(1)
    now = seq * pl.num_programs(1) + block
    if place.pair:
        s = Spot(place)
        barrier = pltpu.get_barrier_semaphore()

        @pl.when(now == 0)
        def _():
            pl.semaphore_signal(barrier, inc=1, device_id=(s.index, 1 - s.me), device_id_type=MESH)
            pl.semaphore_wait(barrier, 1)

    y = dot_nt(gn_ref[0], out_ref[...])
    y_ref[0] = y.astype(BF)
    cross = jnp.sum(y * cot_ref[0].astype(F32), axis=1, keepdims=True)
    row = jnp.broadcast_to(cross, (cross.shape[0], 128)).T[0:8]
    there = pl.ds(pl.multiple_of(block * BLOCK, BLOCK), BLOCK)
    sums[seq, :, there] = jnp.where(iota2(row.shape, 0) == 1, row, stat_ref[0])

    @pl.when(now == place.steps - 1)
    def _():
        total = sums[...]
        if place.pair:
            copy = s.copy(sums, theirs, sem.at[0], sem.at[1], s.index, 1 - s.me)
            copy.start()
            copy.wait()
            total = total + theirs[...]
        back_ref[...] = finish_sums(total, inner_all) if place.pair else total


def finish_sums(total, inner_all):
    lines = lax.broadcasted_iota(jnp.int32, total.shape, 1)
    rms = lax.rsqrt(total[:, 0:1] / inner_all + epsilon)
    pull = rms * rms * rms * (total[:, 1:2] / inner_all)
    return jnp.where(lines == 0, rms, jnp.where(lines == 1, pull, 0.0))


def reduce_kernel(
    place, tok_ref, ge_ref, flat_ref, dg_ref, hidden_ref, cot_ref, gain_ref, y_ref, y_away, back_ref,
    own_ref, sum_ref, gh_ref, output_ref,
    part_buf, core_buf, x_buf, z_buf, acc, dg_buf, bc_buf, bc_send, y_flat, core_flat, x_flat, z_flat, stage,
    core_send, core_recv, x_send, x_recv, z_send, z_recv, flat_send, flat_recv, dg_sem, bc_sem,
):
    spot = Spot(place)
    a, b, c, me, index = spot.a, spot.b, spot.c, spot.me, spot.index
    first, second = place.first, place.second
    scatter = LineScatter(
        spot, part_buf if place.fused else ge_ref, core_buf, x_buf, z_buf, own_ref,
        core_send, core_recv, x_send, x_recv, z_send, z_recv, PIECES,
    )
    spot.greet(place.pair)
    started = []

    def send(*args):
        copy = spot.copy(*args)
        copy.start()
        started.append(copy)

    if place.pair:
        send(flat_ref.at[0:8], y_flat, flat_send.at[0], flat_recv.at[0], index, 1 - me)
        swap = HalfSwap(spot, dg_ref, dg_buf, dg_sem)
        swap.begin()

    def terms(there):
        if place.fused:
            part_buf[there] = lax.dot_general(
                tok_ref[:, there], ge_ref[...], (((0,), (0,)), ((), ())), preferred_element_type=F32
            ).astype(BF)

    work = [(n, j) for j in list(range(1, second)) + [0] for n in range(first)]
    for k, (n, j) in enumerate(work):
        terms(scatter.terms(n, j))
        scatter.give(n, j)
        if k >= 1 and work[k - 1][1] > 0:
            scatter.cross_over(*work[k - 1])

    if place.pair:
        spot.arrived(y_flat, flat_recv.at[0])
        stage[0, 0:8] = flat_ref[0:8] + y_flat[...]
    else:
        stage[0, 0:8] = flat_ref[0:8]
    stage[0, 8:] = flat_ref[8:]
    send(stage.at[0], core_flat, flat_send.at[1], flat_recv.at[1], spot.sibling)
    spot.arrived(core_flat, flat_recv.at[1])
    stage[1] = stage[0] + core_flat[...]
    x_flat[b] = stage[1]
    for j in range(1, second):
        send(stage.at[1], x_flat.at[b], flat_send.at[1 + j], flat_recv.at[2 + b], spot.at(a, spot.aside(j), c))

    scatter.chain(acc)
    for j in range(1, second):
        spot.arrived(x_flat.at[spot.aside(j)], flat_recv.at[2 + spot.aside(j)])
    total = x_flat[0]
    for j in range(1, second):
        total = total + x_flat[j]
    stage[2] = total
    z_flat[a] = total
    for i in range(1, first):
        send(
            stage.at[2], z_flat.at[a], flat_send.at[second + i], flat_recv.at[2 + second + a],
            spot.at(spot.around(i), b, c),
        )

    if place.pair:
        swap.finish()
        here = hidden_ref.shape[1]
        size = 128

        def token_rows(step, carry):
            seq, cut = lax.div(step, here // size), lax.rem(step, here // size)
            mine = pl.ds(pl.multiple_of(cut * size, size), size)
            full = pl.ds(pl.multiple_of(me * here + cut * size, size), size)
            hid = hidden_ref[seq, mine].astype(F32)
            inv = lax.rsqrt(jnp.mean(hid * hid, axis=-1, keepdims=True) + epsilon)
            gain = (dg_ref[seq, full].astype(F32) + dg_buf[seq, mine].astype(F32)) * gain_ref[...]
            pull = inv * inv * inv * jnp.mean(hid * gain, axis=-1, keepdims=True)
            gh_ref[seq, mine] = (cot_ref[seq, mine].astype(F32) + inv * gain - hid * pull).astype(BF)
            rms = compact([back_ref[seq, :, full]])[:, 0:1]
            mixed = y_ref[seq, full].astype(F32) + y_away[seq, mine].astype(F32)
            output_ref[seq, mine] = (hid + rms * mixed).astype(BF)
            return carry

        lax.fori_loop(0, hidden_ref.shape[0] * (here // size), token_rows, 0)
    else:
        gh_ref[...] = jnp.zeros_like(gh_ref)
        output_ref[...] = jnp.zeros_like(output_ref)

    scatter.finish_chain()
    if place.pair:
        edge = own_ref.shape[1] - 128 - 2 * STATE
        bc_send[...] = own_ref[:, edge : edge + 2 * STATE]
        swap_bc = spot.copy(bc_send, bc_buf, bc_sem.at[0], bc_sem.at[1], index, 1 - me)
        swap_bc.start()
    for i in range(1, first):
        spot.arrived(z_flat.at[spot.around(i)], flat_recv.at[2 + second + spot.around(i)])
    total = z_flat[0]
    for i in range(1, first):
        total = total + z_flat[i]
    sum_ref[...] = total
    scatter.wait_sends()
    for copy in started:
        copy.wait_send()
    if place.pair:
        swap_bc.wait()
        own_ref[:, edge : edge + 2 * STATE] = bc_send[...] + bc_buf[...]


def last_kernel(
    heads, own_ref, sum_ref, gh_in, output_in, out_rows, gain_ref,
    output_ref, gh_ref, pre_ref, zx_ref, bc_ref, step_ref, cxw_ref, cxb_ref, cbw_ref, cbb_ref, head_ref, ngain_ref,
    out_ref,
):
    inner = heads * HEADDIM
    wide = 2 * inner
    rows = own_ref.shape[0]
    output_ref[...] = output_in[...]
    gh_ref[...] = gh_in[...]
    pre_ref[...] = sum_ref[5:6] / gain_ref[...]
    zx_ref[...] = own_ref[:, 0:wide]
    bc_ref[...] = own_ref[:, wide : wide + 2 * STATE]
    steps = own_ref[:, wide + 2 * STATE :]
    if rows < 128:
        steps = jnp.concatenate([steps, jnp.zeros((128 - rows, 128), F32)], axis=0)
    step_ref[...] = steps.T[0:heads, 0:rows]
    cxw_ref[...] = sum_ref[8 : 8 + TAPS, 0:inner]
    cxb_ref[...] = sum_ref[8 + TAPS : 9 + TAPS, 0:inner]
    cbw_ref[...] = sum_ref[0:TAPS, 0 : 2 * STATE]
    cbb_ref[...] = sum_ref[TAPS : TAPS + 1, 0 : 2 * STATE]
    skip = exact_dot(jnp.broadcast_to(sum_ref[13:14, 0:inner], (16, inner)), collector(inner, 0))
    head_ref[0:1] = sum_ref[15:16, 0:heads]
    head_ref[1:2] = sum_ref[15:16, 128 : 128 + heads]
    head_ref[2:3] = skip[0:1, 0:heads]
    ngain_ref[...] = sum_ref[14:15, 0:inner]
    out_ref[...] = out_rows[...]


SDS = jax.ShapeDtypeStruct
DMA = pltpu.SemaphoreType.DMA
ANY = pl.BlockSpec(memory_space=pl.ANY)
WHOLE = pl.BlockSpec(memory_space=pltpu.VMEM)


def params(collective=None):
    if collective is None:
        return pltpu.CompilerParams(vmem_limit_bytes=VMEM_LIMIT)
    return pltpu.CompilerParams(vmem_limit_bytes=VMEM_LIMIT, collective_id=collective, has_side_effects=True)


def whole_once(*shape):
    return pl.BlockSpec(shape, lambda s, c: (0,) * len(shape), pipeline_mode=pl.Buffered(1))


def line_sems(place, cuts, lines):
    columns = place.first * max(place.second - 1, 1) * cuts
    blocks = place.first * place.second * cuts
    return [DMA((blocks,)), DMA((blocks,)), DMA((columns,)), DMA((columns,)), DMA((place.first * cuts,)), DMA((lines,))]


def gather_all(place, size, zx, bc, step_t, hidden, gain, cxw, cxb, cbw, cbb, head, ngain, seg, pad):
    seqs, here, width = hidden.shape
    heads, inner = head.shape[1], cxw.shape[1]
    total = 2 * inner + 2 * STATE + 128
    rows = zx.shape[0]
    return pl.pallas_call(
        functools.partial(gather_kernel, place, heads),
        in_specs=[WHOLE] * 13,
        out_specs=[ANY, ANY] + [WHOLE] * 4,
        out_shape=[
            SDS((size * rows, total), BF), SDS((seqs, place.length if place.pair else here, width), BF),
            SDS((seqs, AUX, place.length), F32), SDS((8, inner), F32), SDS((8, 2 * STATE), F32), SDS((2, heads, 128), F32),
        ],
        scratch_shapes=[
            pltpu.VMEM((rows, total), BF), pltpu.VMEM(hidden.shape, BF), pltpu.VMEM((128, 128), F32),
            DMA((1, gather_sites(place.first, place.second))), DMA((1, size)), DMA((1,)), DMA((3,)),
        ],
        compiler_params=params(0),
        name="gather_all",
    )(zx, bc, step_t, hidden, gain, cxw, cxb, cbw, cbb, head, ngain, seg, pad)


def mixer_forward(place, size, tok, weights, aux, cw, cbw, hp, cot_own, out_own):
    seqs, length, width = tok.shape
    heads, inner = hp.shape[1], cw.shape[1]
    wide = 2 * inner + 2 * STATE
    chunks = length // CHUNK
    token = lambda size: pl.BlockSpec((1, BLOCK, size), lambda s, c: (s, c, 0))
    row = lambda high: pl.BlockSpec((1, high, BLOCK), lambda s, c: (s, 0, c))
    return pl.pallas_call(
        functools.partial(forward_kernel, place, heads),
        grid=(seqs, length // BLOCK),
        in_specs=[
            token(width), whole_once(*weights.shape), row(AUX),
            whole_once(8, inner), whole_once(8, 2 * STATE), whole_once(2, heads, 128), WHOLE, ANY,
        ],
        out_specs=[
            token(wide), row(heads), token(inner), token(inner), token(inner), token(inner), token(2 * STATE),
            token(2 * STATE), pl.BlockSpec((1, BLOCK // CHUNK, STATE, inner), lambda s, c: (s, c, 0, 0)), row(8),
            ANY, ANY,
        ],
        out_shape=[
            SDS((seqs, length, wide), BF), SDS((seqs, heads, length), F32),
            SDS((seqs, length, inner), BF), SDS((seqs, length, inner), BF), SDS((seqs, length, inner), BF),
            SDS((seqs, length, inner), BF), SDS((seqs, length, 2 * STATE), BF), SDS((seqs, length, 2 * STATE), BF),
            SDS((seqs, chunks, STATE, inner), BF), SDS((seqs, 8, length), F32),
            SDS((size * out_own.shape[0], inner), BF), SDS((seqs, length, width) if place.pair else (8, 128), BF),
        ],
        scratch_shapes=[
            pltpu.VMEM((STATE, inner), F32), pltpu.VMEM((HALO + CHUNK, inner), F32),
            pltpu.VMEM((HALO + CHUNK, 2 * STATE), F32), pltpu.VMEM((CHUNK, inner), BF),
            pltpu.VMEM((CHUNK, inner), F32), pltpu.VMEM((3, 256, inner), BF), pltpu.VMEM((CHUNK, CHUNK), BF),
            DMA((1, gather_sites(place.first, place.second))), DMA((1, size)), DMA((1,)), DMA((3,)),
        ],
        compiler_params=params(1),
        name="mixer_forward",
    )(tok, weights, aux, cw, cbw, hp, cot_own, out_own)


def out_project(place, inner_all, gn, cot, out_all, stat):
    seqs, length, inner = gn.shape
    width = cot.shape[2]
    token = lambda last: pl.BlockSpec((1, BLOCK, last), lambda s, c: (s, c, 0))
    row = pl.BlockSpec((1, 8, BLOCK), lambda s, c: (s, 0, c))
    shape = (seqs, 8, length)
    return pl.pallas_call(
        functools.partial(out_kernel, place, inner_all),
        grid=(seqs, length // BLOCK),
        in_specs=[token(inner), token(width), whole_once(*out_all.shape), row],
        out_specs=[token(width), pl.BlockSpec(shape, lambda s, c: (0, 0, 0))],
        out_shape=[SDS((seqs, length, width), BF), SDS(shape, F32)],
        scratch_shapes=[pltpu.VMEM(shape, F32), pltpu.VMEM(shape, F32), DMA((2,))],
        compiler_params=params(2 if place.pair else None),
        name="out_project",
    )(gn, cot, out_all, stat)


def mixer_backward(
    place, size, pz, raw, aux, cot, mixed, cv, pre, cbc, pbc, st, stat, cw, cbw, hp, out_all, weights, tok, y, gn
):
    seqs, length, width = cot.shape
    heads, inner = hp.shape[1], cw.shape[1]
    last = length // BLOCK - 1
    here = length // 2 if place.pair else 16
    rows = width // size
    tokens = seqs * length
    fused = place.fused
    token = lambda size: pl.BlockSpec((1, BLOCK, size), lambda s, c: (s, last - c, 0))
    row = lambda high: pl.BlockSpec((1, high, BLOCK), lambda s, c: (s, 0, last - c))
    fixed = lambda *shape: pl.BlockSpec(shape, lambda s, c: (0,) * len(shape))
    gn_all, cot_all = (gn, cot) if fused else (gn[:1, :16], cot[:1, :16])
    gn_all, cot_all = gn_all.reshape(-1, inner), cot_all.reshape(-1, width)
    blocks = place.first * place.second
    columns = place.first * max(place.second - 1, 1)
    rs = lambda count: pltpu.VMEM((count, rows, inner) if fused else (1, 16, 128), BF)
    return pl.pallas_call(
        functools.partial(backward_kernel, place, heads),
        grid=(seqs, length // BLOCK),
        in_specs=[
            token(pz.shape[2]), row(heads), row(AUX), token(width), token(inner), token(inner),
            token(inner), token(2 * STATE), token(2 * STATE),
            pl.BlockSpec((1, BLOCK // CHUNK, STATE, inner), lambda s, c: (s, last - c, 0, 0)), row(8),
            whole_once(8, inner), whole_once(8, 2 * STATE), whole_once(2, heads, 128),
            whole_once(*out_all.shape), whole_once(*weights.shape), token(width), ANY,
            whole_once(*gn_all.shape), whole_once(*cot_all.shape), whole_once(*stat.shape),
        ],
        out_specs=[token(weights.shape[1]), token(width), fixed(16, width), ANY, fixed(rows, inner)],
        out_shape=[
            SDS((seqs, length, weights.shape[1]), BF), SDS((seqs, length, width), BF), SDS((16, width), F32),
            SDS((seqs, here, width), BF), SDS((rows, inner), F32),
        ],
        scratch_shapes=[
            pltpu.VMEM((BLOCK, inner), F32),
            pltpu.VMEM((STATE, inner), F32), pltpu.VMEM((CHUNK + HALO, inner), F32),
            pltpu.VMEM((CHUNK + HALO, 2 * STATE), F32), pltpu.VMEM((CHUNK, inner), BF),
            pltpu.VMEM((CHUNK, inner), BF), pltpu.VMEM((CHUNK, inner), BF), pltpu.VMEM((CHUNK, inner), BF),
            pltpu.VMEM((CHUNK, inner), F32),
            pltpu.VMEM((3, 256, inner), BF), pltpu.VMEM((2, inner, 128), BF),
            pltpu.VMEM((CHUNK, CHUNK), BF), pltpu.VMEM((CHUNK, CHUNK), BF), pltpu.VMEM((2, heads, 128), F32),
            pltpu.VMEM((tokens, inner) if fused else (16, 128), BF),
            pltpu.VMEM((width, inner) if fused else (16, 128), BF),
            rs(blocks), rs(columns), rs(place.first),
        ] + line_sems(place, 1, place.first) + [DMA((2,))],
        compiler_params=params(3 if place.fused or place.pair else None),
        name="mixer_backward",
    )(
        pz, raw, aux, cot, mixed, cv, pre, cbc, pbc, st, stat, cw, cbw, hp, out_all, weights, tok, y,
        gn_all, cot_all, stat,
    )


def reduce_all(place, size, tok, ge, flat, dg, hidden, cot_own, gain, y, y_away, back):
    seqs, length, depth = tok.shape
    width = ge.shape[2]
    rows = depth // size
    if place.fused:
        tok, ge = tok.reshape(seqs * length, depth), ge.reshape(seqs * length, width)
    else:
        ge = jnp.einsum("stp,sty->py", tok, ge, preferred_element_type=F32).astype(BF)
        tok = tok[0, :16]
    if not place.pair:
        flat = jnp.concatenate([lax.psum(flat[:8], "tensor"), flat[8:]])
        dg, hidden, cot_own, y, y_away = [jnp.zeros((1, 16, depth), BF)] * 5
        back = back[:1, :, :128]
    blocks = place.first * place.second * PIECES
    columns = place.first * max(place.second - 1, 1) * PIECES
    lines = 2 * place.first * PIECES
    cut = rows // PIECES
    own, flat, gh, output = pl.pallas_call(
        functools.partial(reduce_kernel, place),
        in_specs=[WHOLE] * 10,
        out_specs=[WHOLE] * 4,
        out_shape=[SDS((rows, width), F32), SDS(flat.shape, F32), SDS(hidden.shape, BF), SDS(hidden.shape, BF)],
        scratch_shapes=[
            pltpu.VMEM((depth, width) if place.fused else (16, 128), BF),
            pltpu.VMEM((blocks, cut, width), BF),
            pltpu.VMEM((columns, cut, width), BF),
            pltpu.VMEM((lines, cut, width), BF),
            pltpu.VMEM((cut, width), F32),
            pltpu.VMEM(hidden.shape, BF),
            pltpu.VMEM((rows, 2 * STATE), F32),
            pltpu.VMEM((rows, 2 * STATE), F32),
            pltpu.VMEM((8, flat.shape[1]), F32),
            pltpu.VMEM(flat.shape, F32),
            pltpu.VMEM((place.second,) + flat.shape, F32),
            pltpu.VMEM((place.first,) + flat.shape, F32),
            pltpu.VMEM((3,) + flat.shape, F32),
        ] + line_sems(place, PIECES, lines) + [
            DMA((1 + place.first + place.second,)), DMA((2 + place.first + place.second,)), DMA((2,)), DMA((2,)),
        ],
        compiler_params=params(4),
        name="reduce_all",
    )(tok, ge, flat, dg, hidden, cot_own, gain, y, y_away, back)
    if not place.pair:
        edge = width - 128 - 2 * STATE
        own = own.at[:, edge : edge + 2 * STATE].set(lax.psum(own[:, edge : edge + 2 * STATE], "tensor"))
    return own, flat, gh, output


def body(
    hidden, pre_gain, zx_weight, bc_weight, step_weight, conv_x_weight, conv_x_bias, conv_bc_weight, conv_bc_bias,
    step_bias, decay_log, skip_gain, norm_gain, out_weight, segment_ids, pad_mask, grad_out,
):
    n, size = lax.axis_size("tensor"), lax.axis_size("dp")
    heads = step_weight.shape[1]
    inner = heads * HEADDIM
    seqs, here, width = hidden.shape
    length = segment_ids.shape[1]
    first, second = factors(size)
    place = Place(first, second, n == 2, (2 * width // size) % 128 == 0, seqs * length // BLOCK, length)
    line = lambda vector: vector.reshape(1, -1)
    gain = line(pre_gain)

    weights, tok, aux, cw, cbw, hp = gather_all(
        place, size, zx_weight, bc_weight, step_weight.T, hidden, gain, conv_x_weight, line(conv_x_bias),
        conv_bc_weight, line(conv_bc_bias), jnp.stack([step_bias, decay_log, skip_gain]), line(norm_gain),
        segment_ids, pad_mask,
    )
    if not place.pair:
        tok = lax.all_gather(tok, "tensor", axis=1, tiled=True)
    pz, raw, mixed, gn, cv, pre, cbc, pbc, st, stat, out_all, cot = mixer_forward(
        place, size, tok, weights, aux, cw, cbw, hp, grad_out, out_weight.T
    )
    if not place.pair:
        cot = lax.all_gather(grad_out, "tensor", axis=1, tiled=True)
    y, back = out_project(place, inner * n, gn, cot, out_all, stat)
    if not place.pair:
        back = finish_sums(lax.psum(back, "tensor"), inner * n)
    ge, dg, flat, y_away, out_rows = mixer_backward(
        place, size, pz, raw, aux, cot, mixed, cv, pre, cbc, pbc, st, back, cw, cbw, hp, out_all, weights, tok, y, gn
    )
    if not place.fused:
        normed_out = (gn.astype(F32) * back[:, 0, :, None]).astype(BF)
        terms = jnp.einsum("str,stc->rc", cot, normed_out, preferred_element_type=F32).astype(BF)
        out_rows = lax.psum_scatter(terms, "dp", scatter_dimension=0, tiled=True).astype(F32)
    own, sums, grad_hidden, output = reduce_all(
        place, size, tok, ge, flat, dg, hidden, grad_out, gain, y, y_away, back
    )
    if not place.pair:
        hidden_f = hidden.astype(F32)
        inv_rms = lax.rsqrt(jnp.mean(hidden_f * hidden_f, axis=-1, keepdims=True) + epsilon)
        scatter = lambda rows: lax.psum_scatter(rows.astype(F32), "tensor", scatter_dimension=1, tiled=True)
        gain_grad = scatter(dg) * pre_gain
        pull = inv_rms**3 * jnp.mean(hidden_f * gain_grad, axis=-1, keepdims=True)
        grad_hidden = (grad_out.astype(F32) + inv_rms * gain_grad - hidden_f * pull).astype(BF)
        output = (hidden_f + scatter(y.astype(F32) * back[:, 0, :, None])).astype(BF)
    rows = own.shape[0]
    output, grad_hidden, grad_pre, gzx, gbc, gstep, gcxw, gcxb, gcbw, gcbb, ghead, gnorm, gout = pl.pallas_call(
        functools.partial(last_kernel, heads),
        in_specs=[WHOLE] * 6,
        out_specs=[WHOLE] * 13,
        out_shape=[
            SDS(hidden.shape, BF), SDS(hidden.shape, BF), SDS((1, width), F32), SDS((rows, 2 * inner), F32),
            SDS((rows, 2 * STATE), F32), SDS((heads, rows), F32), SDS((TAPS, inner), F32), SDS((1, inner), F32),
            SDS((TAPS, 2 * STATE), F32), SDS((1, 2 * STATE), F32), SDS((3, heads), F32), SDS((1, inner), F32),
            SDS((rows, inner), F32),
        ],
        compiler_params=params(),
        name="outputs",
    )(own, sums, grad_hidden, output, out_rows, gain)
    return (
        output, grad_hidden, grad_pre[0], gzx, gbc, gstep.T, gcxw, gcxb[0], gcbw, gcbb[0], ghead[0], ghead[1], ghead[2],
        gnorm[0], gout.T,
    )


def solution(mesh):
    placed = (
        P("dp", "tensor", None), P(), P("dp", "tensor"), P("dp", None), P("dp", "tensor"), P(None, "tensor"),
        P("tensor"), P(), P(), P("tensor"), P("tensor"), P("tensor"), P("tensor"), P("tensor", "dp"),
        P("dp", None), P("dp", None), P("dp", "tensor", None),
    )
    return jax.shard_map(
        body,
        mesh=mesh,
        in_specs=placed,
        out_specs=(
            P("dp", "tensor", None), P("dp", "tensor", None), P(), P("dp", "tensor"), P("dp", None), P("dp", "tensor"),
            P(None, "tensor"), P("tensor"), P(), P(), P("tensor"), P("tensor"), P("tensor"), P("tensor"),
            P("tensor", "dp"),
        ),
        check_vma=False,
    )
```

time: 267 us -> 193 us (0.72)
  local copies, waits for them, and re-layouts: 26.9 us -> 1.3 us
  waiting for transfers between devices: 25 us -> 0 us
  Pallas kernels: 168 us -> 190 us
  between operations: 14.5 us -> 0.69 us
  matrix products: 12.2 us -> 0 us
  other arithmetic: 12.7 us -> 1.27 us
  starting transfers between devices: 6.69 us -> 0 us
    pallas_call x5 -> x6, Pallas kernels: 168 us -> 190 us  [the longest x1 54.5 us: mixer_backward(): pl.pallas_call(functools.partial(backward_kernel, place, heads), grid=(se...]
    ppermute x5 -> x0, waiting for transfers between devices: 21.4 us -> none  [the longest x2 21.4 us: swap_sum(): return value + lax.ppermute(value, 'tensor', [(0, 1), (1, 0)])]
    unnamed x63 -> x0, local copies, waits for them, and re-layouts: 13.4 us -> none
    dot_general x2 -> x0, matrix products: 12.2 us -> none  [the longest x1 8.35 us: body(): jnp.einsum('stp,sty->py', normed, ge, preferred_element_type=F32).astype(BF)]
    ppermute x5 -> x0, starting transfers between devices: 6.61 us -> none  [the longest x2 3.05 us: scatter_sum(): lax.ppermute(make((1 - me) * size).astype(BF), 'tensor', [(0, 1), (1, 0)])]
    convert_element_type x2 -> x0, other arithmetic: 6.3 us -> none  [the longest x1 3.75 us: body(): grad_hidden = (grad_out.astype(F32) + inv_rms * gain_grad - hidden_f * in...]
    slice x13 -> x0, local copies, waits for them, and re-layouts: 4.56 us -> none  [the longest x1 0.83 us: body(): grad_zx_weight = own_rows[:, :wide]]
    reduce_sum x4 -> x0, other arithmetic: 3.83 us -> none  [the longest x1 2.09 us: body(): jnp.mean(hidden_f * gain_grad, axis=-1, keepdims=True)]
  transfers between devices with their start and end apart: 7 -> 0, of which waited for: 3 -> 0; matrix products, arithmetic and copies ran while one was open for 11% -> 0% of each run, Pallas kernels for 47% -> 0%
where the time goes in v4:
time: 193 us
  Pallas kernels  190 us (98%)
    pallas_call x1, Pallas kernels, mixer_backward(): pl.pallas_call(functools.partial(backward_kernel, place, heads), grid=(se...  54.5 us
    pallas_call x1, Pallas kernels, reduce_all(): pl.pallas_call(functools.partial(reduce_kernel, place), in_specs=[WHOLE]...  48.5 us
    pallas_call x1, Pallas kernels, gather_all(): pl.pallas_call(functools.partial(gather_kernel, place, heads), in_specs=[...  39.5 us
    pallas_call x1, Pallas kernels, mixer_forward(): pl.pallas_call(functools.partial(forward_kernel, place, heads), grid=(seq...  32.2 us
    pallas_call x1, Pallas kernels, out_project(): pl.pallas_call(functools.partial(out_kernel, place, inner_all), grid=(seq...  11.1 us

profile of v4, /device:TPU:0, one launch (start us, length us, event | category | flops | bytes accessed | tf_op | source)
XLA Modules:
  0.0 192.8 jit_solution(15678626788716873917)
XLA Ops:
  0.6 1.3 pad_maximum_fusion.head_ref
  1.9 39.5 %gather_all.1 = (bf16[1024,2432]{1,0:T(8,128)(2,1)}, bf16[1,1024,1024]{2,1,0:T(8,128)(2,1)}, f32[1,16,1024]{2,1,0:T(8,128)}, f32[8,1024]{1,0:T(8,128)}, f32[8,256]{1,0:T(8,128)}, /*index=5*/f32[2,16,128]{2,1,0:T(8,128)}) custom-call(bf16[64,2048]{1,0:T(8,128)(2,1)} %zx_ref.1, bf16[64,256]{1,0:T(8,128)(2,1)} %bc_ref.1, bf16[16,64]{1,0:T(8,128)(2,1)} %bitcast.33, ...), custom_call_target="tpu_custom_call" | custom-call | tf_op jit(solution)/shard_map/gather_all/pallas_call | solution.py:1106
  41.5 32.2 %mixer_forward.1 = (bf16[1,1024,2304]{2,1,0:T(8,128)(2,1)}, f32[1,16,1024]{2,1,0:T(8,128)}, bf16[1,1024,1024]{2,1,0:T(8,128)(2,1)}, bf16[1,1024,1024]{2,1,0:T(8,...) custom-call(bf16[1,1024,1024]{2,1,0:T(8,128)(2,1)} %get-tuple-elemen, ...), custom_call_target="tpu_custom_call" | custom-call | tf_op jit(solution)/shard_map/mixer_forward/pallas_call | solution.py:1130
  73.7 11.1 %out_project.1 = (bf16[1,1024,1024]{2,1,0:T(8,128)(2,1)}, f32[1,8,1024]{2,1,0:T(8,128)}) custom-call(bf16[1,1024,1024]{2,1,0:T(8,128)(2,1)} %get-tuple-element.72.gn_ref, bf16[1,1024,1024]{2,1,0:T(8,128)(2,1)} %get-tuple-element.65.cot_ref, bf16[1024,1024]{1,0:T(8,128)(2,1)} %get-tuple-element.73.out_ref, f32[1,8,1024]{2,1,0:T(8,128)} %get-tuple-element.74.stat_ref), custom_call_target="tpu_custom_call" | custom-call | tf_op jit(solution)/shard_map/out_project/pallas_call | solution.py:1166
  84.9 54.5 %mixer_backward.1 = (bf16[1,1024,2432]{2,1,0:T(8,128)(2,1)}, bf16[1,1024,1024]{2,1,0:T(8,128)(2,1)}, f32[16,1024]{1,0:T(8,128)}, bf16[1,512,1024]{2,1,0:T(8,128)(2,1)}, f32[64,1024]{1,0:T(8,128)}) custom-call(bf16[1,1024,2304]{2,1,0:T(8,128)(2,1)} %get-tuple-element.63.pz_ref, f32[1,16,1024]{2,1,0:T(8,128)} %get-tuple-element.64.raw_ref, ...), custom_call_target="tpu_custom_call" | custom-call | tf_op jit(solution)/shard_map/mixer_backward/pallas_call | solution.py:1196
  139.4 48.5 %reduce_all.1 = (f32[64,2432]{1,0:T(8,128)}, f32[16,1024]{1,0:T(8,128)}, bf16[1,512,1024]{2,1,0:T(8,128)(2,1)}, bf16[1,512,1024]{2,1,0:T(8,128)(2,1)}) custom-call(bf16[1024,1024]{1,0:T(8,128)(2,1)} %bitcast.26, bf16[1024,2432]{1,0:T(8,128)(2,1)} %bitcast.28, f32[16,1024]{1,0:T(8,128)} %get-tuple-element.78.flat_ref, ...), custom_call_target="tpu_custom_call" | custom-call | tf_op jit(solution)/shard_map/reduce_all/pallas_call | solution.py:1249
  187.9 3.6 %outputs.1 = (bf16[1,512,1024]{2,1,0:T(8,128)(2,1)}, bf16[1,512,1024]{2,1,0:T(8,128)(2,1)}, f32[1,1024]{1,0:T(1,128)}, f32[64,2048]{1,0:T(8,128)}, f32[64,256]{1...) custom-call(f32[64,2432]{1,0:T(8,128)} %get-tuple-element.81.own_ref, ...), custom_call_target="tpu_custom_call" | custom-call | tf_op jit(solution)/shard_map/outputs/pallas_call | solution.py:1328
  191.5 1.3 slice_bitcast_fusion

commit v5 on v4

--- a/solution.py
+++ b/solution.py
@@ -95,7 +95,7 @@
     return gate, value
 
 
-Place = collections.namedtuple("Place", ("first", "second", "pair", "fused", "steps", "length"))
+Place = collections.namedtuple("Place", ("first", "second", "pair", "steps", "length"))
 
 
 def factors(size):
@@ -395,9 +395,9 @@
 
                 self.start(make)
 
-    def chain(self, acc):
+    def chain(self, acc, order):
         s = self.spot
-        for n in range(s.first):
+        for n in order:
             for q in range(self.cuts):
                 i = self.order[n]
                 total = self.column_sum(n, q)
@@ -572,7 +572,7 @@
         stat_ref[0, :, here] = sums.T[0:8]
         return carry
 
-    lax.fori_loop(0, BLOCK // CHUNK, chunk_step, 0)
+    lax.fori_loop(0, BLOCK // CHUNK, chunk_step, 0, unroll=True)
 
     @pl.when(now == last)
     def _():
@@ -583,11 +583,12 @@
 
 
 def backward_kernel(
-    place, heads, pz_ref, raw_ref, aux_ref, cot_ref, mixed_ref, cv_ref, pre_ref, cbc_ref, pbc_ref,
-    st_ref, stat_ref, cw_ref, cbw_ref, hp_ref, out_ref, w_ref, tok_ref, y_ref, gn_all, cot_all, stat_all,
-    ge_ref, dg_ref, flat_ref, y_away, grad_rows,
-    g_s, dstate, cbuf, dbuf, vd, gm_s, gmc_s, ggate_s, bs_s, expand, collect, tri_ref, suf_ref, ghead_ref,
-    normed_s, part_buf, core_buf, x_buf, z_buf, core_send, core_recv, x_send, x_recv, z_send, z_recv, y_sem,
+    place, heads, inner_all, pz_ref, raw_ref, aux_ref, mixed_ref, cv_ref, pre_ref, cbc_ref, pbc_ref,
+    st_ref, stat_ref, cw_ref, cbw_ref, hp_ref, g_ref, out_ref, gn_all, cot_all,
+    ge_ref, flat_ref, y_keep, y_away, back_ref, grad_rows,
+    dstate, cbuf, dbuf, vd, gm_s, gmc_s, ggate_s, bs_s, expand, collect, tri_ref, suf_ref, ghead_ref,
+    y_s, g_s, fold, sums, theirs, normed_s, part_buf, core_buf, x_buf, z_buf,
+    core_send, core_recv, x_send, x_recv, z_send, z_recv, y_sem, stat_sem,
 ):
     inner = heads * HEADDIM
     pairs = heads // 2
@@ -597,52 +598,73 @@
     first = now == 0
     gch_ref = flat_ref.at[8:16, 0:inner]
     gmap_ref = flat_ref.at[0:8, 0 : 2 * STATE]
-    gpre_ref = flat_ref.at[5:6]
     spot = Spot(place)
-    scatter = None
-    if place.fused:
+    if place.pair:
         scatter = LineScatter(
             spot, part_buf, core_buf, x_buf, z_buf, grad_rows, core_send, core_recv, x_send, x_recv, z_send, z_recv
         )
+        half = HalfSwap(spot, y_s, y_away, y_sem)
+        here_len = y_keep.shape[1]
+        seqs = y_keep.shape[0]
+        per_seq = place.length // CHUNK
 
         def out_terms(there):
             part_buf[there] = lax.dot_general(
                 cot_all[:, there], normed_s[...], (((0,), (0,)), ((), ())), preferred_element_type=F32
             ).astype(BF)
 
-    if place.fused or place.pair:
+        def keep():
+            rows = y_s.at[:, pl.ds(pl.multiple_of(spot.me * here_len, here_len), here_len)]
+            return pltpu.make_async_copy(rows, y_keep, y_sem.at[2])
 
         @pl.when(first)
         def _():
-            spot.greet(place.pair)
-
-    if place.pair:
-        half = HalfSwap(spot, y_ref, y_away, y_sem)
-        pl.when(first)(half.begin)
-
-    if place.fused:
-
-        @pl.when(first)
-        def _():
-            def scale(step, carry):
-                rows = pl.ds(pl.multiple_of(step * CHUNK, CHUNK), CHUNK)
-                seq = lax.div(step, place.length // CHUNK)
-                there = pl.ds(pl.multiple_of(lax.rem(step, place.length // CHUNK) * CHUNK, CHUNK), CHUNK)
-                rms_col = compact([stat_all[seq, :, there]])[:, 0:1]
+            spot.greet(True)
+            for cut in range(out_ref.shape[0] // 256):
+                cols = slice(256 * cut, 256 * cut + 256)
+                for seq in range(seqs):
+                    rows = slice(seq * place.length, (seq + 1) * place.length)
+                    y = dot_nt(gn_all[rows], out_ref[cols])
+                    y_s[seq, :, cols] = y.astype(BF)
+                    y = y * cot_all[rows, cols].astype(F32)
+                    y = y[:, :128] + y[:, 128:]
+                    fold[rows] = y if cut == 0 else fold[rows] + y
+
+            for step in range(seqs * per_seq):
+                rows = slice(step * CHUNK, (step + 1) * CHUNK)
+                seq, cut = divmod(step, per_seq)
+                there = slice(cut * CHUNK, (cut + 1) * CHUNK)
+                cross = jnp.sum(fold[rows], axis=1, keepdims=True)
+                row = jnp.broadcast_to(cross, (CHUNK, 128)).T[0:8]
+                sums[seq, :, there] = jnp.where(iota2(row.shape, 0) == 1, row, stat_ref[seq, :, there])
+            swap = spot.copy(sums, theirs, stat_sem.at[0], stat_sem.at[1], spot.index, 1 - spot.me)
+            swap.start()
+
+            def out_back(step, carry):
+                rows = pl.ds(pl.multiple_of(step * BLOCK, BLOCK), BLOCK)
+                g_s[rows] = dot_nn(cot_all[rows], out_ref[...]).astype(BF)
+                return carry
+
+            lax.fori_loop(0, seqs * place.length // BLOCK, out_back, 0)
+            swap.wait()
+            half.begin()
+            keep().start()
+            back_ref[...] = finish_sums(sums[...] + theirs[...], inner_all)
+
+            for step in range(seqs * per_seq):
+                rows = slice(step * CHUNK, (step + 1) * CHUNK)
+                seq, cut = divmod(step, per_seq)
+                rms_col = compact([back_ref[seq, :, cut * CHUNK : (cut + 1) * CHUNK]])[:, 0:1]
                 normed_s[rows] = (gn_all[rows].astype(F32) * rms_col).astype(BF)
-                return carry
-
-            lax.fori_loop(0, normed_s.shape[0] // CHUNK, scale, 0)
             scatter.produce(out_terms, True)
-
-        @pl.when(now == min(1, last))
-        def _():
+            scatter.produce(out_terms, False)
             scatter.cross()
-            scatter.produce(out_terms, False)
 
         @pl.when(now == min(2, last))
         def _():
             scatter.along()
+    else:
+        pl.when(first)(lambda: back_ref.__setitem__(Ellipsis, stat_ref[...]))
 
     @pl.when(first)
     def _():
@@ -662,14 +684,17 @@
         cbuf[CHUNK:] = jnp.zeros((HALO, inner), F32)
         dbuf[CHUNK:] = jnp.zeros((HALO, 2 * STATE), F32)
 
-    g_s[...] = dot_nn(cot_ref[0], out_ref[...])
+    seq_now = pl.program_id(0)
+    block_start = (pl.num_programs(1) - 1 - pl.program_id(1)) * BLOCK
 
     def chunk_step(step, carry):
         here = pl.ds(pl.multiple_of(BLOCK - CHUNK - step * CHUNK, CHUNK), CHUNK)
+        there = pl.ds(pl.multiple_of(block_start + BLOCK - CHUNK - step * CHUNK, CHUNK), CHUNK)
+        flat_rows = pl.ds(pl.multiple_of(seq_now * place.length + block_start + BLOCK - CHUNK - step * CHUNK, CHUNK), CHUNK)
         aux = aux_ref[0, :, here]
         rate = hp_ref[1]
         dt, cum, carried, toward = pieces(raw_ref[0, :, here], hp_ref[0], rate, aux, tri_ref[...])
-        cols = compact([aux, cum, dt, carried, toward, stat_ref[0, :, here]])
+        cols = compact([aux, cum, dt, carried, toward, back_ref[seq_now, :, there]])
         both = hi_lo(cols)
         dtx = dot_nn(both, expand[0])
         carx = dot_nn(both, expand[1])
@@ -693,7 +718,7 @@
             act = gate * sig
             mixed = mixed_ref[0, here, s].astype(F32)
             gated = mixed * act
-            g = g_s[here, s]
+            g = (g_s[flat_rows, s] if place.pair else g_ref[0, here, s]).astype(F32)
             grad_gated = rms * (g * cw_ref[6:7, s]) - gated * pull
             gm = grad_gated * act
             ggate_s[:, s] = (grad_gated * mixed * (sig * (1.0 + gate * (1.0 - sig)))).astype(BF)
@@ -801,26 +826,22 @@
         return carry
 
     lax.fori_loop(0, BLOCK // CHUNK, chunk_step, 0)
-    dg = dot_nt(ge_ref[0], w_ref[...])
-    dg_ref[0] = dg.astype(BF)
-    gpre_ref[...] += jnp.sum(dg * tok_ref[0].astype(F32), axis=0, keepdims=True)
-
     @pl.when(now == last)
     def _():
         for i in range(2):
             sums = jnp.broadcast_to(jnp.sum(ghead_ref[i], axis=1, keepdims=True), (heads, 128))
             flat_ref[15:16, 128 * i : 128 * i + 128] = compact([sums])[0:1]
-        if place.fused:
+        if place.pair:
             scatter.finish()
+            half.finish()
+            keep().wait()
         else:
             grad_rows[...] = jnp.zeros_like(grad_rows)
-        if place.pair:
-            half.finish()
 
 
 def gather_kernel(
-    place, heads, zx_ref, bc_ref, step_ref, hidden_ref, gain_ref, cxw_ref, cxb_ref, cbw_ref, cbb_ref, head_ref,
-    ngain_ref, seg_ref, pad_ref,
+    place, heads, zx_ref, bc_ref, step_ref, hidden_ref, gain_ref, cxw_ref, cxb_ref, cbw_ref, cbb_ref, bias_ref, decay_ref,
+    skip_ref, ngain_ref, seg_ref, pad_ref,
     w_all, tok_full, aux_ref, cw_ref, cbw_out, hp_ref,
     shard, tok_own, square, send_sem, recv_sem, local_sem, tok_sem,
 ):
@@ -857,7 +878,9 @@
         copy.start()
 
     square[...] = jnp.zeros_like(square)
-    square[0:3, 0:heads] = head_ref[...]
+    square[0:1, 0:heads] = bias_ref[...]
+    square[1:2, 0:heads] = decay_ref[...]
+    square[2:3, 0:heads] = skip_ref[...]
     per_head = square[...].T
     hp_ref[0] = jnp.broadcast_to(per_head[0:heads, 0:1], (heads, 128))
     hp_ref[1] = jnp.broadcast_to(-jnp.exp(per_head[0:heads, 1:2]), (heads, 128))
@@ -900,36 +923,6 @@
     swap.finish() if place.pair else copy.wait()
 
 
-def out_kernel(place, inner_all, gn_ref, cot_ref, out_ref, stat_ref, y_ref, back_ref, sums, theirs, sem):
-    seq, block = pl.program_id(0), pl.program_id(1)
-    now = seq * pl.num_programs(1) + block
-    if place.pair:
-        s = Spot(place)
-        barrier = pltpu.get_barrier_semaphore()
-
-        @pl.when(now == 0)
-        def _():
-            pl.semaphore_signal(barrier, inc=1, device_id=(s.index, 1 - s.me), device_id_type=MESH)
-            pl.semaphore_wait(barrier, 1)
-
-    y = dot_nt(gn_ref[0], out_ref[...])
-    y_ref[0] = y.astype(BF)
-    cross = jnp.sum(y * cot_ref[0].astype(F32), axis=1, keepdims=True)
-    row = jnp.broadcast_to(cross, (cross.shape[0], 128)).T[0:8]
-    there = pl.ds(pl.multiple_of(block * BLOCK, BLOCK), BLOCK)
-    sums[seq, :, there] = jnp.where(iota2(row.shape, 0) == 1, row, stat_ref[0])
-
-    @pl.when(now == place.steps - 1)
-    def _():
-        total = sums[...]
-        if place.pair:
-            copy = s.copy(sums, theirs, sem.at[0], sem.at[1], s.index, 1 - s.me)
-            copy.start()
-            copy.wait()
-            total = total + theirs[...]
-        back_ref[...] = finish_sums(total, inner_all) if place.pair else total
-
-
 def finish_sums(total, inner_all):
     lines = lax.broadcasted_iota(jnp.int32, total.shape, 1)
     rms = lax.rsqrt(total[:, 0:1] / inner_all + epsilon)
@@ -938,18 +931,25 @@
 
 
 def reduce_kernel(
-    place, tok_ref, ge_ref, flat_ref, dg_ref, hidden_ref, cot_ref, gain_ref, y_ref, y_away, back_ref,
+    place, tok_ref, ge_ref, flat_ref, gain_ref, back_ref, w_hbm, hidden_hbm, cot_hbm, keep_hbm, away_hbm,
     own_ref, sum_ref, gh_ref, output_ref,
-    part_buf, core_buf, x_buf, z_buf, acc, dg_buf, bc_buf, bc_send, y_flat, core_flat, x_flat, z_flat, stage,
-    core_send, core_recv, x_send, x_recv, z_send, z_recv, flat_send, flat_recv, dg_sem, bc_sem,
+    w_ref, hidden_ref, cot_ref, keep_ref, away_ref, dg_ref, dg_send, dg_buf,
+    part_buf, core_buf, x_buf, z_buf, acc, bc_buf, bc_send, y_flat, core_flat, x_flat, z_flat, stage,
+    core_send, core_recv, x_send, x_recv, z_send, z_recv, flat_send, flat_recv, dg_sem, load_sem,
 ):
     spot = Spot(place)
     a, b, c, me, index = spot.a, spot.b, spot.c, spot.me, spot.index
     first, second = place.first, place.second
     scatter = LineScatter(
-        spot, part_buf if place.fused else ge_ref, core_buf, x_buf, z_buf, own_ref,
+        spot, part_buf if place.pair else ge_ref, core_buf, x_buf, z_buf, own_ref,
         core_send, core_recv, x_send, x_recv, z_send, z_recv, PIECES,
     )
+    loads = []
+    if place.pair:
+        pairs = ((w_hbm, w_ref), (hidden_hbm, hidden_ref), (cot_hbm, cot_ref), (keep_hbm, keep_ref), (away_hbm, away_ref))
+        for k, (far, near) in enumerate(pairs):
+            loads.append(pltpu.make_async_copy(far, near, load_sem.at[k]))
+        loads[0].start()
     spot.greet(place.pair)
     started = []
 
@@ -958,30 +958,44 @@
         copy.start()
         started.append(copy)
 
-    if place.pair:
-        send(flat_ref.at[0:8], y_flat, flat_send.at[0], flat_recv.at[0], index, 1 - me)
-        swap = HalfSwap(spot, dg_ref, dg_buf, dg_sem)
-        swap.begin()
-
     def terms(there):
-        if place.fused:
+        if place.pair:
             part_buf[there] = lax.dot_general(
                 tok_ref[:, there], ge_ref[...], (((0,), (0,)), ((), ())), preferred_element_type=F32
             ).astype(BF)
 
-    work = [(n, j) for j in list(range(1, second)) + [0] for n in range(first)]
-    for k, (n, j) in enumerate(work):
+    stage[0] = flat_ref[...]
+    here = hidden_ref.shape[1]
+
+    def token_gradient(side, to):
+        for seq in range(hidden_ref.shape[0]):
+            rows = pl.ds(pl.multiple_of(seq * place.length + side * here, here), here)
+            for cut in range(w_ref.shape[0] // 256):
+                cols = slice(256 * cut, 256 * cut + 256)
+                dg = dot_nt(ge_ref[rows], w_ref[cols])
+                to[seq, :, cols] = dg.astype(BF)
+                stage[0, 5:6, cols] += jnp.sum(dg * tok_ref[rows, cols].astype(F32), axis=0, keepdims=True)
+
+    far = [(n, j) for j in range(1, second) for n in range(first)]
+    near = [(n, 0) for n in range(first)]
+    for k, (n, j) in enumerate(far + near[:1]):
         terms(scatter.terms(n, j))
         scatter.give(n, j)
-        if k >= 1 and work[k - 1][1] > 0:
-            scatter.cross_over(*work[k - 1])
-
+        if 1 <= k <= len(far):
+            scatter.cross_over(*far[k - 1])
     if place.pair:
-        spot.arrived(y_flat, flat_recv.at[0])
-        stage[0, 0:8] = flat_ref[0:8] + y_flat[...]
-    else:
-        stage[0, 0:8] = flat_ref[0:8]
-    stage[0, 8:] = flat_ref[8:]
+        loads[0].wait()
+        for load in loads[1:]:
+            load.start()
+        token_gradient(1 - me, dg_send)
+        send(dg_send, dg_buf, dg_sem.at[0], dg_sem.at[1], index, 1 - me)
+    for n, j in near[1:]:
+        terms(scatter.terms(n, j))
+        scatter.give(n, j)
+    scatter.chain(acc, range(1))
+    if place.pair:
+        token_gradient(me, dg_ref)
+
     send(stage.at[0], core_flat, flat_send.at[1], flat_recv.at[1], spot.sibling)
     spot.arrived(core_flat, flat_recv.at[1])
     stage[1] = stage[0] + core_flat[...]
@@ -989,7 +1003,7 @@
     for j in range(1, second):
         send(stage.at[1], x_flat.at[b], flat_send.at[1 + j], flat_recv.at[2 + b], spot.at(a, spot.aside(j), c))
 
-    scatter.chain(acc)
+    scatter.chain(acc, range(1, first))
     for j in range(1, second):
         spot.arrived(x_flat.at[spot.aside(j)], flat_recv.at[2 + spot.aside(j)])
     total = x_flat[0]
@@ -1004,8 +1018,9 @@
         )
 
     if place.pair:
-        swap.finish()
-        here = hidden_ref.shape[1]
+        for load in loads[1:]:
+            load.wait()
+        spot.arrived(dg_buf, dg_sem.at[1])
         size = 128
 
         def token_rows(step, carry):
@@ -1014,11 +1029,11 @@
             full = pl.ds(pl.multiple_of(me * here + cut * size, size), size)
             hid = hidden_ref[seq, mine].astype(F32)
             inv = lax.rsqrt(jnp.mean(hid * hid, axis=-1, keepdims=True) + epsilon)
-            gain = (dg_ref[seq, full].astype(F32) + dg_buf[seq, mine].astype(F32)) * gain_ref[...]
+            gain = (dg_ref[seq, mine].astype(F32) + dg_buf[seq, mine].astype(F32)) * gain_ref[...]
             pull = inv * inv * inv * jnp.mean(hid * gain, axis=-1, keepdims=True)
             gh_ref[seq, mine] = (cot_ref[seq, mine].astype(F32) + inv * gain - hid * pull).astype(BF)
             rms = compact([back_ref[seq, :, full]])[:, 0:1]
-            mixed = y_ref[seq, full].astype(F32) + y_away[seq, mine].astype(F32)
+            mixed = keep_ref[seq, mine].astype(F32) + away_ref[seq, mine].astype(F32)
             output_ref[seq, mine] = (hid + rms * mixed).astype(BF)
             return carry
 
@@ -1027,30 +1042,34 @@
         gh_ref[...] = jnp.zeros_like(gh_ref)
         output_ref[...] = jnp.zeros_like(output_ref)
 
-    scatter.finish_chain()
-    if place.pair:
-        edge = own_ref.shape[1] - 128 - 2 * STATE
-        bc_send[...] = own_ref[:, edge : edge + 2 * STATE]
-        swap_bc = spot.copy(bc_send, bc_buf, bc_sem.at[0], bc_sem.at[1], index, 1 - me)
-        swap_bc.start()
     for i in range(1, first):
         spot.arrived(z_flat.at[spot.around(i)], flat_recv.at[2 + second + spot.around(i)])
     total = z_flat[0]
     for i in range(1, first):
         total = total + z_flat[i]
     sum_ref[...] = total
+    if place.pair:
+        stage[3, 0:8] = total[0:8]
+        send(stage.at[3, 0:8], y_flat, flat_send.at[0], flat_recv.at[0], index, 1 - me)
+    scatter.finish_chain()
+    if place.pair:
+        edge = own_ref.shape[1] - 128 - 2 * STATE
+        bc_send[...] = own_ref[:, edge : edge + 2 * STATE]
+        send(bc_send, bc_buf, dg_sem.at[2], dg_sem.at[3], index, 1 - me)
     scatter.wait_sends()
+    if place.pair:
+        spot.arrived(y_flat, flat_recv.at[0])
+        sum_ref[0:8] = stage[3, 0:8] + y_flat[...]
+        spot.arrived(bc_buf, dg_sem.at[3])
+        own_ref[:, edge : edge + 2 * STATE] = bc_send[...] + bc_buf[...]
     for copy in started:
         copy.wait_send()
-    if place.pair:
-        swap_bc.wait()
-        own_ref[:, edge : edge + 2 * STATE] = bc_send[...] + bc_buf[...]
 
 
 def last_kernel(
     heads, own_ref, sum_ref, gh_in, output_in, out_rows, gain_ref,
-    output_ref, gh_ref, pre_ref, zx_ref, bc_ref, step_ref, cxw_ref, cxb_ref, cbw_ref, cbb_ref, head_ref, ngain_ref,
-    out_ref,
+    output_ref, gh_ref, pre_ref, zx_ref, bc_ref, step_ref, cxw_ref, cxb_ref, cbw_ref, cbb_ref, bias_ref, decay_ref,
+    skip_ref, ngain_ref, out_ref,
 ):
     inner = heads * HEADDIM
     wide = 2 * inner
@@ -1069,9 +1088,9 @@
     cbw_ref[...] = sum_ref[0:TAPS, 0 : 2 * STATE]
     cbb_ref[...] = sum_ref[TAPS : TAPS + 1, 0 : 2 * STATE]
     skip = exact_dot(jnp.broadcast_to(sum_ref[13:14, 0:inner], (16, inner)), collector(inner, 0))
-    head_ref[0:1] = sum_ref[15:16, 0:heads]
-    head_ref[1:2] = sum_ref[15:16, 128 : 128 + heads]
-    head_ref[2:3] = skip[0:1, 0:heads]
+    bias_ref[...] = sum_ref[15:16, 0:heads]
+    decay_ref[...] = sum_ref[15:16, 128 : 128 + heads]
+    skip_ref[...] = skip[0:1, 0:heads]
     ngain_ref[...] = sum_ref[14:15, 0:inner]
     out_ref[...] = out_rows[...]
 
@@ -1098,14 +1117,14 @@
     return [DMA((blocks,)), DMA((blocks,)), DMA((columns,)), DMA((columns,)), DMA((place.first * cuts,)), DMA((lines,))]
 
 
-def gather_all(place, size, zx, bc, step_t, hidden, gain, cxw, cxb, cbw, cbb, head, ngain, seg, pad):
+def gather_all(place, size, zx, bc, step_t, hidden, gain, cxw, cxb, cbw, cbb, bias, decay, skip, ngain, seg, pad):
     seqs, here, width = hidden.shape
-    heads, inner = head.shape[1], cxw.shape[1]
+    heads, inner = bias.shape[1], cxw.shape[1]
     total = 2 * inner + 2 * STATE + 128
     rows = zx.shape[0]
     return pl.pallas_call(
         functools.partial(gather_kernel, place, heads),
-        in_specs=[WHOLE] * 13,
+        in_specs=[WHOLE] * 15,
         out_specs=[ANY, ANY] + [WHOLE] * 4,
         out_shape=[
             SDS((size * rows, total), BF), SDS((seqs, place.length if place.pair else here, width), BF),
@@ -1117,7 +1136,7 @@
         ],
         compiler_params=params(0),
         name="gather_all",
-    )(zx, bc, step_t, hidden, gain, cxw, cxb, cbw, cbb, head, ngain, seg, pad)
+    )(zx, bc, step_t, hidden, gain, cxw, cxb, cbw, cbb, bias, decay, skip, ngain, seg, pad)
 
 
 def mixer_forward(place, size, tok, weights, aux, cw, cbw, hp, cot_own, out_own):
@@ -1157,121 +1176,107 @@
     )(tok, weights, aux, cw, cbw, hp, cot_own, out_own)
 
 
-def out_project(place, inner_all, gn, cot, out_all, stat):
-    seqs, length, inner = gn.shape
-    width = cot.shape[2]
-    token = lambda last: pl.BlockSpec((1, BLOCK, last), lambda s, c: (s, c, 0))
-    row = pl.BlockSpec((1, 8, BLOCK), lambda s, c: (s, 0, c))
-    shape = (seqs, 8, length)
-    return pl.pallas_call(
-        functools.partial(out_kernel, place, inner_all),
-        grid=(seqs, length // BLOCK),
-        in_specs=[token(inner), token(width), whole_once(*out_all.shape), row],
-        out_specs=[token(width), pl.BlockSpec(shape, lambda s, c: (0, 0, 0))],
-        out_shape=[SDS((seqs, length, width), BF), SDS(shape, F32)],
-        scratch_shapes=[pltpu.VMEM(shape, F32), pltpu.VMEM(shape, F32), DMA((2,))],
-        compiler_params=params(2 if place.pair else None),
-        name="out_project",
-    )(gn, cot, out_all, stat)
-
-
 def mixer_backward(
-    place, size, pz, raw, aux, cot, mixed, cv, pre, cbc, pbc, st, stat, cw, cbw, hp, out_all, weights, tok, y, gn
+    place, size, inner_all, pz, raw, aux, mixed, cv, pre, cbc, pbc, st, stat, cw, cbw, hp, g, out_all, gn, cot
 ):
-    seqs, length, width = cot.shape
-    heads, inner = hp.shape[1], cw.shape[1]
+    seqs, length, inner = mixed.shape
+    width, wide = out_all.shape[0], pz.shape[2] + 128
+    heads = hp.shape[1]
     last = length // BLOCK - 1
-    here = length // 2 if place.pair else 16
+    pair = place.pair
+    here = length // 2 if pair else 16
     rows = width // size
     tokens = seqs * length
-    fused = place.fused
     token = lambda size: pl.BlockSpec((1, BLOCK, size), lambda s, c: (s, last - c, 0))
     row = lambda high: pl.BlockSpec((1, high, BLOCK), lambda s, c: (s, 0, last - c))
     fixed = lambda *shape: pl.BlockSpec(shape, lambda s, c: (0,) * len(shape))
-    gn_all, cot_all = (gn, cot) if fused else (gn[:1, :16], cot[:1, :16])
-    gn_all, cot_all = gn_all.reshape(-1, inner), cot_all.reshape(-1, width)
+    if pair:
+        g = cbw
+        gn_all, cot_all = gn.reshape(-1, inner), cot.reshape(-1, width)
+    else:
+        gn_all, cot_all, out_all = gn[0, :16, :128], cot[0, :16, :128], out_all[:16, :128]
     blocks = place.first * place.second
     columns = place.first * max(place.second - 1, 1)
-    rs = lambda count: pltpu.VMEM((count, rows, inner) if fused else (1, 16, 128), BF)
+    tile = lambda *shape: pltpu.VMEM(shape if pair else (1,) * (len(shape) - 2) + (16, 128), BF)
+    rowed = pltpu.VMEM((seqs, 8, length), F32)
     return pl.pallas_call(
-        functools.partial(backward_kernel, place, heads),
+        functools.partial(backward_kernel, place, heads, inner_all),
         grid=(seqs, length // BLOCK),
         in_specs=[
-            token(pz.shape[2]), row(heads), row(AUX), token(width), token(inner), token(inner),
+            token(pz.shape[2]), row(heads), row(AUX), token(inner), token(inner),
             token(inner), token(2 * STATE), token(2 * STATE),
-            pl.BlockSpec((1, BLOCK // CHUNK, STATE, inner), lambda s, c: (s, last - c, 0, 0)), row(8),
+            pl.BlockSpec((1, BLOCK // CHUNK, STATE, inner), lambda s, c: (s, last - c, 0, 0)), whole_once(*stat.shape),
             whole_once(8, inner), whole_once(8, 2 * STATE), whole_once(2, heads, 128),
-            whole_once(*out_all.shape), whole_once(*weights.shape), token(width), ANY,
-            whole_once(*gn_all.shape), whole_once(*cot_all.shape), whole_once(*stat.shape),
+            whole_once(*g.shape) if pair else token(inner),
+            whole_once(*out_all.shape), whole_once(*gn_all.shape), whole_once(*cot_all.shape),
         ],
-        out_specs=[token(weights.shape[1]), token(width), fixed(16, width), ANY, fixed(rows, inner)],
+        out_specs=[token(wide), fixed(16, width), ANY, ANY, fixed(seqs, 8, length), fixed(rows, inner)],
         out_shape=[
-            SDS((seqs, length, weights.shape[1]), BF), SDS((seqs, length, width), BF), SDS((16, width), F32),
-            SDS((seqs, here, width), BF), SDS((rows, inner), F32),
+            SDS((seqs, length, wide), BF), SDS((16, width), F32), SDS((seqs, here, width), BF),
+            SDS((seqs, here, width), BF), SDS((seqs, 8, length), F32), SDS((rows, inner), F32),
         ],
         scratch_shapes=[
-            pltpu.VMEM((BLOCK, inner), F32),
             pltpu.VMEM((STATE, inner), F32), pltpu.VMEM((CHUNK + HALO, inner), F32),
             pltpu.VMEM((CHUNK + HALO, 2 * STATE), F32), pltpu.VMEM((CHUNK, inner), BF),
             pltpu.VMEM((CHUNK, inner), BF), pltpu.VMEM((CHUNK, inner), BF), pltpu.VMEM((CHUNK, inner), BF),
             pltpu.VMEM((CHUNK, inner), F32),
             pltpu.VMEM((3, 256, inner), BF), pltpu.VMEM((2, inner, 128), BF),
             pltpu.VMEM((CHUNK, CHUNK), BF), pltpu.VMEM((CHUNK, CHUNK), BF), pltpu.VMEM((2, heads, 128), F32),
-            pltpu.VMEM((tokens, inner) if fused else (16, 128), BF),
-            pltpu.VMEM((width, inner) if fused else (16, 128), BF),
-            rs(blocks), rs(columns), rs(place.first),
-        ] + line_sems(place, 1, place.first) + [DMA((2,))],
-        compiler_params=params(3 if place.fused or place.pair else None),
+            tile(seqs, length, width), tile(tokens, inner), pltpu.VMEM((tokens, 128), F32), rowed, rowed,
+            tile(tokens, inner), tile(width, inner),
+            tile(blocks, rows, inner), tile(columns, rows, inner), tile(place.first, rows, inner),
+        ] + line_sems(place, 1, place.first) + [DMA((3,)), DMA((2,))],
+        compiler_params=params(3 if pair else None),
         name="mixer_backward",
     )(
-        pz, raw, aux, cot, mixed, cv, pre, cbc, pbc, st, stat, cw, cbw, hp, out_all, weights, tok, y,
-        gn_all, cot_all, stat,
+        pz, raw, aux, mixed, cv, pre, cbc, pbc, st, stat, cw, cbw, hp, g, out_all, gn_all, cot_all,
     )
 
 
-def reduce_all(place, size, tok, ge, flat, dg, hidden, cot_own, gain, y, y_away, back):
+def reduce_all(place, size, tok, ge, flat, gain, back, weights, hidden, cot_own, y_keep, y_away):
     seqs, length, depth = tok.shape
     width = ge.shape[2]
     rows = depth // size
-    if place.fused:
+    pair = place.pair
+    if pair:
         tok, ge = tok.reshape(seqs * length, depth), ge.reshape(seqs * length, width)
     else:
         ge = jnp.einsum("stp,sty->py", tok, ge, preferred_element_type=F32).astype(BF)
-        tok = tok[0, :16]
-    if not place.pair:
+        tok, weights = tok[0, :16], weights[:16, :128]
         flat = jnp.concatenate([lax.psum(flat[:8], "tensor"), flat[8:]])
-        dg, hidden, cot_own, y, y_away = [jnp.zeros((1, 16, depth), BF)] * 5
+        hidden, cot_own, y_keep, y_away = [jnp.zeros((1, 16, depth), BF)] * 4
         back = back[:1, :, :128]
     blocks = place.first * place.second * PIECES
     columns = place.first * max(place.second - 1, 1) * PIECES
     lines = 2 * place.first * PIECES
     cut = rows // PIECES
+    tokens = pltpu.VMEM(hidden.shape, BF)
+    small = pltpu.VMEM((rows, 2 * STATE), F32)
     own, flat, gh, output = pl.pallas_call(
         functools.partial(reduce_kernel, place),
-        in_specs=[WHOLE] * 10,
+        in_specs=[WHOLE] * 5 + [ANY] * 5,
         out_specs=[WHOLE] * 4,
         out_shape=[SDS((rows, width), F32), SDS(flat.shape, F32), SDS(hidden.shape, BF), SDS(hidden.shape, BF)],
         scratch_shapes=[
-            pltpu.VMEM((depth, width) if place.fused else (16, 128), BF),
+            pltpu.VMEM(weights.shape, BF), tokens, tokens, tokens, tokens, tokens, tokens, tokens,
+            pltpu.VMEM((depth, width) if pair else (16, 128), BF),
             pltpu.VMEM((blocks, cut, width), BF),
             pltpu.VMEM((columns, cut, width), BF),
             pltpu.VMEM((lines, cut, width), BF),
             pltpu.VMEM((cut, width), F32),
-            pltpu.VMEM(hidden.shape, BF),
-            pltpu.VMEM((rows, 2 * STATE), F32),
-            pltpu.VMEM((rows, 2 * STATE), F32),
+            small, small,
             pltpu.VMEM((8, flat.shape[1]), F32),
             pltpu.VMEM(flat.shape, F32),
             pltpu.VMEM((place.second,) + flat.shape, F32),
             pltpu.VMEM((place.first,) + flat.shape, F32),
-            pltpu.VMEM((3,) + flat.shape, F32),
+            pltpu.VMEM((4,) + flat.shape, F32),
         ] + line_sems(place, PIECES, lines) + [
-            DMA((1 + place.first + place.second,)), DMA((2 + place.first + place.second,)), DMA((2,)), DMA((2,)),
+            DMA((1 + place.first + place.second,)), DMA((2 + place.first + place.second,)), DMA((4,)), DMA((5,)),
         ],
         compiler_params=params(4),
         name="reduce_all",
-    )(tok, ge, flat, dg, hidden, cot_own, gain, y, y_away, back)
-    if not place.pair:
+    )(tok, ge, flat, gain, back, weights, hidden, cot_own, y_keep, y_away)
+    if not pair:
         edge = width - 128 - 2 * STATE
         own = own.at[:, edge : edge + 2 * STATE].set(lax.psum(own[:, edge : edge + 2 * STATE], "tensor"))
     return own, flat, gh, output
@@ -1287,13 +1292,13 @@
     seqs, here, width = hidden.shape
     length = segment_ids.shape[1]
     first, second = factors(size)
-    place = Place(first, second, n == 2, (2 * width // size) % 128 == 0, seqs * length // BLOCK, length)
+    place = Place(first, second, n == 2 and (2 * width // size) % 128 == 0, seqs * length // BLOCK, length)
     line = lambda vector: vector.reshape(1, -1)
     gain = line(pre_gain)
 
     weights, tok, aux, cw, cbw, hp = gather_all(
         place, size, zx_weight, bc_weight, step_weight.T, hidden, gain, conv_x_weight, line(conv_x_bias),
-        conv_bc_weight, line(conv_bc_bias), jnp.stack([step_bias, decay_log, skip_gain]), line(norm_gain),
+        conv_bc_weight, line(conv_bc_bias), line(step_bias), line(decay_log), line(skip_gain), line(norm_gain),
         segment_ids, pad_mask,
     )
     if not place.pair:
@@ -1303,44 +1308,49 @@
     )
     if not place.pair:
         cot = lax.all_gather(grad_out, "tensor", axis=1, tiled=True)
-    y, back = out_project(place, inner * n, gn, cot, out_all, stat)
+    g = y = None
     if not place.pair:
-        back = finish_sums(lax.psum(back, "tensor"), inner * n)
-    ge, dg, flat, y_away, out_rows = mixer_backward(
-        place, size, pz, raw, aux, cot, mixed, cv, pre, cbc, pbc, st, back, cw, cbw, hp, out_all, weights, tok, y, gn
+        y = jnp.einsum("stc,rc->str", gn, out_all, preferred_element_type=F32)
+        cross = jnp.sum(y * cot.astype(F32), axis=-1)
+        stat = finish_sums(lax.psum(stat.at[:, 1].set(cross), "tensor"), inner * n)
+        g = jnp.einsum("str,rc->stc", cot, out_all, preferred_element_type=F32).astype(BF)
+    ge, flat, y_keep, y_away, back, out_rows = mixer_backward(
+        place, size, inner * n, pz, raw, aux, mixed, cv, pre, cbc, pbc, st, stat, cw, cbw, hp, g, out_all, gn, cot
     )
-    if not place.fused:
+    if not place.pair:
         normed_out = (gn.astype(F32) * back[:, 0, :, None]).astype(BF)
         terms = jnp.einsum("str,stc->rc", cot, normed_out, preferred_element_type=F32).astype(BF)
         out_rows = lax.psum_scatter(terms, "dp", scatter_dimension=0, tiled=True).astype(F32)
+        dg = jnp.einsum("sty,py->stp", ge, weights, preferred_element_type=F32)
+        flat = flat.at[5].add(jnp.sum(dg * tok.astype(F32), axis=(0, 1)))
     own, sums, grad_hidden, output = reduce_all(
-        place, size, tok, ge, flat, dg, hidden, grad_out, gain, y, y_away, back
+        place, size, tok, ge, flat, gain, back, weights, hidden, grad_out, y_keep, y_away
     )
     if not place.pair:
         hidden_f = hidden.astype(F32)
         inv_rms = lax.rsqrt(jnp.mean(hidden_f * hidden_f, axis=-1, keepdims=True) + epsilon)
-        scatter = lambda rows: lax.psum_scatter(rows.astype(F32), "tensor", scatter_dimension=1, tiled=True)
+        scatter = lambda rows: lax.psum_scatter(rows, "tensor", scatter_dimension=1, tiled=True)
         gain_grad = scatter(dg) * pre_gain
         pull = inv_rms**3 * jnp.mean(hidden_f * gain_grad, axis=-1, keepdims=True)
         grad_hidden = (grad_out.astype(F32) + inv_rms * gain_grad - hidden_f * pull).astype(BF)
-        output = (hidden_f + scatter(y.astype(F32) * back[:, 0, :, None])).astype(BF)
+        output = (hidden_f + scatter(y * back[:, 0, :, None])).astype(BF)
     rows = own.shape[0]
-    output, grad_hidden, grad_pre, gzx, gbc, gstep, gcxw, gcxb, gcbw, gcbb, ghead, gnorm, gout = pl.pallas_call(
+    output, grad_hidden, grad_pre, gzx, gbc, gstep, gcxw, gcxb, gcbw, gcbb, gbias, gdecay, gskip, gnorm, gout = pl.pallas_call(
         functools.partial(last_kernel, heads),
         in_specs=[WHOLE] * 6,
-        out_specs=[WHOLE] * 13,
+        out_specs=[WHOLE] * 15,
         out_shape=[
             SDS(hidden.shape, BF), SDS(hidden.shape, BF), SDS((1, width), F32), SDS((rows, 2 * inner), F32),
             SDS((rows, 2 * STATE), F32), SDS((heads, rows), F32), SDS((TAPS, inner), F32), SDS((1, inner), F32),
-            SDS((TAPS, 2 * STATE), F32), SDS((1, 2 * STATE), F32), SDS((3, heads), F32), SDS((1, inner), F32),
-            SDS((rows, inner), F32),
+            SDS((TAPS, 2 * STATE), F32), SDS((1, 2 * STATE), F32), SDS((1, heads), F32), SDS((1, heads), F32),
+            SDS((1, heads), F32), SDS((1, inner), F32), SDS((rows, inner), F32),
         ],
         compiler_params=params(),
         name="outputs",
     )(own, sums, grad_hidden, output, out_rows, gain)
     return (
-        output, grad_hidden, grad_pre[0], gzx, gbc, gstep.T, gcxw, gcxb[0], gcbw, gcbb[0], ghead[0], ghead[1], ghead[2],
-        gnorm[0], gout.T,
+        output, grad_hidden, grad_pre[0], gzx, gbc, gstep.T, gcxw, gcxb[0], gcbw, gcbb[0], gbias[0], gdecay[0],
+        gskip[0], gnorm[0], gout.T,
     )
 
 

time: 193 us -> 175 us (0.907)
  Pallas kernels: 190 us -> 174 us
    pallas_call x2 -> x1, Pallas kernels: 65.7 us -> 48.6 us  [mixer_backward(): pl.pallas_call(functools.partial(backward_kernel, place, heads, inner_all...]
where the time goes in v5:
time: 175 us; the launch traced here: 174 us
  Pallas kernels  174 us (99%)
    pallas_call x1, Pallas kernels, reduce_all(): pl.pallas_call(functools.partial(reduce_kernel, place), in_specs=[WHOLE]...  49.7 us
    pallas_call x1, Pallas kernels, mixer_backward(): pl.pallas_call(functools.partial(backward_kernel, place, heads, inner_all...  48.6 us
    pallas_call x1, Pallas kernels, gather_all(): pl.pallas_call(functools.partial(gather_kernel, place, heads), in_specs=[...  39.6 us
    pallas_call x1, Pallas kernels, mixer_forward(): pl.pallas_call(functools.partial(forward_kernel, place, heads), grid=(seq...  32.2 us
    pallas_call x1, Pallas kernels, body(): pl.pallas_call(functools.partial(last_kernel, heads), in_specs=[WHOLE] *...  3.59 us

profile of v5, /device:TPU:0, one launch (start us, length us, event | category | flops | bytes accessed | tf_op | source)
XLA Modules:
  0.0 174.4 jit_solution(5808218692154568171)
XLA Ops:
  0.7 39.6 %gather_all.1 = (bf16[1024,2432]{1,0:T(8,128)(2,1)}, bf16[1,1024,1024]{2,1,0:T(8,128)(2,1)}, f32[1,16,1024]{2,1,0:T(8,128)}, f32[8,1024]{1,0:T(8,128)}, f32[8,256]{1,0:T(8,128)}, /*index=5*/f32[2,16,128]{2,1,0:T(8,128)}) custom-call(bf16[64,2048]{1,0:T(8,128)(2,1)} %zx_ref.1, bf16[64,256]{1,0:T(8,128)(2,1)} %bc_ref.1, bf16[16,64]{1,0:T(8,128)(2,1)} %bitcast.30, ...), custom_call_target="tpu_custom_call" | custom-call | tf_op jit(solution)/shard_map/gather_all/pallas_call | solution.py:1125
  40.2 32.2 %mixer_forward.1 = (bf16[1,1024,2304]{2,1,0:T(8,128)(2,1)}, f32[1,16,1024]{2,1,0:T(8,128)}, bf16[1,1024,1024]{2,1,0:T(8,128)(2,1)}, bf16[1,1024,1024]{2,1,0:T(8,...) custom-call(bf16[1,1024,1024]{2,1,0:T(8,128)(2,1)} %get-tuple-elemen, ...), custom_call_target="tpu_custom_call" | custom-call | tf_op jit(solution)/shard_map/mixer_forward/pallas_call | solution.py:1149
  72.4 48.6 %mixer_backward.1 = (bf16[1,1024,2432]{2,1,0:T(8,128)(2,1)}, f32[16,1024]{1,0:T(8,128)}, bf16[1,512,1024]{2,1,0:T(8,128)(2,1)}, bf16[1,512,1024]{2,1,0:T(8,128)(...) custom-call(bf16[1,1024,2304]{2,1,0:T(8,128)(2,1)} %get-tuple-element.64.pz_ref, ...), custom_call_target="tpu_custom_call" | custom-call | tf_op jit(solution)/shard_map/mixer_backward/pallas_call | solution.py:1202
  121.0 49.7 %reduce_all.1 = (f32[64,2432]{1,0:T(8,128)}, f32[16,1024]{1,0:T(8,128)}, bf16[1,512,1024]{2,1,0:T(8,128)(2,1)}, bf16[1,512,1024]{2,1,0:T(8,128)(2,1)}) custom-call(bf16[1024,1024]{1,0:T(8,128)(2,1)} %bitcast.22, bf16[1024,2432]{1,0:T(8,128)(2,1)} %bitcast.23, f32[16,1024]{1,0:T(8,128)} %get-tuple-element.77.flat_ref, f32[1,1024]{1,0:T(1,128)} %bitcast.28, ...), custom_call_target="tpu_custom_call" | custom-call | tf_op jit(solution)/shard_map/reduce_all/pallas_call | solution.py:1255
  170.8 3.6 %outputs.1 = (bf16[1,512,1024]{2,1,0:T(8,128)(2,1)}, bf16[1,512,1024]{2,1,0:T(8,128)(2,1)}, f32[1,1024]{1,0:T(1,128)}, f32[64,2048]{1,0:T(8,128)}, f32[64,256]{1...) custom-call(f32[64,2432]{1,0:T(8,128)} %get-tuple-element.81.own_ref, ...), custom_call_target="tpu_custom_call" | custom-call | tf_op jit(solution)/shard_map/outputs/pallas_call | solution.py:1338

commit v6 on v5

--- a/solution.py
+++ b/solution.py
@@ -157,16 +157,22 @@
     return (2 + second) + (first - 1) * 2 * (1 + second) + (2 * first - 1) * (second - 1)
 
 
+def row_sites(first, second):
+    return (2 + second) + 3 * (second - 1) + (first - 1) * 4 * second
+
+
 class LineGather:
-    def __init__(self, spot, arrays, send_sem, recv_sem, local_sem):
-        self.spot, self.arrays = spot, arrays
+    def __init__(self, spot, arrays, send_sem, recv_sem, local_sem, columns=None, part=0, parts=1):
+        self.spot, self.arrays, self.columns = spot, arrays, columns
+        self.part, self.parts = part, parts
         self.send_sem, self.recv_sem, self.local_sem = send_sem, recv_sem, local_sem
         self.sites = []
 
     def rows(self, which, shard):
         own, full = self.arrays[which]
         rows = own.shape[0]
-        return full.at[pl.ds(pl.multiple_of(shard * rows, rows), rows)]
+        there = pl.ds(pl.multiple_of((shard * self.parts + self.part) * rows, rows), rows)
+        return full.at[there] if self.columns is None else full.at[there, self.columns]
 
     def copies(self, site, shard, target, mine=False):
         return [
@@ -246,6 +252,26 @@
             )
         for copy in self.local():
             copy.wait()
+
+
+class RowGather(LineGather):
+    def cross(self):
+        s = self.spot
+        for j in range(1, s.second):
+            shard = lambda j=j: s.at(s.a, s.aside(j), s.c)
+            self.arrive(None, shard())
+            self.send(lambda: s.a < s.first - 1, shard, lambda: s.at(s.a + 1, s.b, s.c))
+            self.send(lambda: s.a > 0, shard, lambda: s.at(s.a - 1, s.b, s.c))
+            self.send(None, shard, lambda: s.sibling)
+
+    def along(self, hop):
+        s = self.spot
+        for j in range(s.second):
+            for valid, origin, onward, target in self.sides(hop):
+                shard = lambda origin=origin, j=j: s.at(origin(), s.aside(j), s.c)
+                self.arrive(valid(), shard())
+                self.send(lambda valid=valid, onward=onward: valid() & onward(), shard, target)
+                self.send(valid, shard, lambda: s.sibling)
 
 
 class TokenSwap:
@@ -843,7 +869,7 @@
     place, heads, zx_ref, bc_ref, step_ref, hidden_ref, gain_ref, cxw_ref, cxb_ref, cbw_ref, cbb_ref, bias_ref, decay_ref,
     skip_ref, ngain_ref, seg_ref, pad_ref,
     w_all, tok_full, aux_ref, cw_ref, cbw_out, hp_ref,
-    shard, tok_own, square, send_sem, recv_sem, local_sem, tok_sem,
+    shard, tok_own, square, send_sem, recv_sem, local_sem, side_send, side_recv, side_local, tok_sem,
 ):
     inner = heads * HEADDIM
     wide = 2 * inner
@@ -855,8 +881,19 @@
     square[0:heads, 0:rows] = step_ref[...].astype(F32)
     shard[:, wide + 2 * STATE :] = square[...].T[0:rows].astype(BF)
     spot.greet(place.pair)
-    gather = LineGather(spot, [(shard, w_all)], send_sem, recv_sem, local_sem)
-    gather.begin()
+    main, other = slice(0, wide), slice(wide, wide + 2 * STATE + 128)
+    half = rows // PIECES
+    gathers = [
+        LineGather(
+            spot, [(shard.at[half * q : half * q + half, main], w_all)],
+            send_sem.at[q], recv_sem.at[q], local_sem.at[q], main, q, PIECES,
+        )
+        for q in range(PIECES)
+    ]
+    side = RowGather(spot, [(shard.at[:, other], w_all)], side_send, side_recv, side_local, other)
+    for gather in gathers:
+        gather.begin()
+    side.begin()
 
     size = 64
     seqs, here = hidden_ref.shape[0], hidden_ref.shape[1]
@@ -913,13 +950,18 @@
             aux_ref[seq, 6:7, cut] = flag(block == tail)
             before = tail
 
-    gather.across(0) if place.first == 1 else None
     for hop in range(1, place.first):
-        gather.along(hop)
-        gather.across(hop - 1)
-    if place.first > 1:
+        for gather in gathers:
+            gather.along(hop)
+        side.cross() if hop == 1 else side.along(hop - 1)
+        for gather in gathers:
+            gather.across(hop - 1)
+    side.along(place.first - 1) if place.first > 1 else side.cross()
+    for gather in gathers:
         gather.across(place.first - 1)
-    gather.finish()
+    for gather in gathers:
+        gather.finish()
+    side.finish()
     swap.finish() if place.pair else copy.wait()
 
 
@@ -996,26 +1038,30 @@
     if place.pair:
         token_gradient(me, dg_ref)
 
-    send(stage.at[0], core_flat, flat_send.at[1], flat_recv.at[1], spot.sibling)
-    spot.arrived(core_flat, flat_recv.at[1])
-    stage[1] = stage[0] + core_flat[...]
-    x_flat[b] = stage[1]
+    z_flat[a] = stage[0]
+    for i in range(1, first):
+        send(
+            stage.at[0], z_flat.at[a], flat_send.at[second + i], flat_recv.at[2 + second + a],
+            spot.at(spot.around(i), b, c),
+        )
+    scatter.chain(acc, range(1, min(2, first)))
+    for i in range(1, first):
+        spot.arrived(z_flat.at[spot.around(i)], flat_recv.at[2 + second + spot.around(i)])
+    total = z_flat[0]
+    for i in range(1, first):
+        total = total + z_flat[i]
+    stage[1] = total
+    x_flat[b] = total
     for j in range(1, second):
         send(stage.at[1], x_flat.at[b], flat_send.at[1 + j], flat_recv.at[2 + b], spot.at(a, spot.aside(j), c))
-
-    scatter.chain(acc, range(1, first))
+    scatter.chain(acc, range(2, first))
     for j in range(1, second):
         spot.arrived(x_flat.at[spot.aside(j)], flat_recv.at[2 + spot.aside(j)])
     total = x_flat[0]
     for j in range(1, second):
         total = total + x_flat[j]
     stage[2] = total
-    z_flat[a] = total
-    for i in range(1, first):
-        send(
-            stage.at[2], z_flat.at[a], flat_send.at[second + i], flat_recv.at[2 + second + a],
-            spot.at(spot.around(i), b, c),
-        )
+    send(stage.at[2], core_flat, flat_send.at[1], flat_recv.at[1], spot.sibling)
 
     if place.pair:
         for load in loads[1:]:
@@ -1042,11 +1088,8 @@
         gh_ref[...] = jnp.zeros_like(gh_ref)
         output_ref[...] = jnp.zeros_like(output_ref)
 
-    for i in range(1, first):
-        spot.arrived(z_flat.at[spot.around(i)], flat_recv.at[2 + second + spot.around(i)])
-    total = z_flat[0]
-    for i in range(1, first):
-        total = total + z_flat[i]
+    spot.arrived(core_flat, flat_recv.at[1])
+    total = stage[2] + core_flat[...]
     sum_ref[...] = total
     if place.pair:
         stage[3, 0:8] = total[0:8]
@@ -1132,7 +1175,8 @@
         ],
         scratch_shapes=[
             pltpu.VMEM((rows, total), BF), pltpu.VMEM(hidden.shape, BF), pltpu.VMEM((128, 128), F32),
-            DMA((1, gather_sites(place.first, place.second))), DMA((1, size)), DMA((1,)), DMA((3,)),
+            DMA((PIECES, 1, gather_sites(place.first, place.second))), DMA((PIECES, 1, size)), DMA((PIECES, 1)),
+            DMA((1, row_sites(place.first, place.second))), DMA((1, size)), DMA((1,)), DMA((3,)),
         ],
         compiler_params=params(0),
         name="gather_all",

time: 175 us -> 168 us (0.960)
  Pallas kernels: 174 us -> 166 us
    pallas_call x1, Pallas kernels: 49.7 us -> 45.6 us  [reduce_all(): pl.pallas_call(functools.partial(reduce_kernel, place), in_specs=[WHOLE]...]
    pallas_call x1, Pallas kernels: 39.6 us -> 35.8 us  [gather_all(): pl.pallas_call(functools.partial(gather_kernel, place, heads), in_specs=[...]
where the time goes in v6:
time: 168 us; the launch traced here: 167 us
  Pallas kernels  166 us (99%)
    pallas_call x1, Pallas kernels, mixer_backward(): pl.pallas_call(functools.partial(backward_kernel, place, heads, inner_all...  48.8 us
    pallas_call x1, Pallas kernels, reduce_all(): pl.pallas_call(functools.partial(reduce_kernel, place), in_specs=[WHOLE]...  45.6 us
    pallas_call x1, Pallas kernels, gather_all(): pl.pallas_call(functools.partial(gather_kernel, place, heads), in_specs=[...  35.8 us
    pallas_call x1, Pallas kernels, mixer_forward(): pl.pallas_call(functools.partial(forward_kernel, place, heads), grid=(seq...  31.9 us
    pallas_call x1, Pallas kernels, body(): pl.pallas_call(functools.partial(last_kernel, heads), in_specs=[WHOLE] *...  3.6 us

profile of v6, /device:TPU:0, one launch (start us, length us, event | category | flops | bytes accessed | tf_op | source)
XLA Modules:
  0.0 166.6 jit_solution(181959014286914823)
XLA Ops:
  0.7 35.8 %gather_all.1 = (bf16[1024,2432]{1,0:T(8,128)(2,1)}, bf16[1,1024,1024]{2,1,0:T(8,128)(2,1)}, f32[1,16,1024]{2,1,0:T(8,128)}, f32[8,1024]{1,0:T(8,128)}, f32[8,256]{1,0:T(8,128)}, /*index=5*/f32[2,16,128]{2,1,0:T(8,128)}) custom-call(bf16[64,2048]{1,0:T(8,128)(2,1)} %zx_ref.1, bf16[64,256]{1,0:T(8,128)(2,1)} %bc_ref.1, bf16[16,64]{1,0:T(8,128)(2,1)} %bitcast.30, ...), custom_call_target="tpu_custom_call" | custom-call | tf_op jit(solution)/shard_map/gather_all/pallas_call | solution.py:1168
  36.5 31.9 %mixer_forward.1 = (bf16[1,1024,2304]{2,1,0:T(8,128)(2,1)}, f32[1,16,1024]{2,1,0:T(8,128)}, bf16[1,1024,1024]{2,1,0:T(8,128)(2,1)}, bf16[1,1024,1024]{2,1,0:T(8,...) custom-call(bf16[1,1024,1024]{2,1,0:T(8,128)(2,1)} %get-tuple-elemen, ...), custom_call_target="tpu_custom_call" | custom-call | tf_op jit(solution)/shard_map/mixer_forward/pallas_call | solution.py:1193
  68.4 48.8 %mixer_backward.1 = (bf16[1,1024,2432]{2,1,0:T(8,128)(2,1)}, f32[16,1024]{1,0:T(8,128)}, bf16[1,512,1024]{2,1,0:T(8,128)(2,1)}, bf16[1,512,1024]{2,1,0:T(8,128)(...) custom-call(bf16[1,1024,2304]{2,1,0:T(8,128)(2,1)} %get-tuple-element.64.pz_ref, ...), custom_call_target="tpu_custom_call" | custom-call | tf_op jit(solution)/shard_map/mixer_backward/pallas_call | solution.py:1246
  117.2 45.6 %reduce_all.1 = (f32[64,2432]{1,0:T(8,128)}, f32[16,1024]{1,0:T(8,128)}, bf16[1,512,1024]{2,1,0:T(8,128)(2,1)}, bf16[1,512,1024]{2,1,0:T(8,128)(2,1)}) custom-call(bf16[1024,1024]{1,0:T(8,128)(2,1)} %bitcast.22, bf16[1024,2432]{1,0:T(8,128)(2,1)} %bitcast.23, f32[16,1024]{1,0:T(8,128)} %get-tuple-element.77.flat_ref, f32[1,1024]{1,0:T(1,128)} %bitcast.28, ...), custom_call_target="tpu_custom_call" | custom-call | tf_op jit(solution)/shard_map/reduce_all/pallas_call | solution.py:1299
  162.9 3.6 %outputs.1 = (bf16[1,512,1024]{2,1,0:T(8,128)(2,1)}, bf16[1,512,1024]{2,1,0:T(8,128)(2,1)}, f32[1,1024]{1,0:T(1,128)}, f32[64,2048]{1,0:T(8,128)}, f32[64,256]{1...) custom-call(f32[64,2432]{1,0:T(8,128)} %get-tuple-element.81.own_ref, ...), custom_call_target="tpu_custom_call" | custom-call | tf_op jit(solution)/shard_map/outputs/pallas_call | solution.py:1382

commit v7 on v6

--- a/solution.py
+++ b/solution.py
@@ -477,9 +477,9 @@
 
 
 def forward_kernel(
-    place, heads, tok_ref, w_ref, aux_ref, cw_ref, cbw_ref, hp_ref, cot_own, out_own,
+    place, heads, tok_ref, w_hbm, aux_ref, cw_ref, cbw_ref, hp_ref, cot_own, out_own,
     pz_ref, raw_ref, mixed_ref, gated_ref, cv_ref, pre_ref, cbc_ref, pbc_ref, st_ref, stat_ref, out_all, cot_full,
-    state, ubuf, bbuf, vd, yint, expand, tri_ref, send_sem, recv_sem, local_sem, cot_sem,
+    state, ubuf, bbuf, vd, yint, expand, tri_ref, w_ref, send_sem, recv_sem, local_sem, cot_sem, load_sem,
 ):
     inner = heads * HEADDIM
     pairs = heads // 2
@@ -493,10 +493,13 @@
 
     @pl.when(first)
     def _():
+        load = pltpu.make_async_copy(w_hbm, w_ref, load_sem)
+        load.start()
         spot.greet(place.pair)
         gather.begin()
         if swap:
             swap.begin()
+        load.wait()
 
     for hop in range(1, place.first):
 
@@ -610,11 +613,12 @@
 
 def backward_kernel(
     place, heads, inner_all, pz_ref, raw_ref, aux_ref, mixed_ref, cv_ref, pre_ref, cbc_ref, pbc_ref,
-    st_ref, stat_ref, cw_ref, cbw_ref, hp_ref, g_ref, out_ref, gn_all, cot_all,
+    st_ref, stat_ref, cw_ref, cbw_ref, hp_ref, g_ref, out_hbm, gn_hbm, cot_hbm,
     ge_ref, flat_ref, y_keep, y_away, back_ref, grad_rows,
     dstate, cbuf, dbuf, vd, gm_s, gmc_s, ggate_s, bs_s, expand, collect, tri_ref, suf_ref, ghead_ref,
     y_s, g_s, fold, sums, theirs, normed_s, part_buf, core_buf, x_buf, z_buf,
     core_send, core_recv, x_send, x_recv, z_send, z_recv, y_sem, stat_sem,
+    out_ref, gn_all, cot_all, load_sem,
 ):
     inner = heads * HEADDIM
     pairs = heads // 2
@@ -645,7 +649,15 @@
 
         @pl.when(first)
         def _():
+            loads = [
+                pltpu.make_async_copy(far, near, load_sem.at[k])
+                for k, (far, near) in enumerate(((gn_hbm, gn_all), (out_hbm, out_ref), (cot_hbm, cot_all)))
+            ]
+            for load in loads:
+                load.start()
             spot.greet(True)
+            for load in loads:
+                load.wait()
             for cut in range(out_ref.shape[0] // 256):
                 cols = slice(256 * cut, 256 * cut + 256)
                 for seq in range(seqs):
@@ -973,11 +985,11 @@
 
 
 def reduce_kernel(
-    place, tok_ref, ge_ref, flat_ref, gain_ref, back_ref, w_hbm, hidden_hbm, cot_hbm, keep_hbm, away_hbm,
+    place, tok_hbm, ge_hbm, flat_ref, gain_ref, back_ref, w_hbm, hidden_hbm, cot_hbm, keep_hbm, away_hbm,
     own_ref, sum_ref, gh_ref, output_ref,
-    w_ref, hidden_ref, cot_ref, keep_ref, away_ref, dg_ref, dg_send, dg_buf,
+    tok_ref, ge_ref, w_ref, hidden_ref, cot_ref, keep_ref, away_ref, dg_ref, dg_send, dg_buf,
     part_buf, core_buf, x_buf, z_buf, acc, bc_buf, bc_send, y_flat, core_flat, x_flat, z_flat, stage,
-    core_send, core_recv, x_send, x_recv, z_send, z_recv, flat_send, flat_recv, dg_sem, load_sem,
+    core_send, core_recv, x_send, x_recv, z_send, z_recv, flat_send, flat_recv, dg_sem, load_sem, first_sem,
 ):
     spot = Spot(place)
     a, b, c, me, index = spot.a, spot.b, spot.c, spot.me, spot.index
@@ -986,6 +998,11 @@
         spot, part_buf if place.pair else ge_ref, core_buf, x_buf, z_buf, own_ref,
         core_send, core_recv, x_send, x_recv, z_send, z_recv, PIECES,
     )
+    ahead = [
+        pltpu.make_async_copy(ge_hbm, ge_ref, first_sem.at[0]), pltpu.make_async_copy(tok_hbm, tok_ref, first_sem.at[1])
+    ]
+    for load in ahead:
+        load.start()
     loads = []
     if place.pair:
         pairs = ((w_hbm, w_ref), (hidden_hbm, hidden_ref), (cot_hbm, cot_ref), (keep_hbm, keep_ref), (away_hbm, away_ref))
@@ -993,6 +1010,8 @@
             loads.append(pltpu.make_async_copy(far, near, load_sem.at[k]))
         loads[0].start()
     spot.greet(place.pair)
+    for load in ahead:
+        load.wait()
     started = []
 
     def send(*args):
@@ -1194,7 +1213,7 @@
         functools.partial(forward_kernel, place, heads),
         grid=(seqs, length // BLOCK),
         in_specs=[
-            token(width), whole_once(*weights.shape), row(AUX),
+            token(width), ANY, row(AUX),
             whole_once(8, inner), whole_once(8, 2 * STATE), whole_once(2, heads, 128), WHOLE, ANY,
         ],
         out_specs=[
@@ -1213,7 +1232,8 @@
             pltpu.VMEM((STATE, inner), F32), pltpu.VMEM((HALO + CHUNK, inner), F32),
             pltpu.VMEM((HALO + CHUNK, 2 * STATE), F32), pltpu.VMEM((CHUNK, inner), BF),
             pltpu.VMEM((CHUNK, inner), F32), pltpu.VMEM((3, 256, inner), BF), pltpu.VMEM((CHUNK, CHUNK), BF),
-            DMA((1, gather_sites(place.first, place.second))), DMA((1, size)), DMA((1,)), DMA((3,)),
+            pltpu.VMEM(weights.shape, BF),
+            DMA((1, gather_sites(place.first, place.second))), DMA((1, size)), DMA((1,)), DMA((3,)), DMA,
         ],
         compiler_params=params(1),
         name="mixer_forward",
@@ -1252,7 +1272,7 @@
             pl.BlockSpec((1, BLOCK // CHUNK, STATE, inner), lambda s, c: (s, last - c, 0, 0)), whole_once(*stat.shape),
             whole_once(8, inner), whole_once(8, 2 * STATE), whole_once(2, heads, 128),
             whole_once(*g.shape) if pair else token(inner),
-            whole_once(*out_all.shape), whole_once(*gn_all.shape), whole_once(*cot_all.shape),
+            ANY, ANY, ANY,
         ],
         out_specs=[token(wide), fixed(16, width), ANY, ANY, fixed(seqs, 8, length), fixed(rows, inner)],
         out_shape=[
@@ -1269,7 +1289,9 @@
             tile(seqs, length, width), tile(tokens, inner), pltpu.VMEM((tokens, 128), F32), rowed, rowed,
             tile(tokens, inner), tile(width, inner),
             tile(blocks, rows, inner), tile(columns, rows, inner), tile(place.first, rows, inner),
-        ] + line_sems(place, 1, place.first) + [DMA((3,)), DMA((2,))],
+        ] + line_sems(place, 1, place.first) + [DMA((3,)), DMA((2,))] + [
+            pltpu.VMEM(out_all.shape, BF), pltpu.VMEM(gn_all.shape, BF), pltpu.VMEM(cot_all.shape, BF), DMA((3,)),
+        ],
         compiler_params=params(3 if pair else None),
         name="mixer_backward",
     )(
@@ -1298,11 +1320,11 @@
     small = pltpu.VMEM((rows, 2 * STATE), F32)
     own, flat, gh, output = pl.pallas_call(
         functools.partial(reduce_kernel, place),
-        in_specs=[WHOLE] * 5 + [ANY] * 5,
+        in_specs=[ANY] * 2 + [WHOLE] * 3 + [ANY] * 5,
         out_specs=[WHOLE] * 4,
         out_shape=[SDS((rows, width), F32), SDS(flat.shape, F32), SDS(hidden.shape, BF), SDS(hidden.shape, BF)],
         scratch_shapes=[
-            pltpu.VMEM(weights.shape, BF), tokens, tokens, tokens, tokens, tokens, tokens, tokens,
+            pltpu.VMEM(tok.shape, BF), pltpu.VMEM(ge.shape, BF), pltpu.VMEM(weights.shape, BF), tokens, tokens, tokens, tokens, tokens, tokens, tokens,
             pltpu.VMEM((depth, width) if pair else (16, 128), BF),
             pltpu.VMEM((blocks, cut, width), BF),
             pltpu.VMEM((columns, cut, width), BF),
@@ -1315,7 +1337,7 @@
             pltpu.VMEM((place.first,) + flat.shape, F32),
             pltpu.VMEM((4,) + flat.shape, F32),
         ] + line_sems(place, PIECES, lines) + [
-            DMA((1 + place.first + place.second,)), DMA((2 + place.first + place.second,)), DMA((4,)), DMA((5,)),
+            DMA((1 + place.first + place.second,)), DMA((2 + place.first + place.second,)), DMA((4,)), DMA((5,)), DMA((2,)),
         ],
         compiler_params=params(4),
         name="reduce_all",

time: 168 us -> 165 us (0.982)
  Pallas kernels: 166 us -> 163 us
where the time goes in v7:
time: 165 us; the launch traced here: 163 us
  Pallas kernels  163 us (99%)
    pallas_call x1, Pallas kernels, mixer_backward(): pl.pallas_call(functools.partial(backward_kernel, place, heads, inner_all...  48.2 us
    pallas_call x1, Pallas kernels, reduce_all(): pl.pallas_call(functools.partial(reduce_kernel, place), in_specs=[ANY] *...  44.5 us
    pallas_call x1, Pallas kernels, gather_all(): pl.pallas_call(functools.partial(gather_kernel, place, heads), in_specs=[...  35.8 us
    pallas_call x1, Pallas kernels, mixer_forward(): pl.pallas_call(functools.partial(forward_kernel, place, heads), grid=(seq...  30.5 us
    pallas_call x1, Pallas kernels, body(): pl.pallas_call(functools.partial(last_kernel, heads), in_specs=[WHOLE] *...  3.59 us

profile of v7, /device:TPU:0, one launch (start us, length us, event | category | flops | bytes accessed | tf_op | source)
XLA Modules:
  0.0 163.3 jit_solution(17191312711149226202)
XLA Ops:
  0.7 35.8 %gather_all.1 = (bf16[1024,2432]{1,0:T(8,128)(2,1)}, bf16[1,1024,1024]{2,1,0:T(8,128)(2,1)}, f32[1,16,1024]{2,1,0:T(8,128)}, f32[8,1024]{1,0:T(8,128)}, f32[8,256]{1,0:T(8,128)}, /*index=5*/f32[2,16,128]{2,1,0:T(8,128)}) custom-call(bf16[64,2048]{1,0:T(8,128)(2,1)} %zx_ref.1, bf16[64,256]{1,0:T(8,128)(2,1)} %bc_ref.1, bf16[16,64]{1,0:T(8,128)(2,1)} %bitcast.30, ...), custom_call_target="tpu_custom_call" | custom-call | tf_op jit(solution)/shard_map/gather_all/pallas_call | solution.py:1187
  36.5 30.5 %mixer_forward.1 = (bf16[1,1024,2304]{2,1,0:T(8,128)(2,1)}, f32[1,16,1024]{2,1,0:T(8,128)}, bf16[1,1024,1024]{2,1,0:T(8,128)(2,1)}, bf16[1,1024,1024]{2,1,0:T(8,...) custom-call(bf16[1,1024,1024]{2,1,0:T(8,128)(2,1)} %get-tuple-elemen, ...), custom_call_target="tpu_custom_call" | custom-call | tf_op jit(solution)/shard_map/mixer_forward/pallas_call | solution.py:1212
  66.9 48.2 %mixer_backward.1 = (bf16[1,1024,2432]{2,1,0:T(8,128)(2,1)}, f32[16,1024]{1,0:T(8,128)}, bf16[1,512,1024]{2,1,0:T(8,128)(2,1)}, bf16[1,512,1024]{2,1,0:T(8,128)(...) custom-call(bf16[1,1024,2304]{2,1,0:T(8,128)(2,1)} %get-tuple-element.64.pz_ref, ...), custom_call_target="tpu_custom_call" | custom-call | tf_op jit(solution)/shard_map/mixer_backward/pallas_call | solution.py:1266
  115.1 44.5 %reduce_all.1 = (f32[64,2432]{1,0:T(8,128)}, f32[16,1024]{1,0:T(8,128)}, bf16[1,512,1024]{2,1,0:T(8,128)(2,1)}, bf16[1,512,1024]{2,1,0:T(8,128)(2,1)}) custom-call(bf16[1024,1024]{1,0:T(8,128)(2,1)} %bitcast.22, bf16[1024,2432]{1,0:T(8,128)(2,1)} %bitcast.23, f32[16,1024]{1,0:T(8,128)} %get-tuple-element.77.flat_ref, f32[1,1024]{1,0:T(1,128)} %bitcast.28, ...), custom_call_target="tpu_custom_call" | custom-call | tf_op jit(solution)/shard_map/reduce_all/pallas_call | solution.py:1321
  159.7 3.6 %outputs.1 = (bf16[1,512,1024]{2,1,0:T(8,128)(2,1)}, bf16[1,512,1024]{2,1,0:T(8,128)(2,1)}, f32[1,1024]{1,0:T(1,128)}, f32[64,2048]{1,0:T(8,128)}, f32[64,256]{1...) custom-call(f32[64,2432]{1,0:T(8,128)} %get-tuple-element.81.own_ref, ...), custom_call_target="tpu_custom_call" | custom-call | tf_op jit(solution)/shard_map/outputs/pallas_call | solution.py:1404

commit v8 on v7

--- a/solution.py
+++ b/solution.py
@@ -986,10 +986,10 @@
 
 def reduce_kernel(
     place, tok_hbm, ge_hbm, flat_ref, gain_ref, back_ref, w_hbm, hidden_hbm, cot_hbm, keep_hbm, away_hbm,
-    own_ref, sum_ref, gh_ref, output_ref,
-    tok_ref, ge_ref, w_ref, hidden_ref, cot_ref, keep_ref, away_ref, dg_ref, dg_send, dg_buf,
+    own_ref, sum_ref, gh_hbm, output_hbm,
+    gh_ref, output_ref, tok_ref, ge_ref, w_ref, hidden_ref, cot_ref, keep_ref, away_ref, dg_ref, dg_send, dg_buf,
     part_buf, core_buf, x_buf, z_buf, acc, bc_buf, bc_send, y_flat, core_flat, x_flat, z_flat, stage,
-    core_send, core_recv, x_send, x_recv, z_send, z_recv, flat_send, flat_recv, dg_sem, load_sem, first_sem,
+    core_send, core_recv, x_send, x_recv, z_send, z_recv, flat_send, flat_recv, dg_sem, load_sem, first_sem, leave_sem,
 ):
     spot = Spot(place)
     a, b, c, me, index = spot.a, spot.b, spot.c, spot.me, spot.index
@@ -1106,6 +1106,12 @@
     else:
         gh_ref[...] = jnp.zeros_like(gh_ref)
         output_ref[...] = jnp.zeros_like(output_ref)
+    leaving = [
+        pltpu.make_async_copy(gh_ref, gh_hbm, leave_sem.at[0]),
+        pltpu.make_async_copy(output_ref, output_hbm, leave_sem.at[1]),
+    ]
+    for copy in leaving:
+        copy.start()
 
     spot.arrived(core_flat, flat_recv.at[1])
     total = stage[2] + core_flat[...]
@@ -1126,6 +1132,8 @@
         own_ref[:, edge : edge + 2 * STATE] = bc_send[...] + bc_buf[...]
     for copy in started:
         copy.wait_send()
+    for copy in leaving:
+        copy.wait()
 
 
 def last_kernel(
@@ -1321,10 +1329,10 @@
     own, flat, gh, output = pl.pallas_call(
         functools.partial(reduce_kernel, place),
         in_specs=[ANY] * 2 + [WHOLE] * 3 + [ANY] * 5,
-        out_specs=[WHOLE] * 4,
+        out_specs=[WHOLE] * 2 + [ANY] * 2,
         out_shape=[SDS((rows, width), F32), SDS(flat.shape, F32), SDS(hidden.shape, BF), SDS(hidden.shape, BF)],
         scratch_shapes=[
-            pltpu.VMEM(tok.shape, BF), pltpu.VMEM(ge.shape, BF), pltpu.VMEM(weights.shape, BF), tokens, tokens, tokens, tokens, tokens, tokens, tokens,
+            tokens, tokens, pltpu.VMEM(tok.shape, BF), pltpu.VMEM(ge.shape, BF), pltpu.VMEM(weights.shape, BF), tokens, tokens, tokens, tokens, tokens, tokens, tokens,
             pltpu.VMEM((depth, width) if pair else (16, 128), BF),
             pltpu.VMEM((blocks, cut, width), BF),
             pltpu.VMEM((columns, cut, width), BF),
@@ -1337,7 +1345,7 @@
             pltpu.VMEM((place.first,) + flat.shape, F32),
             pltpu.VMEM((4,) + flat.shape, F32),
         ] + line_sems(place, PIECES, lines) + [
-            DMA((1 + place.first + place.second,)), DMA((2 + place.first + place.second,)), DMA((4,)), DMA((5,)), DMA((2,)),
+            DMA((1 + place.first + place.second,)), DMA((2 + place.first + place.second,)), DMA((4,)), DMA((5,)), DMA((2,)), DMA((2,)),
         ],
         compiler_params=params(4),
         name="reduce_all",

time: 165 us -> 165 us (level)
  no operation moved by 1% of the time
where the time goes in v8:
time: 165 us; the launch traced here: 163 us
  Pallas kernels  162 us (98%)
    pallas_call x1, Pallas kernels, mixer_backward(): pl.pallas_call(functools.partial(backward_kernel, place, heads, inner_all...  48.2 us
    pallas_call x1, Pallas kernels, reduce_all(): pl.pallas_call(functools.partial(reduce_kernel, place), in_specs=[ANY] *...  43.9 us
    pallas_call x1, Pallas kernels, gather_all(): pl.pallas_call(functools.partial(gather_kernel, place, heads), in_specs=[...  35.8 us
    pallas_call x1, Pallas kernels, mixer_forward(): pl.pallas_call(functools.partial(forward_kernel, place, heads), grid=(seq...  30.5 us
    pallas_call x1, Pallas kernels, body(): pl.pallas_call(functools.partial(last_kernel, heads), in_specs=[WHOLE] *...  3.6 us

profile of v8, /device:TPU:0, one launch (start us, length us, event | category | flops | bytes accessed | tf_op | source)
XLA Modules:
  0.0 162.7 jit_solution(11502371143738619984)
XLA Ops:
  0.7 35.8 %gather_all.1 = (bf16[1024,2432]{1,0:T(8,128)(2,1)}, bf16[1,1024,1024]{2,1,0:T(8,128)(2,1)}, f32[1,16,1024]{2,1,0:T(8,128)}, f32[8,1024]{1,0:T(8,128)}, f32[8,256]{1,0:T(8,128)}, /*index=5*/f32[2,16,128]{2,1,0:T(8,128)}) custom-call(bf16[64,2048]{1,0:T(8,128)(2,1)} %zx_ref.1, bf16[64,256]{1,0:T(8,128)(2,1)} %bc_ref.1, bf16[16,64]{1,0:T(8,128)(2,1)} %bitcast.30, ...), custom_call_target="tpu_custom_call" | custom-call | tf_op jit(solution)/shard_map/gather_all/pallas_call | solution.py:1195
  36.5 30.5 %mixer_forward.1 = (bf16[1,1024,2304]{2,1,0:T(8,128)(2,1)}, f32[1,16,1024]{2,1,0:T(8,128)}, bf16[1,1024,1024]{2,1,0:T(8,128)(2,1)}, bf16[1,1024,1024]{2,1,0:T(8,...) custom-call(bf16[1,1024,1024]{2,1,0:T(8,128)(2,1)} %get-tuple-elemen, ...), custom_call_target="tpu_custom_call" | custom-call | tf_op jit(solution)/shard_map/mixer_forward/pallas_call | solution.py:1220
  66.9 48.2 %mixer_backward.1 = (bf16[1,1024,2432]{2,1,0:T(8,128)(2,1)}, f32[16,1024]{1,0:T(8,128)}, bf16[1,512,1024]{2,1,0:T(8,128)(2,1)}, bf16[1,512,1024]{2,1,0:T(8,128)(...) custom-call(bf16[1,1024,2304]{2,1,0:T(8,128)(2,1)} %get-tuple-element.64.pz_ref, ...), custom_call_target="tpu_custom_call" | custom-call | tf_op jit(solution)/shard_map/mixer_backward/pallas_call | solution.py:1274
  115.1 43.9 %reduce_all.1 = (f32[64,2432]{1,0:T(8,128)}, f32[16,1024]{1,0:T(8,128)}, bf16[1,512,1024]{2,1,0:T(8,128)(2,1)}, bf16[1,512,1024]{2,1,0:T(8,128)(2,1)}) custom-call(bf16[1024,1024]{1,0:T(8,128)(2,1)} %bitcast.22, bf16[1024,2432]{1,0:T(8,128)(2,1)} %bitcast.23, f32[16,1024]{1,0:T(8,128)} %get-tuple-element.77.flat_ref, f32[1,1024]{1,0:T(1,128)} %bitcast.28, ...), custom_call_target="tpu_custom_call" | custom-call | tf_op jit(solution)/shard_map/reduce_all/pallas_call | solution.py:1329
  159.0 3.6 %outputs.1 = (bf16[1,512,1024]{2,1,0:T(8,128)(2,1)}, bf16[1,512,1024]{2,1,0:T(8,128)(2,1)}, f32[1,1024]{1,0:T(1,128)}, f32[64,2048]{1,0:T(8,128)}, f32[64,256]{1...) custom-call(f32[64,2432]{1,0:T(8,128)} %get-tuple-element.81.own_ref, ...), custom_call_target="tpu_custom_call" | custom-call | tf_op jit(solution)/shard_map/outputs/pallas_call | solution.py:1412
